TPU v7x, 32 devices: a whole 2x2x4 slice. The times are simulated.
32 devices in a mesh: clip: 4 (over z), frame: 8 (over y, x, core).
Axes of the slice: x: 2, y: 2, z: 4, core: 2. Of those that a mesh axis runs over, the one named last changes fastest.
Arguments:
- tokens: bfloat16 [16, 16, 256, 768], P('clip', 'frame'), may hold values from -6 to 6
- frame_counts: int32 [16], P('clip'), may hold values from 8 to 16, as said below
- norm_gain: float32 [2, 2, 768], replicated, may hold values from 0.25 to 1.75
- norm_bias: float32 [2, 2, 768], replicated, may hold values from -2.5 to 2.5
- project_in: bfloat16 [2, 768, 2304], replicated, may hold values from -0.21875 to 0.21875
- project_out: bfloat16 [2, 768, 768], replicated, may hold values from -0.875 to 0.875
- expand_weight: bfloat16 [2, 768, 3072], replicated, may hold values from -0.21875 to 0.21875
- expand_bias: float32 [2, 3072], replicated, may hold values from -3 to 3
- reduce_weight: bfloat16 [2, 3072, 768], replicated, may hold values from -0.109375 to 0.109375
- cotangent: bfloat16 [16, 16, 256, 768], P('clip', 'frame'), may hold values from -6 to 6
Outputs:
- mixed: bfloat16 [16, 16, 256, 768], P('clip', 'frame')
- grad_tokens: bfloat16 [16, 16, 256, 768], P('clip', 'frame')
- grad_norm_gain: float32 [2, 2, 768], P(None, None, 'frame')
- grad_norm_bias: float32 [2, 2, 768], P(None, None, 'frame')
- grad_project_in: float32 [2, 768, 2304], P(None, 'frame')
- grad_project_out: float32 [2, 768, 768], P(None, 'frame')
- grad_expand_weight: float32 [2, 768, 3072], P(None, 'frame')
- grad_expand_bias: float32 [2, 3072], P(None, 'frame')
- grad_reduce_weight: float32 [2, 3072, 768], P(None, 'frame')
Inputs may be any that keep to these rules, and one draw needn't show every extreme that they name: `frame_counts`: each entry is 8 or 16; at least one clip has 8 frames and at least one has 16; each aligned block of 4 consecutive clips (the clips of one device along `clip`) holds at least one clip of 16 frames.
All inputs are finite; a program needn't handle non-finite values.
Results may differ from a plain program's by a relative error of at most 0.02.
Values may be sent and summed in bfloat16 or wider, within the bound.
No kernel may reach another device: no remote copies, remote signals or barrier semaphores. Data moves between devices by JAX's collectives and lax.ppermute only.
A program may use at most 1.1875 GiB of HBM per device.

v0:
```python
import jax
import jax.numpy as jnp
from jax import lax
from jax.sharding import PartitionSpec as P

HEAD_DIM = 64
TUBE = 16


EPSILON = 1e-05
LOWTYPE = jnp.bfloat16
WIDETYPE = jnp.float32


def norm_rows(stream, gain_row, shift_row):
    center = stream - jnp.mean(stream, axis=-1, keepdims=True)
    spread = jnp.mean(center * center, axis=-1, keepdims=True)
    return center * lax.rsqrt(spread + EPSILON) * gain_row + shift_row


def norm_back(stream, gain_row, shift_row, grad_out):
    unused, pullback = jax.vjp(norm_rows, stream, gain_row, shift_row)
    return pullback(grad_out)


def exact_gelu(value):
    return jax.nn.gelu(value, approximate=False)


def outer_sum(left, right):
    return jnp.einsum(
        "ni,nj->ij",
        left.reshape(-1, left.shape[-1]),
        right.reshape(-1, right.shape[-1]),
        preferred_element_type=WIDETYPE,
    )


def times_transpose(left, matrix):
    return jnp.einsum("...j,ij->...i", left, matrix, preferred_element_type=WIDETYPE)


def masked_scores(queries, keys_in, kept_keys):
    scores = jnp.einsum("bftphe,bgtqhe->bthfpgq", queries, keys_in, preferred_element_type=WIDETYPE)
    scores = scores * queries.shape[-1] ** (-0.5)
    return jnp.where(kept_keys[:, None, None, None, None, :, None], scores, -1e30)


def attend_forward(queries, keys_in, values, kept_keys):
    scores = masked_scores(queries, keys_in, kept_keys)
    row_peak = jnp.max(scores, axis=(5, 6), keepdims=True)
    raised = jnp.exp(scores - row_peak)
    totals = jnp.sum(raised, axis=(5, 6), keepdims=True)
    softmax_low = (raised / totals).astype(LOWTYPE)
    attended = jnp.einsum(
        "bthfpgq,bgtqhe->bftphe", softmax_low, values, preferred_element_type=WIDETYPE
    )
    return (attended.astype(LOWTYPE), row_peak + jnp.log(totals))


def attend_backward(queries, keys_in, values, kept_keys, log_total, grad_attended):
    scores = masked_scores(queries, keys_in, kept_keys)
    softmax_out = jnp.exp(scores - log_total)
    grad_softmax = jnp.einsum(
        "bftphe,bgtqhe->bthfpgq", grad_attended, values, preferred_element_type=WIDETYPE
    )
    grad_values = jnp.einsum(
        "bthfpgq,bftphe->bgtqhe",
        softmax_out.astype(LOWTYPE),
        grad_attended,
        preferred_element_type=WIDETYPE,
    )
    row_inner = jnp.sum(softmax_out * grad_softmax, axis=(5, 6), keepdims=True)
    grad_scores = (softmax_out * (grad_softmax - row_inner)).astype(LOWTYPE)
    score_scale = queries.shape[-1] ** (-0.5)
    grad_queries = (
        jnp.einsum("bthfpgq,bgtqhe->bftphe", grad_scores, keys_in, preferred_element_type=WIDETYPE)
        * score_scale
    )
    grad_keys = (
        jnp.einsum("bthfpgq,bftphe->bgtqhe", grad_scores, queries, preferred_element_type=WIDETYPE)
        * score_scale
    )
    return jnp.stack((grad_queries, grad_keys, grad_values), axis=-3).astype(LOWTYPE)


def block_forward(
    stream,
    kept_keys,
    gain_pair,
    shift_pair,
    project_in,
    project_out,
    expand_weight,
    expand_bias,
    reduce_weight,
):
    layout = stream.shape[:-1]
    model_width = stream.shape[-1]
    head_count = model_width // HEAD_DIM
    normed = norm_rows(stream, gain_pair[0], shift_pair[0]).astype(LOWTYPE)
    triple = jnp.dot(normed, project_in, preferred_element_type=WIDETYPE).astype(LOWTYPE)
    triple = triple.reshape(layout + (3, head_count, HEAD_DIM))
    attended, log_total = attend_forward(
        triple[..., 0, :, :], triple[..., 1, :, :], triple[..., 2, :, :], kept_keys
    )
    attended = attended.reshape(layout + (model_width,))
    middle = stream + jnp.dot(attended, project_out, preferred_element_type=WIDETYPE)
    normed_two = norm_rows(middle, gain_pair[1], shift_pair[1]).astype(LOWTYPE)
    pre_act = jnp.dot(normed_two, expand_weight, preferred_element_type=WIDETYPE) + expand_bias
    activated = exact_gelu(pre_act).astype(LOWTYPE)
    result = middle + jnp.dot(activated, reduce_weight, preferred_element_type=WIDETYPE)
    return (result, (normed, triple, attended, log_total, middle, normed_two, pre_act, activated))


def block_backward(
    stream,
    kept_keys,
    gain_pair,
    shift_pair,
    project_in,
    project_out,
    expand_weight,
    expand_bias,
    reduce_weight,
    saved,
    grad_result,
):
    normed, triple, attended, log_total, middle, normed_two, pre_act, activated = saved
    layout = stream.shape[:-1]
    model_width = stream.shape[-1]
    head_count = model_width // HEAD_DIM
    grad_branch = grad_result.astype(LOWTYPE)
    grad_reduce = outer_sum(activated, grad_branch)
    grad_activated = times_transpose(grad_branch, reduce_weight)
    unused, gelu_pull = jax.vjp(exact_gelu, pre_act)
    grad_pre = gelu_pull(grad_activated)[0].astype(LOWTYPE)
    grad_bias = jnp.sum(grad_pre.reshape(-1, grad_pre.shape[-1]), axis=0, dtype=WIDETYPE)
    grad_expand = outer_sum(normed_two, grad_pre)
    grad_normed_two = times_transpose(grad_pre, expand_weight)
    grad_middle_norm, grad_gain_two, grad_shift_two = norm_back(
        middle, gain_pair[1], shift_pair[1], grad_normed_two
    )
    grad_middle = grad_result + grad_middle_norm
    grad_attn_branch = grad_middle.astype(LOWTYPE)
    grad_project_out = outer_sum(attended, grad_attn_branch)
    grad_attended = times_transpose(grad_attn_branch, project_out).astype(LOWTYPE)
    grad_attended = grad_attended.reshape(layout + (head_count, HEAD_DIM))
    grad_triple = attend_backward(
        triple[..., 0, :, :],
        triple[..., 1, :, :],
        triple[..., 2, :, :],
        kept_keys,
        log_total,
        grad_attended,
    )
    grad_triple = grad_triple.reshape(layout + (3 * model_width,))
    grad_project_in = outer_sum(normed, grad_triple)
    grad_normed = times_transpose(grad_triple, project_in)
    grad_stream_norm, grad_gain_one, grad_shift_one = norm_back(
        stream, gain_pair[0], shift_pair[0], grad_normed
    )
    grad_stream = grad_middle + grad_stream_norm
    return (
        grad_stream,
        (
            jnp.stack((grad_gain_one, grad_gain_two)),
            jnp.stack((grad_shift_one, grad_shift_two)),
            grad_project_in,
            grad_project_out,
            grad_expand,
            grad_bias,
            grad_reduce,
        ),
    )


def local(
    tokens,
    frame_counts,
    norm_gain,
    norm_bias,
    project_in,
    project_out,
    expand_weight,
    expand_bias,
    reduce_weight,
    cotangent,
):
    clip_count, frames_here, tok_frame, model_width = tokens.shape
    frame_devices = lax.axis_size("frame")
    frame_total = frames_here * frame_devices
    tubes_here = tok_frame // TUBE // frame_devices
    spatial_weights = (
        norm_gain[0],
        norm_bias[0],
        project_in[0],
        project_out[0],
        expand_weight[0],
        expand_bias[0],
        reduce_weight[0],
    )
    tube_weights = (
        norm_gain[1],
        norm_bias[1],
        project_in[1],
        project_out[1],
        expand_weight[1],
        expand_bias[1],
        reduce_weight[1],
    )
    cotangent_tubes = lax.all_to_all(cotangent, "frame", split_axis=2, concat_axis=1, tiled=True)
    spatial_in = tokens.astype(WIDETYPE).reshape(
        clip_count * frames_here, 1, 1, tok_frame, model_width
    )
    all_kept = jnp.ones((clip_count * frames_here, 1), dtype=bool)
    spatial_out, spatial_saved = block_forward(spatial_in, all_kept, *spatial_weights)
    boundary = spatial_out.astype(LOWTYPE).reshape(clip_count, frames_here, tok_frame, model_width)
    boundary_tubes = lax.all_to_all(boundary, "frame", split_axis=2, concat_axis=1, tiled=True)
    tube_shape = (clip_count, frame_total, tubes_here, TUBE, model_width)
    tube_flat = (clip_count, frame_total, tubes_here * TUBE, model_width)
    tube_in = boundary_tubes.astype(WIDETYPE).reshape(tube_shape)
    frame_kept = (
        lax.broadcasted_iota(jnp.int32, (clip_count, frame_total), 1) < frame_counts[:, None]
    )
    tube_out, tube_saved = block_forward(tube_in, frame_kept, *tube_weights)
    mixed = lax.all_to_all(
        tube_out.astype(LOWTYPE).reshape(tube_flat),
        "frame",
        split_axis=1,
        concat_axis=2,
        tiled=True,
    )
    grad_tube_in, tube_grads = block_backward(
        tube_in,
        frame_kept,
        *tube_weights,
        tube_saved,
        cotangent_tubes.astype(WIDETYPE).reshape(tube_shape)
    )
    grad_boundary = lax.all_to_all(
        grad_tube_in.astype(LOWTYPE).reshape(tube_flat),
        "frame",
        split_axis=1,
        concat_axis=2,
        tiled=True,
    )
    grad_spatial_in, spatial_grads = block_backward(
        spatial_in,
        all_kept,
        *spatial_weights,
        spatial_saved,
        grad_boundary.astype(WIDETYPE).reshape(spatial_in.shape)
    )
    shared_rows = (
        lax.psum_scatter(
            spatial_grads[0].astype(jnp.bfloat16), "frame", scatter_dimension=1, tiled=True
        ).astype(jnp.float32),
        lax.psum_scatter(
            spatial_grads[1].astype(jnp.bfloat16), "frame", scatter_dimension=1, tiled=True
        ).astype(jnp.float32),
        lax.psum_scatter(
            spatial_grads[2].astype(jnp.bfloat16), "frame", scatter_dimension=0, tiled=True
        ).astype(jnp.float32),
        lax.psum_scatter(
            spatial_grads[3].astype(jnp.bfloat16), "frame", scatter_dimension=0, tiled=True
        ).astype(jnp.float32),
        lax.psum_scatter(
            spatial_grads[4].astype(jnp.bfloat16), "frame", scatter_dimension=0, tiled=True
        ).astype(jnp.float32),
        lax.psum_scatter(
            spatial_grads[5].astype(jnp.bfloat16), "frame", scatter_dimension=0, tiled=True
        ).astype(jnp.float32),
        lax.psum_scatter(
            spatial_grads[6].astype(jnp.bfloat16), "frame", scatter_dimension=0, tiled=True
        ).astype(jnp.float32),
        lax.psum_scatter(
            tube_grads[0].astype(jnp.bfloat16), "frame", scatter_dimension=1, tiled=True
        ).astype(jnp.float32),
        lax.psum_scatter(
            tube_grads[1].astype(jnp.bfloat16), "frame", scatter_dimension=1, tiled=True
        ).astype(jnp.float32),
        lax.psum_scatter(
            tube_grads[2].astype(jnp.bfloat16), "frame", scatter_dimension=0, tiled=True
        ).astype(jnp.float32),
        lax.psum_scatter(
            tube_grads[3].astype(jnp.bfloat16), "frame", scatter_dimension=0, tiled=True
        ).astype(jnp.float32),
        lax.psum_scatter(
            tube_grads[4].astype(jnp.bfloat16), "frame", scatter_dimension=0, tiled=True
        ).astype(jnp.float32),
        lax.psum_scatter(
            tube_grads[5].astype(jnp.bfloat16), "frame", scatter_dimension=0, tiled=True
        ).astype(jnp.float32),
        lax.psum_scatter(
            tube_grads[6].astype(jnp.bfloat16), "frame", scatter_dimension=0, tiled=True
        ).astype(jnp.float32),
    )
    summed = (
        lax.psum(shared_rows[0].astype(jnp.bfloat16), "clip").astype(jnp.float32),
        lax.psum(shared_rows[1].astype(jnp.bfloat16), "clip").astype(jnp.float32),
        lax.psum(shared_rows[2].astype(jnp.bfloat16), "clip").astype(jnp.float32),
        lax.psum(shared_rows[3].astype(jnp.bfloat16), "clip").astype(jnp.float32),
        lax.psum(shared_rows[4].astype(jnp.bfloat16), "clip").astype(jnp.float32),
        lax.psum(shared_rows[5].astype(jnp.bfloat16), "clip").astype(jnp.float32),
        lax.psum(shared_rows[6].astype(jnp.bfloat16), "clip").astype(jnp.float32),
        lax.psum(shared_rows[7].astype(jnp.bfloat16), "clip").astype(jnp.float32),
        lax.psum(shared_rows[8].astype(jnp.bfloat16), "clip").astype(jnp.float32),
        lax.psum(shared_rows[9].astype(jnp.bfloat16), "clip").astype(jnp.float32),
        lax.psum(shared_rows[10].astype(jnp.bfloat16), "clip").astype(jnp.float32),
        lax.psum(shared_rows[11].astype(jnp.bfloat16), "clip").astype(jnp.float32),
        lax.psum(shared_rows[12].astype(jnp.bfloat16), "clip").astype(jnp.float32),
        lax.psum(shared_rows[13].astype(jnp.bfloat16), "clip").astype(jnp.float32),
    )
    spatial_grads = summed[:7]
    tube_grads = summed[7:]
    grad_tokens = grad_spatial_in.reshape(tokens.shape).astype(LOWTYPE)
    stacked = tuple((jnp.stack((spatial_grads[index], tube_grads[index])) for index in range(7)))
    return (mixed, grad_tokens) + stacked


def solution(mesh):
    in_specs = (
        P("clip", "frame", None, None),
        P("clip"),
        P(),
        P(),
        P(),
        P(),
        P(),
        P(),
        P(),
        P("clip", "frame", None, None),
    )
    out_specs = (
        P("clip", "frame", None, None),
        P("clip", "frame", None, None),
        P(None, None, "frame"),
        P(None, None, "frame"),
        P(None, "frame", None),
        P(None, "frame", None),
        P(None, "frame", None),
        P(None, "frame"),
        P(None, "frame", None),
    )
    return jax.shard_map(local, mesh=mesh, in_specs=in_specs, out_specs=out_specs, check_vma=False)
```

profile of v0, /device:TPU:0, one launch (start us, length us, event | category | flops | bytes accessed | tf_op | source)
XLA Modules:
  0.0 2126.8 jit_solution(9400309277083822236)
XLA Ops:
  89.6 24.3 %fusion.49 = (u8[256,3072]{1,0:T(8,128)(4,1)S(1)}, u8[256,3072]{1,0:T(8,128)(4,1)S(1)}, f32[8,256,3072]{2,1,0:T(8,128)}) fusion(f32[3072]{0:T(1024)S(1)} %bitcast.418, bf16[2,768,3072]{2,1,0:T(8,128)(2,1)} %param.16, f32[8,256,768]{2,1,0:T(8,128)} %copy-done.12, f32[768]{0:T(1024)S(1)} %get-tuple-element.32, f32[768]{0:T(1024)S(1)} %get-tuple-element.98, ...), kind=kOutput, calls=%fused_computation.135 | convolution fusion | flops 9758048256 | bytes 37783552 | tf_op jit(solution)/shard_map/dot_general | solution.py:110
  114.0 60.5 %multiply_convert_fusion.3 = (bf16[8,256,3072]{2,1,0:T(8,128)(2,1)S(1)}, f32[8,256,3072]{2,1,0:T(8,128)}) fusion(f32[8,256,3072]{2,1,0:T(8,128)} %get-tuple-element.78, f32[3072]{0:T(1024)S(1)} %bitcast.419, u8[256,3072]{1,0:T(8,128)(4,1)S(1)} %get-tuple-element.12, u8[256,3072]{1,0:T(8,128)(4,1)S(1)} %get-tuple-element.11), kind=kLoop, calls=%fused_computation.44 | loop fusion | flops 446693376 | bytes 64499712 | tf_op jit(solution)/shard_map/convert_element_type | solution.py:111
  208.0 31.9 %all-to-all-done = bf16[4,2,256,768]{3,1,0,2:T(2,128)(2,1)S(1)} async-done(((bf16[4,2,256,768]{3,1,0,2:T(2,128)(2,1)}), bf16[4,2,256,768]{3,1,0,2:T(2,128)(2,1)S(1)}, u32[]{:S(2)}, u32[]{:S(2)}) %all-to-all-start) | async-done | bytes 3145760 | tf_op jit(solution)/shard_map/all_to_all | solution.py:219
  256.9 25.6 %all-to-all-done.2 = bf16[4,2,256,768]{3,0,1,2:T(4,128)(2,1)} async-done(((bf16[4,2,256,768]{3,0,1,2:T(4,128)(2,1)}), bf16[4,2,256,768]{3,0,1,2:T(4,128)(2,1)}, u32[]{:S(2)}, u32[]{:S(2)}) %all-to-all-start.2) | async-done | bytes 3145760 | tf_op jit(solution)/shard_map/all_to_all | solution.py:212
  305.0 28.7 %reshape.774 = bf16[4,16,2,16,3,12,64]{6,5,4,3,2,1,0:T(8,128)(2,1)} reshape(bf16[4,16,2,16,2304]{4,3,2,1,0:T(8,128)(2,1)} %convolution_convert_fusion) | data formatting | bytes 18874368 | tf_op jit(solution)/shard_map/reshape | solution.py:103
  351.7 74.0 %fusion.5 = (f32[4,2,12,16,16]{4,3,2,1,0:T(8,128)S(1)}, f32[4,2,12,16,16,16,16]{4,6,5,3,2,1,0:T(8,128)}) fusion(pred[4,16]{1,0:T(4,128)(4,1)S(1)} %iota_compare_fusion, bf16[4,16,2,16,1,12,64]{6,5,4,3,2,1,0:T(8,128)(2,1)} %get-tuple-element.63, bf16[4,16,2,16,1,12,64]{6,5,4,3,2,1,0:T(8,128)(2,1)} %get-tuple-element.62), kind=kOutput, calls=%fused_computation.11 | convolution fusion | flops 824156160 | bytes 31555648 | tf_op jit(solution)/shard_map/bftphe,bgtqhe->bthfpgq/dot_general | solution.py:44
  425.7 61.2 %fusion = f32[4,2,12,16,16]{4,3,2,1,0:T(8,128)S(1)} fusion(f32[4,2,12,16,16]{4,3,2,1,0:T(8,128)S(1)} %get-tuple-element.79, f32[4,2,12,16,16,16,16]{4,6,5,3,2,1,0:T(8,128)} %get-tuple-element.80, pred[4,16]{1,0:T(4,128)(4,1)S(1)} %iota_compare_fusion), kind=kLoop, calls=%fused_computation.6 | loop fusion | flops 25141248 | bytes 25362496 | tf_op jit(solution)/shard_map/reduce_sum | solution.py:53
  487.9 75.0 %fusion.29 = bf16[4,16,2,16,12,64]{5,3,1,4,2,0:T(8,128)(2,1)} fusion(f32[4,2,12,16,16]{4,3,2,1,0:T(8,128)S(1)} %fusion, f32[4,2,12,16,16]{4,3,2,1,0:T(8,128)S(1)} %get-tuple-element.79, f32[4,2,12,16,16,16,16]{4,6,5,3,2,1,0:T(8,128)} %get-tuple-element.80, pred[4,16]{1,0:T(4,128)(4,1)S(1)} %iota_compare_fusion, ...), kind=kOutput, calls=%fused_computation.86 | convolution fusion | flops 838336512 | bytes 31653952 | tf_op jit(solution)/shard_map/bthfpgq,bgtqhe->bftphe/dot_general | solution.py:55
  596.0 24.3 %fusion.27 = (u16[4,2,16,3072]{3,2,1,0:T(8,128)(2,1)}, u16[4,2,16,3072]{3,2,1,0:T(8,128)(2,1)}, f32[4,16,2,16,3072]{4,3,2,1,0:T(8,128)}) fusion(f32[3072]{0:T(1024)S(1)} %bitcast.421, bf16[2,768,3072]{2,1,0:T(8,128)(2,1)} %param.16, f32[4,16,2,16,768]{4,3,2,1,0:T(8,128)S(1)} %get-tuple-element.82, f32[768]{0:T(1024)S(1)} %copy-done.71, ...), kind=kOutput, calls=%fused_computation.73 | convolution fusion | flops 9758834688 | bytes 37783552 | tf_op jit(solution)/shard_map/dot_general | solution.py:110
  620.3 61.3 %multiply_convert_fusion.2 = (bf16[4,16,2,16,3072]{4,3,2,1,0:T(8,128)(2,1)}, f32[4,16,2,16,3072]{4,3,2,1,0:T(8,128)}) fusion(f32[4,16,2,16,3072]{4,3,2,1,0:T(8,128)} %get-tuple-element.83, f32[3072]{0:T(1024)S(1)} %bitcast.422, u16[4,2,16,3072]{3,2,1,0:T(8,128)(2,1)} %get-tuple-element.10, u16[4,2,16,3072]{3,2,1,0:T(8,128)(2,1)} %get-tuple-element.9), kind=kLoop, calls=%fused_computation.31 | loop fusion | flops 446693376 | bytes 64499712 | tf_op jit(solution)/shard_map/convert_element_type | solution.py:111
  681.6 27.9 %fusion.132 = (bf16[3072]{0:T(1024)(128)(2,1)}, bf16[4,16,2,16,3072]{4,3,2,1,0:T(8,128)(2,1)}) fusion(f32[4,16,2,16,3072]{4,3,2,1,0:T(8,128)} %get-tuple-element.56, bf16[4,16,2,16,768]{4,3,2,1,0:T(8,128)(2,1)S(1)} %bitcast.384, bf16[2,3072,768]{2,1,0:T(8,128)(2,1)} %param.18, f32[4,16,2,16,3072]{4,3,2,1,0:T(8,128)} %get-tuple-element.83, ...), kind=kOutput, calls=%fused_computation.255 | convolution fusion | flops 9764336640 | bytes 70797312 | tf_op jit(solution)/shard_map/...j,ij->...i/dot_general | solution.py:40
  709.5 19.8 multiply_reduce_fusion.3
  753.7 141.1 %multiply_reduce_fusion = (f32[4,2,12,16,16]{4,3,2,1,0:T(8,128)S(1)}, f32[4,2,12,16,16,16,16]{4,6,5,3,2,1,0:T(8,128)}) fusion(f32[4,2,12,16,16]{4,3,2,1,0:T(8,128)S(1)} %copy-done.19, f32[4,2,12,16,16,16,16]{4,6,5,3,2,1,0:T(8,128)} %get-tuple-element.80, pred[4,16]{1,0:T(4,128)(4,1)S(1)} %copy-done.30, ...), kind=kOutput, calls=%fused_computation.1 | convolution fusion | flops 836739072 | bytes 56819776 | tf_op jit(solution)/shard_map/bftphe,bgtqhe->bthfpgq/dot_general | solution.py:64
  894.8 197.8 %multiply_convert_fusion = (bf16[4,2,12,16,16,16,16]{4,6,5,3,2,1,0:T(8,128)(2,1)}, bf16[4,2,12,16,16,16,16]{4,6,5,3,2,1,0:T(8,128)(2,1)}) fusion(f32[4,2,12,16,16,16,16]{4,6,5,3,2,1,0:T(8,128)} %get-tuple-element.86, f32[4,2,12,16,16]{4,3,2,1,0:T(8,128)S(1)} %get-tuple-element.85, f32[4,2,12,16,16]{4,3,2,1,0:T(8,128)S(1)} %copy-done.19, ...), kind=kLoop, calls=%fused_computation | loop fusion | flops 44040192 | bytes 75694144 | tf_op jit(solution)/shard_map/convert_element_type | solution.py:74
  1092.6 44.8 %fusion.32 = bf16[4,16,2,16,1,12,64]{6,3,1,5,2,0,4:T(8,128)(2,1)} fusion(bf16[4,2,12,16,16,16,16]{4,6,5,3,2,1,0:T(8,128)(2,1)} %get-tuple-element.59, bf16[4,16,2,16,1,12,64]{6,5,4,3,2,1,0:T(8,128)(2,1)} %get-tuple-element.62), kind=kOutput, calls=%fused_computation.89 | convolution fusion | flops 808452096 | bytes 18874368 | tf_op jit(solution)/shard_map/bthfpgq,bftphe->bgtqhe/dot_general | solution.py:81
  1137.3 41.3 %fusion.30 = bf16[4,16,2,16,1,12,64]{6,3,1,5,2,0,4:T(8,128)(2,1)} fusion(bf16[4,2,12,16,16,16,16]{4,6,5,3,2,1,0:T(8,128)(2,1)} %get-tuple-element.59, bf16[4,16,2,16,1,12,64]{6,5,4,3,2,1,0:T(8,128)(2,1)} %get-tuple-element.63), kind=kOutput, calls=%fused_computation.87 | convolution fusion | flops 808452096 | bytes 18874368 | tf_op jit(solution)/shard_map/bthfpgq,bgtqhe->bftphe/dot_general | solution.py:77
  1178.8 44.7 %fusion.31 = bf16[4,16,2,16,1,12,64]{6,3,1,5,2,0,4:T(8,128)(2,1)} fusion(bf16[4,2,12,16,16,16,16]{4,6,5,3,2,1,0:T(8,128)(2,1)} %get-tuple-element.60, bf16[4,16,2,16,12,64,1]{5,4,3,2,1,0,6:T(8,128)(2,1)} %bitcast.378), kind=kOutput, calls=%fused_computation.88 | convolution fusion | flops 806879232 | bytes 18874368 | tf_op jit(solution)/shard_map/bthfpgq,bftphe->bgtqhe/dot_general | solution.py:67
  1233.5 30.8 %copy.136 = bf16[4,16,2,16,3,12,64]{6,5,4,3,2,1,0:T(8,128)(2,1)} copy(bf16[4,16,2,16,3,12,64]{6,3,1,5,2,0,4:T(8,128)(2,1)S(1)} %pad_maximum_fusion) | data formatting | bytes 18874368 | tf_op jit(solution)/shard_map/stack | solution.py:84
  1264.3 30.2 %convert_element_type.319 = bf16[4,16,2,16,2304]{4,3,2,1,0:T(8,128)(2,1)} reshape(bf16[4,16,2,16,3,12,64]{6,5,4,3,2,1,0:T(8,128)(2,1)} %copy.136) | data formatting | bytes 18874368 | tf_op jit(solution)/shard_map/convert_element_type | solution.py:84
  1365.2 29.6 %fusion.133 = (bf16[3072]{0:T(1024)(128)(2,1)}, bf16[8,256,3072]{2,1,0:T(8,128)(2,1)}) fusion(f32[8,256,3072]{2,1,0:T(8,128)} %get-tuple-element.58, bf16[8,256,768]{2,1,0:T(8,128)(2,1)S(1)} %bitcast.380, bf16[2,3072,768]{2,1,0:T(8,128)(2,1)} %param.18, f32[8,256,3072]{2,1,0:T(8,128)} %get-tuple-element.78, f32[3072]{0:T(1024)S(1)} %bitcast.420), kind=kOutput, calls=%fused_computation.256 | convolution fusion | flops 9764336640 | bytes 70797312 | tf_op jit(solution)/shard_map/...j,ij->...i/dot_general | solution.py:40
  1425.1 30.5 %convert_element_type.334 = bf16[2048,2304]{1,0:T(8,128)(2,1)} reshape(bf16[4,16,2,16,3,12,64]{6,5,4,3,2,1,0:T(8,128)(2,1)} %copy.136) | data formatting | bytes 18874368 | tf_op jit(solution)/shard_map/convert_element_type | solution.py:84
  1484.7 18.5 bitcast_convert_fusion.3
  1511.7 19.9 multiply_reduce_fusion.1
  1531.6 23.4 %multiply_convert_fusion.1 = bf16[8,12,256,256]{2,3,1,0:T(8,128)(2,1)} fusion(f32[8,12,256,256]{2,3,1,0:T(8,128)} %get-tuple-element.90, f32[8,12,256,256]{2,3,1,0:T(8,128)} %get-tuple-element.75, f32[8,12,256]{2,1,0:T(8,128)S(1)} %get-tuple-element.89, f32[8,12,256]{2,1,0:T(8,128)S(1)} %log_add_fusion.1), kind=kLoop, calls=%fused_computation.26 | loop fusion | flops 31457280 | bytes 63111168 | tf_op jit(solution)/shard_map/convert_element_type | solution.py:74
  1599.1 19.4 copy.146
  1731.9 32.8 %reduce-scatter.33.cloned.1.call-done = bf16[384,768]{1,0:T(8,128)(2,1)} async-done(((bf16[3072,768]{1,0:T(8,128)(2,1)}), bf16[384,768]{1,0:T(8,128)(2,1)}) %reduce-scatter.33.cloned.1.call-update) | async-done | bytes 589840 | tf_op jit(solution)/shard_map/reduce_scatter | solution.py:274
  1764.7 57.8 %reduce-scatter.29.cloned.1.call-done = bf16[96,3072]{1,0:T(8,128)(2,1)} async-done(((bf16[768,3072]{1,0:T(8,128)(2,1)}), bf16[96,3072]{1,0:T(8,128)(2,1)}) %reduce-scatter.29.cloned.1.call-update) | async-done | bytes 589840 | tf_op jit(solution)/shard_map/reduce_scatter | solution.py:268
  1823.7 35.9 %reduce-scatter.39.cloned.1.call-done = bf16[96,2]{1,0:T(8,128)(2,1)} async-done(((bf16[768,2]{1,0:T(8,128)(2,1)}), bf16[96,2]{1,0:T(8,128)(2,1)}) %reduce-scatter.39.cloned.1.call-update) | async-done | bytes 400
  1860.4 36.5 %reduce-scatter.43.cloned.1.call-done = bf16[96,2]{1,0:T(8,128)(2,1)} async-done(((bf16[768,2]{1,0:T(8,128)(2,1)}), bf16[96,2]{1,0:T(8,128)(2,1)}) %reduce-scatter.43.cloned.1.call-update) | async-done | bytes 400
  1901.6 22.6 %all-reduce.2 = (bf16[3072]{0:T(1024)(128)(2,1)S(1)}, bf16[3072]{0:T(1024)(128)(2,1)S(1)}) all-reduce(bf16[3072]{0:T(1024)(128)(2,1)S(1)} %copy-done.67, bf16[3072]{0:T(1024)(128)(2,1)S(1)} %copy-done.68), channel_id=13, replica_groups=mesh['clip'=4,'frame'=8] {'frame'}, use_global_device_ids=true, to_apply=%region_54.55.clone | all-reduce | flops 6144 | bytes 24576
  1934.9 35.9 %reduce-scatter.41.cloned.1.call-done = bf16[96,2]{1,0:T(8,128)(2,1)} async-done(((bf16[768,2]{1,0:T(8,128)(2,1)}), bf16[96,2]{1,0:T(8,128)(2,1)}) %reduce-scatter.41.cloned.1.call-update) | async-done | bytes 400
  1985.3 124.8 %all-reduce.7.cloned.1.call-done = (bf16[1,96,2304]{2,1,0:T(8,128)(2,1)}, bf16[1,96,2304]{2,1,0:T(8,128)(2,1)}, bf16[1,96,768]{2,1,0:T(8,128)(2,1)}, bf16[1,96,7...) async-done(((bf16[1,96,2304]{2,1,0:T(8,128)(2,1)}, ...) | async-done | bytes 3538960 | tf_op jit(solution)/shard_map/psum | solution.py:309
  (343 shorter events, 577.9 us)
Async XLA Ops:
  15.5 98.4 %copy-start.53 = (f32[1,3072]{1,0:T(1,128)}, f32[1,3072]{1,0:T(1,128)S(1)}, u32[]{:S(2)}) copy-start(f32[1,3072]{1,0:T(1,128)S(1)} %get-tuple-element.69) | copy-start | bytes 36868
  17.0 72.6 %copy-start.61 = (f32[768]{0:T(1024)}, f32[768]{0:T(1024)S(1)}, u32[]{:S(2)}) copy-start(f32[768]{0:T(1024)S(1)} %get-tuple-element.98) | copy-start | bytes 9220
  17.0 72.6 %copy-start.69 = (f32[768]{0:T(1024)}, f32[768]{0:T(1024)S(1)}, u32[]{:S(2)}) copy-start(f32[768]{0:T(1024)S(1)} %get-tuple-element.32) | copy-start | bytes 9220
  113.9 60.5 %copy-start.13 = (f32[8,256,768]{2,1,0:T(8,128)S(1)}, f32[8,256,768]{2,1,0:T(8,128)}, u32[]{:S(2)}) copy-start(f32[8,256,768]{2,1,0:T(8,128)} %copy-done.12) | copy-start | bytes 18874372
  196.8 47.9 %copy-start.80 = (s32[4]{0:T(128)S(1)}, s32[4]{0:T(128)}, u32[]{:S(2)}) copy-start(s32[4]{0:T(128)} %param.11) | copy-start | bytes 52
  196.8 43.2 %all-to-all-start = ((bf16[4,2,256,768]{3,1,0,2:T(2,128)(2,1)}), bf16[4,2,256,768]{3,1,0,2:T(2,128)(2,1)S(1)}, u32[]{:S(2)}, u32[]{:S(2)}) async-start(bf16[4,2,256,768]{3,1,0,2:T(2,128)(2,1)} %copy.120), calls=%async_computation | async-start | bytes 6291456 | tf_op jit(solution)/shard_map/all_to_all | solution.py:219
  239.9 42.6 %all-to-all-start.2 = ((bf16[4,2,256,768]{3,0,1,2:T(4,128)(2,1)}), bf16[4,2,256,768]{3,0,1,2:T(4,128)(2,1)}, u32[]{:S(2)}, u32[]{:S(2)}) async-start(bf16[4,2,256,768]{3,0,1,2:T(4,128)(2,1)} %copy.129), calls=%async_computation.2 | async-start | bytes 6291456 | tf_op jit(solution)/shard_map/all_to_all | solution.py:212
  244.7 243.2 %copy-start.29 = (pred[4,16]{1,0:T(4,128)(4,1)}, pred[4,16]{1,0:T(4,128)(4,1)S(1)}, u32[]{:S(2)}) copy-start(pred[4,16]{1,0:T(4,128)(4,1)S(1)} %iota_compare_fusion) | copy-start | bytes 196
  595.0 134.4 %copy-start.31 = (f32[4,16,2,16]{3,2,1,0:T(2,128)}, f32[4,16,2,16]{3,2,1,0:T(2,128)S(1)}, u32[]{:S(2)}) copy-start(f32[4,16,2,16]{3,2,1,0:T(2,128)S(1)} %broadcast_multiply_fusion) | copy-start | bytes 24580
  595.9 133.5 %copy-start.37 = (f32[4,16,2,16]{3,2,1,0:T(2,128)}, f32[4,16,2,16]{3,2,1,0:T(2,128)S(1)}, u32[]{:S(2)}) copy-start(f32[4,16,2,16]{3,2,1,0:T(2,128)S(1)} %fusion.114) | copy-start | bytes 24580
  620.3 61.3 %copy-start.9 = (bf16[4,2,8,32,768]{4,3,1,2,0:T(8,128)(2,1)S(1)}, bf16[4,2,8,32,768]{4,3,1,2,0:T(8,128)(2,1)}, u32[]{:S(2)}) copy-start(bf16[4,2,8,32,768]{4,3,1,2,0:T(8,128)(2,1)} %copy.130) | copy-start | bytes 9437188
  1264.3 44.1 %slice-start.2 = ((s8[6291456]{0:T(1024)(128)(4,1)}), s8[2097152]{0:T(1024)(128)(4,1)S(1)}, s32[]{:S(2)}) async-start(s8[6291456]{0:T(1024)(128)(4,1)} %bitcast.368), calls=%async_computation.31 | async-start | bytes 4194304
  1319.9 41.5 %all-to-all-start.3 = ((bf16[4,16,32,768]{3,2,0,1:T(8,128)(2,1)}), bf16[4,16,32,768]{3,2,0,1:T(8,128)(2,1)S(1)}, u32[]{:S(2)}, u32[]{:S(2)}) async-start(bf16[4,16,32,768]{3,2,0,1:T(8,128)(2,1)} %copy.137), calls=%async_computation.3 | async-start | bytes 6291456 | tf_op jit(solution)/shard_map/all_to_all | solution.py:241
  1323.5 408.2 %reduce-scatter.27.cloned.1.call-start = ((), (), s32[]{:S(2)}) async-start(), calls=%async_computation.19 | async-start | bytes 1327104 | tf_op jit(solution)/shard_map/reduce_scatter | solution.py:286
  1347.9 383.8 %reduce-scatter.25.cloned.1.call-start = ((), (), s32[]{:S(2)}) async-start(), calls=%async_computation.18 | async-start | bytes 1327104 | tf_op jit(solution)/shard_map/reduce_scatter | solution.py:265
  1365.2 50.5 %copy-start.7 = (bf16[4,2,8,32,768]{4,3,2,1,0:T(8,128)(2,1)}, bf16[4,2,8,32,768]{4,3,2,1,0:T(8,128)(2,1)S(1)}, u32[]{:S(2)}) copy-start(bf16[4,2,8,32,768]{4,3,2,1,0:T(8,128)(2,1)S(1)} %copy.139) | copy-start | bytes 9437188
  1425.0 306.8 %reduce-scatter.23.cloned.1.call-start = ((), (), s32[]{:S(2)}) async-start(), calls=%async_computation.17 | async-start | bytes 3981312 | tf_op jit(solution)/shard_map/reduce_scatter | solution.py:283
  1469.0 262.9 %reduce-scatter.35.cloned.1.call-start = ((), (), s32[]{:S(2)}) async-start(), calls=%async_computation.23 | async-start | bytes 5308416 | tf_op jit(solution)/shard_map/reduce_scatter | solution.py:295
  1483.6 248.2 %reduce-scatter.31.cloned.1.call-start = ((), (), s32[]{:S(2)}) async-start(), calls=%async_computation.21 | async-start | bytes 5308416 | tf_op jit(solution)/shard_map/reduce_scatter | solution.py:289
  1503.2 228.7 %reduce-scatter.21.cloned.1.call-start = ((), (), s32[]{:S(2)}) async-start(), calls=%async_computation.16 | async-start | bytes 3981312 | tf_op jit(solution)/shard_map/reduce_scatter | solution.py:262
  1644.1 120.5 %reduce-scatter.33.cloned.1.call-start = ((), (), s32[]{:S(2)}) async-start(), calls=%async_computation.22 | async-start | bytes 5308416 | tf_op jit(solution)/shard_map/reduce_scatter | solution.py:274
  1658.8 163.7 %reduce-scatter.29.cloned.1.call-start = ((), (), s32[]{:S(2)}) async-start(), calls=%async_computation.20 | async-start | bytes 5308416 | tf_op jit(solution)/shard_map/reduce_scatter | solution.py:268
  1694.2 203.6 %all-to-all-start.1 = ((bf16[4,16,32,768]{3,2,0,1:T(8,128)(2,1)}), bf16[4,16,32,768]{3,2,0,1:T(8,128)(2,1)}, u32[]{:S(2)}, u32[]{:S(2)}) async-start(bf16[4,16,32,768]{3,2,0,1:T(8,128)(2,1)} %copy.127), calls=%async_computation.1 | async-start | bytes 6291456 | tf_op jit(solution)/shard_map/all_to_all | solution.py:227
  1698.7 160.9 %reduce-scatter.39.cloned.1.call-start = ((), (), s32[]{:S(2)}) async-start(), calls=%async_computation.25 | async-start | bytes 221184
  1699.7 197.2 %reduce-scatter.43.cloned.1.call-start = ((), (), s32[]{:S(2)}) async-start(), calls=%async_computation.27 | async-start | bytes 221184
  1700.7 233.4 %reduce-scatter.37.cloned.1.call-start = ((), (), s32[]{:S(2)}) async-start(), calls=%async_computation.24 | async-start | bytes 221184
  1723.9 98.6 %copy-start.81 = (u32[32]{0:T(128)S(1)}, u32[32]{0:T(128)}, u32[]{:S(2)}) copy-start(u32[32]{0:T(128)} %constant.22) | copy-start | bytes 388
  1726.5 175.1 %copy-start.67 = (bf16[3072]{0:T(1024)(128)(2,1)S(1)}, bf16[3072]{0:T(1024)(128)(2,1)}, u32[]{:S(2)}) copy-start(bf16[3072]{0:T(1024)(128)(2,1)} %get-tuple-element.92) | copy-start | bytes 18436
  1726.5 175.1 %copy-start.68 = (bf16[3072]{0:T(1024)(128)(2,1)S(1)}, bf16[3072]{0:T(1024)(128)(2,1)}, u32[]{:S(2)}) copy-start(bf16[3072]{0:T(1024)(128)(2,1)} %get-tuple-element.94) | copy-start | bytes 18436
  1726.5 197.8 %copy-start.48 = (f32[8,256]{1,0:T(8,128)S(1)}, f32[8,256]{1,0:T(8,128)}, u32[]{:S(2)}) copy-start(f32[8,256]{1,0:T(8,128)} %copy-done.47) | copy-start | bytes 24580
  1730.7 240.1 %reduce-scatter.41.cloned.1.call-start = ((), (), s32[]{:S(2)}) async-start(), calls=%async_computation.26 | async-start | bytes 221184
  1731.7 378.4 %all-reduce.7.cloned.1.call-start = ((), (), s32[]{:S(2)}) async-start(), calls=%async_computation.28 | async-start | bytes 7077888 | tf_op jit(solution)/shard_map/psum | solution.py:309
  (75 other events, 939.5 us)
Sparse Core Ops, SparseCore 0:
  1348.1 38.3 reduce-scatter.26
  1425.1 36.1 reduce-scatter.24
  1469.1 47.3 reduce-scatter.22
  1519.8 53.8 reduce-scatter.34
  1577.4 53.8 reduce-scatter.30
  1644.2 47.2 reduce-scatter.20
  1695.0 69.6 reduce-scatter.32
  1768.5 53.8 reduce-scatter.28
  1826.1 33.5 reduce-scatter.38
  1863.4 33.5 reduce-scatter.42
  1900.6 33.4 reduce-scatter.36
  1937.3 33.5 reduce-scatter.40
  1973.8 136.2 all-reduce.6
where the time goes:
time: 2140 us; the launch traced here: 2130 us
  matrix products  847 us (40%)
  other arithmetic  497 us (23%)
  waiting for transfers between devices  397 us (19%)
  local copies, waits for them, and re-layouts  317 us (15%)
  blocking collectives  34.5 us (2%)
    convert_element_type x2, other arithmetic, attend_backward(): grad_scores = (softmax_out * (grad_softmax - row_inner)).astype(LOWTYPE)  221 us
    dot_general x2, matrix products, attend_backward(): jnp.einsum('bftphe,bgtqhe->bthfpgq', grad_attended, values, preferred_ele...  161 us
    dot_general x8, matrix products, times_transpose(): jnp.einsum('...j,ij->...i', left, matrix, preferred_element_type=WIDETYPE)  130 us
    psum x1, waiting for transfers between devices, local(): lax.psum(shared_rows[9].astype(jnp.bfloat16), 'clip').astype(jnp.float32)  125 us
    convert_element_type x2, other arithmetic, block_forward(): activated = exact_gelu(pre_act).astype(LOWTYPE)  122 us
    unnamed x17, waiting for transfers between devices  110 us
    dot_general x8, matrix products, outer_sum(): jnp.einsum('ni,nj->ij', left.reshape(-1, left.shape[-1]), right.reshape(-...  103 us
    dot_general x2, matrix products, masked_scores(): jnp.einsum('bftphe,bgtqhe->bthfpgq', queries, keys_in, preferred_element_...  88.7 us
  transfers between devices with their start and end apart: 17, of which 10 were waited for; matrix products, arithmetic and copies ran while one was open for 19% of the time, Pallas kernels for 0%

commit v1 on v0

v1 whole, which is shorter than its diff:
```python
import functools

import jax
import jax.numpy as jnp
from jax import lax
from jax.experimental import pallas as pl
from jax.experimental.pallas import tpu as pltpu
from jax.sharding import PartitionSpec as P

HEAD_DIM = 64
TUBE = 16
PAIR = 2 * HEAD_DIM
EPSILON = 1e-05
HALF_ROOT = 0.7071067811865476
BELL_PEAK = 0.3989422804014327
LOW = jnp.bfloat16
WIDE = jnp.float32
VMEM_BYTES = 62 * 1024 * 1024


def dot(left, right, left_dim=1, right_dim=0):
    return lax.dot_general(
        left, right, (((left_dim,), (right_dim,)), ((), ())), preferred_element_type=WIDE
    )


def normalize(x):
    center = x - jnp.mean(x, axis=-1, keepdims=True)
    scale = lax.rsqrt(jnp.mean(center * center, axis=-1, keepdims=True) + EPSILON)
    return center * scale, scale


def normalize_back(n, scale, gain, grad):
    e = grad * gain
    return scale * (
        e - jnp.mean(e, axis=-1, keepdims=True) - n * jnp.mean(e * n, axis=-1, keepdims=True)
    )


def chunks(total, size):
    return [slice(start, start + size) for start in range(0, total, size)]


def load_window(ref, layout, window, length):
    if layout == "rows":
        return ref[window * length : (window + 1) * length, :]
    if layout == "frames":
        block = ref[:, 0, window]
    else:
        block = ref[:, 0, :, window * TUBE : (window + 1) * TUBE, :]
    return block.reshape(length, ref.shape[-1])


def store_window(ref, layout, window, length, value):
    if layout == "rows":
        ref[window * length : (window + 1) * length, :] = value
    elif layout == "frames":
        ref[:, 0, window] = value.reshape(ref.shape[0], ref.shape[3], ref.shape[4])
    else:
        ref[:, 0, :, window * TUBE : (window + 1) * TUBE, :] = value.reshape(
            ref.shape[0], ref.shape[2], TUBE, ref.shape[4]
        )


def load_rows(ref, layout, windows, length):
    if layout == "rows":
        return ref[...]
    return jnp.concatenate([load_window(ref, layout, w, length) for w in range(windows)], axis=0)


def split_heads(first, value):
    zero = jnp.zeros_like(value)
    return jnp.where(first, value, zero), jnp.where(first, zero, value)


def forward_kernel(
    dims, counts, x, gain, shift, w_in, w_out, w_expand, b_expand, w_reduce, *refs
):
    block, windows, length, width, hidden, in_layout, out_layout, first_clip, masked, n_alias = dims
    refs = refs[n_alias:]
    out, normed_o, triple_o, recip_o, raised_o, attended_o, middle_o, normed2_o, active_o, slope_o = refs
    rows = windows * length
    stream = load_rows(x, in_layout, windows, length).astype(WIDE)
    n, unused = normalize(stream)
    normed_o[...] = (n * gain[block, 0] + shift[block, 0]).astype(LOW)
    for c in chunks(3 * width, width):
        triple_o[:, c] = dot(normed_o[...], w_in[:, c]).astype(LOW)
    first = lax.broadcasted_iota(jnp.int32, (length, PAIR), 1) < HEAD_DIM
    ones_a, ones_b = split_heads(first, jnp.ones((length, PAIR), LOW))
    if masked:
        kept = counts[first_clip + pl.program_id(0)] * TUBE
        bias = jnp.where(
            lax.broadcasted_iota(jnp.int32, (1, length), 1) < kept, 0.0, -1e30
        ).astype(WIDE)
    for w in range(windows):
        span = slice(w * length, (w + 1) * length)
        for p, c in enumerate(chunks(width, PAIR)):
            queries = triple_o[span, c] * LOW(HEAD_DIM**-0.5)
            keys = triple_o[span, c.start + width : c.stop + width]
            values = triple_o[span, c.start + 2 * width : c.stop + 2 * width]
            raised = []
            for q in split_heads(first, queries):
                scores = dot(q, keys, 1, 1)
                if masked:
                    scores = scores + bias
                raised.append(
                    jnp.exp(scores - jnp.max(scores, axis=1, keepdims=True)).astype(LOW)
                )
            raised = jnp.concatenate(raised, axis=1)
            raised_o[w, p] = raised
            values_a, values_b = split_heads(first, values)
            sums = dot(
                raised,
                jnp.concatenate(
                    [
                        jnp.concatenate([values_a, ones_a], axis=1),
                        jnp.concatenate([values_b, ones_b], axis=1),
                    ],
                    axis=0,
                ),
            )
            recip = 1.0 / sums[:, PAIR:]
            recip_o[span, c] = recip
            attended_o[span, c] = (sums[:, :PAIR] * recip).astype(LOW)
    middle = stream + dot(attended_o[...], w_out[...])
    middle_o[...] = middle
    n, unused = normalize(middle)
    normed2_o[...] = (n * gain[block, 1] + shift[block, 1]).astype(LOW)
    total = middle
    for c in chunks(hidden, 512):
        pre = dot(normed2_o[...], w_expand[:, c]) + b_expand[block : block + 1, c]
        below = 0.5 + 0.5 * lax.erf(pre * HALF_ROOT)
        active = (pre * below).astype(LOW)
        active_o[:, c] = active
        slope_o[:, c] = (below + pre * (BELL_PEAK * jnp.exp(-0.5 * pre * pre))).astype(LOW)
        total = total + dot(active, w_reduce[c, :])
    total = total.astype(LOW)
    for w in range(windows):
        store_window(out, out_layout, w, length, total[w * length : (w + 1) * length])


def mlp_back_kernel(
    dims, g, slope, middle, gain, w_expand, w_reduce, *refs
):
    block, windows, length, width, hidden, g_layout, n_alias = dims
    refs = refs[n_alias:]
    rows_o, pre_o, mid_o, bias_o, gain_o, shift_o = refs
    grad = load_rows(g, g_layout, windows, length)
    rows_o[...] = grad
    first_step = pl.program_id(0) == 0

    @pl.when(first_step)
    def _():
        bias_o[...] = jnp.zeros_like(bias_o)
        gain_o[...] = jnp.zeros_like(gain_o)
        shift_o[...] = jnp.zeros_like(shift_o)

    total = None
    for c in chunks(hidden, 512):
        pre = (dot(grad, w_reduce[c, :], 1, 1) * slope[:, c].astype(WIDE)).astype(LOW)
        pre_o[:, c] = pre
        bias_o[:, c] += jnp.sum(pre.astype(WIDE), axis=0, keepdims=True)
        part = dot(pre, w_expand[:, c], 1, 1)
        total = part if total is None else total + part
    n, scale = normalize(middle[...])
    gain_o[...] += jnp.sum(total * n, axis=0, keepdims=True)
    shift_o[...] += jnp.sum(total, axis=0, keepdims=True)
    mid_o[...] = (
        grad.astype(WIDE) + normalize_back(n, scale, gain[block, 1], total)
    ).astype(mid_o.dtype)


def attention_back_kernel(
    dims, x, mid, triple, recip, raised, attended, gain, w_in, w_out, *refs
):
    block, windows, length, width, x_layout, out_layout, n_alias = dims
    refs = refs[n_alias:]
    out, triple_o, gain_o, shift_o, grad_s = refs
    first_step = pl.program_id(0) == 0

    @pl.when(first_step)
    def _():
        gain_o[...] = jnp.zeros_like(gain_o)
        shift_o[...] = jnp.zeros_like(shift_o)

    grad_s[...] = dot(mid[...].astype(LOW), w_out[...], 1, 1).astype(LOW)
    first = lax.broadcasted_iota(jnp.int32, (length, PAIR), 1) < HEAD_DIM
    minus = jnp.full((length, PAIR), -1.0, LOW)
    root = HEAD_DIM**-0.5
    for w in range(windows):
        span = slice(w * length, (w + 1) * length)
        for p, c in enumerate(chunks(width, PAIR)):
            c_keys = slice(c.start + width, c.stop + width)
            c_values = slice(c.start + 2 * width, c.stop + 2 * width)
            grad = grad_s[span, c]
            grad_wide = grad.astype(WIDE)
            share = recip[span, c]
            inner = (grad_wide * attended[span, c].astype(WIDE)).astype(LOW)
            grad_scaled = (grad_wide * share).astype(LOW)
            queries = (triple[span, c].astype(WIDE) * (share * root)).astype(LOW)
            keys = triple[span, c_keys] * LOW(root)
            values = jnp.concatenate([triple[span, c_values], minus], axis=1)
            scores = []
            for i, (a, b) in enumerate(zip(split_heads(first, grad), split_heads(first, inner))):
                delta = dot(jnp.concatenate([a, b], axis=1), values, 1, 1)
                e = raised[w, p, :, i * length : (i + 1) * length]
                scores.append((e.astype(WIDE) * delta).astype(LOW))
            grad_q = (
                dot(
                    jnp.concatenate(scores, axis=1),
                    jnp.concatenate(split_heads(first, keys), axis=0),
                )
                * share
            )
            grad_k = dot(
                jnp.concatenate(scores, axis=0),
                jnp.concatenate(split_heads(first, queries), axis=0),
                0,
                0,
            )
            grad_v = dot(
                jnp.concatenate(
                    [raised[w, p, :, :length], raised[w, p, :, length:]], axis=0
                ),
                jnp.concatenate(split_heads(first, grad_scaled), axis=0),
                0,
                0,
            )
            triple_o[span, c] = grad_q.astype(LOW)
            triple_o[span, c_keys] = grad_k.astype(LOW)
            triple_o[span, c_values] = grad_v.astype(LOW)
    total = dot(triple_o[...], w_in[...], 1, 1)
    n, scale = normalize(load_rows(x, x_layout, windows, length).astype(WIDE))
    gain_o[...] += jnp.sum(total * n, axis=0, keepdims=True)
    shift_o[...] += jnp.sum(total, axis=0, keepdims=True)
    grad_x = (
        mid[...].astype(WIDE) + normalize_back(n, scale, gain[block, 0], total)
    ).astype(LOW)
    for w in range(windows):
        store_window(out, out_layout, w, length, grad_x[w * length : (w + 1) * length])


def whole(shape):
    return pl.BlockSpec(shape, lambda i: (0,) * len(shape), pipeline_mode=pl.Buffered(1))


def layer(shape, block):
    return pl.BlockSpec(
        (None,) + shape, lambda i: (block,) + (0,) * len(shape), pipeline_mode=pl.Buffered(1)
    )


def row_spec(rows, width, first):
    return pl.BlockSpec((rows, width), lambda i: (i + first, 0))


def stream_spec(array_shape, layout, rows, first):
    if layout == "rows":
        return row_spec(rows, array_shape[-1], first)
    parts, clips, frames, tokens, width = array_shape
    return pl.BlockSpec((parts, 1, frames, tokens, width), lambda i: (0, i + first, 0, 0, 0))


ANY = pl.BlockSpec(memory_space=pl.ANY)


def params():
    return pltpu.CompilerParams(vmem_limit_bytes=VMEM_BYTES)


def cost(flops, size, exps=0):
    return pl.CostEstimate(flops=int(flops), bytes_accessed=int(size), transcendentals=int(exps))


def forward(
    block, x, in_layout, cut_shape, out_layout, weights, counts, first, clips, all_clips, length, saved, x_first
):
    gain, shift, w_in, w_out, w_expand, b_expand, w_reduce = weights
    width, hidden = w_expand.shape[1:]
    parts, frames, tokens = cut_shape
    windows = frames
    rows = windows * length
    total = all_clips * rows
    out_shape = jax.ShapeDtypeStruct((parts, clips, frames, tokens, width), LOW)
    kept = [
        ((total, width), LOW),
        ((total, 3 * width), LOW),
        ((total, width), WIDE),
        ((all_clips * windows, width // PAIR, length, 2 * length), LOW),
        ((total, width), LOW),
        ((total, width), WIDE),
        ((total, width), LOW),
        ((total, hidden), LOW),
        ((total, hidden), LOW),
    ]
    out_specs = [stream_spec(out_shape.shape, out_layout, rows, 0)]
    for shape, unused in kept:
        if len(shape) == 2:
            out_specs.append(row_spec(rows, shape[1], first))
        else:
            out_specs.append(
                pl.BlockSpec((windows,) + shape[1:], lambda i: (i + first, 0, 0, 0))
            )
    saved = [] if saved is None else list(saved)
    dims = (
        block, windows, length, width, hidden, in_layout, out_layout, first, block == 1, len(saved)
    )
    ins = [counts, x, gain, shift, w_in, w_out, w_expand, b_expand, w_reduce]
    in_specs = [
        pl.BlockSpec(memory_space=pltpu.SMEM),
        stream_spec(x.shape, in_layout, rows, x_first),
        whole(gain.shape),
        whole(shift.shape),
        layer(w_in.shape[1:], block),
        layer(w_out.shape[1:], block),
        layer(w_expand.shape[1:], block),
        whole(b_expand.shape),
        layer(w_reduce.shape[1:], block),
    ]
    got = pl.pallas_call(
        functools.partial(forward_kernel, dims),
        grid=(clips,),
        in_specs=in_specs + [ANY] * len(saved),
        out_specs=out_specs,
        out_shape=[out_shape] + [jax.ShapeDtypeStruct(*k) for k in kept],
        input_output_aliases={len(ins) + i: 1 + i for i in range(len(saved))},
        compiler_params=params(),
        cost_estimate=cost(
            clips * rows * 2 * (4 + 2 * hidden // width) * width * width,
            clips * rows * 40 * width,
            clips * rows * 2 * hidden,
        ),
        name=f"forward_{block}",
    )(*ins, *saved)
    return got[0], got[1:]


def mlp_back(block, g, g_layout, weights, saved, length, windows):
    gain, shift, w_in, w_out, w_expand, b_expand, w_reduce = weights
    width, hidden = w_expand.shape[1:]
    rows = windows * length
    total = saved[5].shape[0]
    dims = (block, windows, length, width, hidden, g_layout, 0)
    shapes = [
        ((total, width), LOW),
        ((total, hidden), LOW),
        ((total, width), WIDE),
        ((1, hidden), WIDE),
        ((1, width), WIDE),
        ((1, width), WIDE),
    ]
    return pl.pallas_call(
        functools.partial(mlp_back_kernel, dims),
        grid=(total // rows,),
        in_specs=[
            stream_spec(g.shape, g_layout, rows, 0),
            row_spec(rows, hidden, 0),
            row_spec(rows, width, 0),
            whole(gain.shape),
            layer(w_expand.shape[1:], block),
            layer(w_reduce.shape[1:], block),
        ],
        out_specs=[row_spec(rows, s[1], 0) for s, unused in shapes[:3]]
        + [pl.BlockSpec(s, lambda i: (0, 0)) for s, unused in shapes[3:]],
        out_shape=[jax.ShapeDtypeStruct(*s) for s in shapes],
        compiler_params=params(),
        cost_estimate=cost(total * 4 * hidden * width, total * 16 * width),
        name=f"mlp_back_{block}",
    )(g, saved[8], saved[5], gain, w_expand, w_reduce)


def attention_back(block, x, x_layout, mid, out_shape, out_layout, weights, saved, length, windows):
    gain, shift, w_in, w_out, w_expand, b_expand, w_reduce = weights
    width = w_out.shape[1]
    rows = windows * length
    total = mid.shape[0]
    normed, triple, recip, raised, attended = saved[:5]
    dims = (block, windows, length, width, x_layout, out_layout, 0)
    return pl.pallas_call(
        functools.partial(attention_back_kernel, dims),
        grid=(total // rows,),
        in_specs=[
            stream_spec(x.shape, x_layout, rows, 0),
            row_spec(rows, width, 0),
            row_spec(rows, 3 * width, 0),
            row_spec(rows, width, 0),
            pl.BlockSpec((windows,) + raised.shape[1:], lambda i: (i, 0, 0, 0)),
            row_spec(rows, width, 0),
            whole(gain.shape),
            layer(w_in.shape[1:], block),
            layer(w_out.shape[1:], block),
        ],
        out_specs=[
            stream_spec(out_shape, out_layout, rows, 0),
            row_spec(rows, 3 * width, 0),
            pl.BlockSpec((1, width), lambda i: (0, 0)),
            pl.BlockSpec((1, width), lambda i: (0, 0)),
        ],
        out_shape=[
            jax.ShapeDtypeStruct(out_shape, LOW),
            jax.ShapeDtypeStruct((total, 3 * width), LOW),
            jax.ShapeDtypeStruct((1, width), WIDE),
            jax.ShapeDtypeStruct((1, width), WIDE),
        ],
        scratch_shapes=[pltpu.VMEM((rows, width), LOW)],
        compiler_params=params(),
        cost_estimate=cost(total * (8 * width * width + 10 * length * width * 2), total * 40 * width),
        name=f"attention_back_{block}",
    )(x, mid, triple, recip, raised, attended, gain, w_in, w_out)


def split_rows(value, same, send, keep):
    value = value.astype(LOW)
    pairs, length = keep.shape[0], keep.shape[1]
    for p in range(pairs):
        low = value[2 * p * length : (2 * p + 1) * length]
        high = value[(2 * p + 1) * length : (2 * p + 2) * length]
        keep[p] = jnp.where(same, low, high)
        send[p] = jnp.where(same, high, low)


def mlp_weights_kernel(core, active, grad, normed2, pre, send_r, keep_r, send_e, keep_e):
    same = core[0] == 0
    split_rows(dot(active[...], grad[...], 0, 0), same, send_r, keep_r)
    split_rows(dot(normed2[...], pre[...], 0, 0), same, send_e, keep_e)


def attention_weights_kernel(core, normed, triple, attended, mid, send, keep):
    same = core[0] == 0
    step = pl.program_id(0)
    last = pl.num_programs(0) - 1

    @pl.when(step < last)
    def _():
        split_rows(dot(normed[...], triple[...], 0, 0), same, send, keep)

    @pl.when(step == last)
    def _():
        split_rows(dot(attended[...], mid[...].astype(LOW), 0, 0), same, send, keep)


def mlp_weights(core, active, grad, normed2, pre, parts):
    total, width = grad.shape
    hidden = pre.shape[1]
    steps = hidden // width
    group = parts // steps
    reduce_rows, expand_rows = hidden // parts, width // parts
    reduce_spec = pl.BlockSpec((group // 2, reduce_rows, width), lambda i: (i, 0, 0))
    expand_spec = pl.BlockSpec((parts // 2, expand_rows, width), lambda i: (0, i, 0))
    reduce_shape = jax.ShapeDtypeStruct((parts // 2, reduce_rows, width), LOW)
    expand_shape = jax.ShapeDtypeStruct((parts // 2, steps * expand_rows, width), LOW)
    return pl.pallas_call(
        mlp_weights_kernel,
        grid=(steps,),
        in_specs=[
            pl.BlockSpec(memory_space=pltpu.SMEM),
            pl.BlockSpec((total, width), lambda i: (0, i)),
            whole((total, width)),
            whole((total, width)),
            pl.BlockSpec((total, width), lambda i: (0, i)),
        ],
        out_specs=[reduce_spec, reduce_spec, expand_spec, expand_spec],
        out_shape=[reduce_shape, reduce_shape, expand_shape, expand_shape],
        compiler_params=params(),
        cost_estimate=cost(4 * total * width * hidden, 4 * total * (width + hidden)),
        name="mlp_weights",
    )(core, active, grad, normed2, pre)


def attention_weights(core, normed, triple, attended, mid, parts):
    total, width = normed.shape
    steps = triple.shape[1] // width + 1
    rows = width // parts
    spec = pl.BlockSpec((parts // 2, rows, width), lambda i: (0, i, 0))
    shape = jax.ShapeDtypeStruct((parts // 2, steps * rows, width), LOW)
    return pl.pallas_call(
        attention_weights_kernel,
        grid=(steps,),
        in_specs=[
            pl.BlockSpec(memory_space=pltpu.SMEM),
            whole((total, width)),
            pl.BlockSpec((total, width), lambda i: (0, jnp.minimum(i, steps - 2))),
            whole((total, width)),
            whole((total, width)),
        ],
        out_specs=[spec, spec],
        out_shape=[shape, shape],
        compiler_params=params(),
        cost_estimate=cost(2 * total * width * width * steps, 16 * total * width),
        name="attention_weights",
    )(core, normed, triple, attended, mid)


def sum_parts(value):
    return jnp.sum(value.astype(WIDE), axis=0)


def swap_core(value):
    size = lax.axis_size("frame")
    return lax.ppermute(value, "frame", [(i, i ^ 1) for i in range(size)])


def across_frames(value):
    size = lax.axis_size("frame")
    groups = [list(range(parity, size, 2)) for parity in range(2)]
    return sum_parts(lax.all_to_all(value, "frame", 0, 0, axis_index_groups=groups)).astype(LOW)


def across_clips(value):
    size = lax.axis_size("clip")
    blocks = value.reshape(size, value.shape[0] // size, value.shape[1])
    mine = sum_parts(lax.all_to_all(blocks, "clip", 0, 0)).astype(LOW)
    return lax.all_to_all(jnp.broadcast_to(mine[None], blocks.shape), "clip", 0, 0).reshape(value.shape)


def reduce_groups(pairs):
    got = [swap_core(send) for send, unused in pairs]
    total = jnp.concatenate(
        [
            (keep.astype(WIDE) + other.astype(WIDE)).astype(LOW)
            for (unused, keep), other in zip(pairs, got)
        ],
        axis=1,
    )
    return across_clips(across_frames(total))


def exchange(value):
    return lax.all_to_all(value, "frame", 0, 0)


def local(
    tokens,
    frame_counts,
    norm_gain,
    norm_bias,
    project_in,
    project_out,
    expand_weight,
    expand_bias,
    reduce_weight,
    cotangent,
):
    clips, frames, length, width = tokens.shape
    hidden = expand_weight.shape[2]
    parts = lax.axis_size("frame")
    owned = length // parts
    cut = (parts, frames, owned)
    half = clips // 2
    weights = (
        norm_gain, norm_bias, project_in, project_out, expand_weight, expand_bias, reduce_weight
    )
    core = (lax.axis_index("frame") % 2).astype(jnp.int32).reshape(1)

    cotangent_tubes = exchange(
        cotangent.reshape(clips, frames, parts, owned, width).transpose(2, 0, 1, 3, 4)
    )
    rows = tokens.reshape(-1, width)
    saved0 = None
    boundary = []
    for start in (0, half):
        out, saved0 = forward(
            0, rows, "rows", cut, "frames", weights, frame_counts, start, half, clips, length, saved0, start
        )
        boundary.append(exchange(out))
    saved1 = None
    mixed = []
    for index, start in enumerate((0, half)):
        out, saved1 = forward(
            1, boundary[index], "tubes", cut, "tubes", weights, frame_counts, start, half, clips, length, saved1, 0
        )
        mixed.append(exchange(out))
    boundary_all = jnp.concatenate(boundary, axis=1)

    grads = {}
    small = {}

    def back(block, g, g_layout, x, x_layout, out_shape, out_layout, saved):
        g_rows, pre, mid, bias_sum, gain2, shift2 = mlp_back(
            block, g, g_layout, weights, saved, length, frames
        )
        send_r, keep_r, send_e, keep_e = mlp_weights(core, saved[7], g_rows, saved[6], pre, parts)
        grads["mlp", block] = ((send_r, keep_r), (send_e, keep_e))
        out, triple, gain1, shift1 = attention_back(
            block, x, x_layout, mid, out_shape, out_layout, weights, saved, length, frames
        )
        pair = attention_weights(core, saved[0], triple, saved[4], mid, parts)
        grads["attention", block] = (pair,)
        small[block] = jnp.concatenate(
            [
                v.reshape(parts, -1)
                for v in (gain1, gain2, shift1, shift2, bias_sum)
            ],
            axis=1,
        )
        return out

    cut_shape = (parts, clips, frames, owned, width)
    grad_boundary = exchange(
        back(1, cotangent_tubes, "tubes", boundary_all, "tubes", cut_shape, "tubes", saved1)
    )
    grad_tokens = back(0, grad_boundary, "frames", rows, "rows", rows.shape, "rows", saved0)

    summed = {key: reduce_groups(value) for key, value in grads.items()}
    small_rows = jnp.stack([small[0], small[1]], axis=1)
    small_sum = lax.psum(
        lax.psum_scatter(small_rows, "frame", scatter_dimension=0, tiled=True), "clip"
    )[0]
    part = width // parts
    norm_gain_grad = small_sum[:, : 2 * part].reshape(2, 2, part)
    norm_bias_grad = small_sum[:, 2 * part : 4 * part].reshape(2, 2, part)
    expand_bias_grad = small_sum[:, 4 * part :]

    def columns(value):
        return value.reshape(-1, part, width).transpose(1, 0, 2).reshape(part, -1)

    per_block = []
    for block in range(2):
        mlp, attention = summed["mlp", block], summed["attention", block]
        per_block.append(
            (
                columns(attention[: 3 * part]),
                attention[3 * part :],
                columns(mlp[hidden // parts :]),
                mlp[: hidden // parts],
            )
        )
    stacked = [jnp.stack(pair).astype(WIDE) for pair in zip(*per_block)]
    mixed_all = (
        jnp.concatenate(mixed, axis=1).transpose(1, 2, 0, 3, 4).reshape(tokens.shape)
    )
    return (
        mixed_all,
        grad_tokens.reshape(tokens.shape),
        norm_gain_grad,
        norm_bias_grad,
        stacked[0],
        stacked[1],
        stacked[2],
        expand_bias_grad,
        stacked[3],
    )


def solution(mesh):
    in_specs = (
        P("clip", "frame", None, None),
        P("clip"),
        P(),
        P(),
        P(),
        P(),
        P(),
        P(),
        P(),
        P("clip", "frame", None, None),
    )
    out_specs = (
        P("clip", "frame", None, None),
        P("clip", "frame", None, None),
        P(None, None, "frame"),
        P(None, None, "frame"),
        P(None, "frame", None),
        P(None, "frame", None),
        P(None, "frame", None),
        P(None, "frame"),
        P(None, "frame", None),
    )
    return jax.shard_map(local, mesh=mesh, in_specs=in_specs, out_specs=out_specs, check_vma=False)
```

time: 2140 us -> 845 us (0.39)
  matrix products: 847 us -> 0 us
  other arithmetic: 497 us -> 48.8 us
  Pallas kernels: 0 us -> 377 us
  local copies, waits for them, and re-layouts: 317 us -> 21.4 us
  waiting for transfers between devices: 397 us -> 228 us
  blocking collectives: 34.5 us -> 87.7 us
  starting transfers between devices: 18.6 us -> 71 us
    dot_general x36 -> x0, matrix products: 847 us -> none  [the longest x2 161 us: attend_backward(): jnp.einsum('bftphe,bgtqhe->bthfpgq', grad_attended, values, preferred_ele...]
    pallas_call x0 -> x12, Pallas kernels: none -> 377 us  [the longest x4 145 us: forward(): pl.pallas_call(functools.partial(forward_kernel, dims), grid=(clips,), in...]
    convert_element_type x11 -> x10, other arithmetic: 362 us -> 21.7 us  [the longest x6 16.4 us: reduce_groups(): (keep.astype(WIDE) + other.astype(WIDE)).astype(LOW)]
    all_to_all x4 -> x16, waiting for transfers between devices: 70.9 us -> 227 us  [the longest x4 62.2 us: across_clips(): mine = sum_parts(lax.all_to_all(blocks, 'clip', 0, 0)).astype(LOW)]
    psum x1 -> x0, waiting for transfers between devices: 125 us -> none  [local(): lax.psum(shared_rows[9].astype(jnp.bfloat16), 'clip').astype(jnp.float32)]
    unnamed x17 -> x0, waiting for transfers between devices: 110 us -> none
    convert_element_type x7 -> x0, local copies, waits for them, and re-layouts: 98.2 us -> none  [the longest x2 60.6 us: attend_backward(): jnp.stack((grad_queries, grad_keys, grad_values), axis=-3).astype(LOWTYPE)]
    reduce_scatter x8 -> x0, waiting for transfers between devices: 90.7 us -> none  [the longest x1 57.8 us: local(): lax.psum_scatter(spatial_grads[4].astype(jnp.bfloat16), 'frame', scatter_...]
  transfers between devices with their start and end apart: 17 -> 22, of which waited for: 10 -> 12; matrix products, arithmetic and copies ran while one was open for 19% -> 7% of each run, Pallas kernels for 0% -> 26%
where the time goes in v1:
time: 845 us; the launch traced here: 836 us
  Pallas kernels  377 us (45%)
  waiting for transfers between devices  228 us (27%)
  blocking collectives  87.7 us (10%)
  starting transfers between devices  71 us (8%)
  other arithmetic  48.8 us (6%)
  local copies, waits for them, and re-layouts  21.4 us (3%)
    pallas_call x4, Pallas kernels, forward(): pl.pallas_call(functools.partial(forward_kernel, dims), grid=(clips,), in...  145 us
    pallas_call x2, Pallas kernels, attention_back(): pl.pallas_call(functools.partial(attention_back_kernel, dims), grid=(tota...  82.2 us
    pallas_call x2, Pallas kernels, mlp_back(): pl.pallas_call(functools.partial(mlp_back_kernel, dims), grid=(total // r...  63.3 us
    all_to_all x4, waiting for transfers between devices, across_clips(): mine = sum_parts(lax.all_to_all(blocks, 'clip', 0, 0)).astype(LOW)  62.2 us
    all_to_all x4, waiting for transfers between devices, exchange(): return lax.all_to_all(value, 'frame', 0, 0)  62 us
    pallas_call x2, Pallas kernels, mlp_weights(): pl.pallas_call(mlp_weights_kernel, grid=(steps,), in_specs=[pl.BlockSpec(...  52.6 us
    all_to_all x4, waiting for transfers between devices, across_frames(): lax.all_to_all(value, 'frame', 0, 0, axis_index_groups=groups)  52 us
    all_to_all x2, blocking collectives, exchange(): return lax.all_to_all(value, 'frame', 0, 0)  51.5 us
  transfers between devices with their start and end apart: 22, of which 12 were waited for; matrix products, arithmetic and copies ran while one was open for 7% of the time, Pallas kernels for 26%

profile of v1, /device:TPU:0, one launch (start us, length us, event | category | flops | bytes accessed | tf_op | source)
XLA Modules:
  0.0 835.7 jit_solution(13749647710093889369)
XLA Ops:
  0.6 36.1 %forward_0.2 = (bf16[8,2,2,32,768]{4,3,2,1,0:T(8,128)(2,1)}, bf16[2048,768]{1,0:T(8,128)(2,1)}, bf16[2048,2304]{1,0:T(8,128)(2,1)}, f32[2048,768]{1,0:T(8,128)},...) custom-call(s32[4]{0:T(128)} %counts.7, ...), custom_call_target="tpu_custom_call" | custom-call | flops 14495514624 | bytes 31457280 | tf_op jit(solution)/shard_map/forward_0/pallas_call | solution.py:320
  36.7 36.2 %forward_0.3 = (bf16[8,2,2,32,768]{4,3,2,1,0:T(8,128)(2,1)}, bf16[2048,768]{1,0:T(8,128)(2,1)}, bf16[2048,2304]{1,0:T(8,128)(2,1)}, f32[2048,768]{1,0:T(8,128)},...) custom-call(s32[4]{0:T(128)} %counts.7, ...), custom_call_target="tpu_custom_call", output_to_operand_aliasing={{1}: (9, {}), {2}: (10, {}), {3}: (11, {}), {4}: (12, {}), ... | custom-call | flops 14495514624 | bytes 31457280 | tf_op jit(solution)/shard_map/forward_0/pallas_call | solution.py:320
  72.9 26.2 %all_to_all.90.x = bf16[8,2,2,32,768]{4,3,2,1,0:T(8,128)(2,1)S(1)} all-to-all(bf16[8,2,2,32,768]{4,3,2,1,0:T(8,128)(2,1)} %get-tuple-element.92), channel_id=1, replica_groups=mesh['clip'=4,'frame'=8] {'frame'}, dimensions={0} | all-to-all | bytes 3145728 | tf_op jit(solution)/shard_map/all_to_all | solution.py:529
  106.5 17.1 %all-to-all-done.x = bf16[8,2,2,32,768]{4,3,2,1,0:T(8,128)(2,1)S(1)} async-done(((bf16[8,2,2,32,768]{4,3,2,1,0:T(8,128)(2,1)}), bf16[8,2,2,32,768]{4,3,2,1,0:T(8,128)(2,1)S(1)}, u32[]{:S(2)}, u32[]{:S(2)}) %all-to-all-start) | async-done | bytes 1572896 | tf_op jit(solution)/shard_map/all_to_all | solution.py:529
  123.7 4.9 all-to-all-start.4
  130.5 36.1 %forward_1.2 = (bf16[8,2,2,32,768]{4,3,2,1,0:T(8,128)(2,1)}, bf16[2048,768]{1,0:T(8,128)(2,1)}, bf16[2048,2304]{1,0:T(8,128)(2,1)}, f32[2048,768]{1,0:T(8,128)},...) custom-call(s32[4]{0:T(128)} %counts.7, ...), custom_call_target="tpu_custom_call" | custom-call | flops 14495514624 | bytes 31457280 | tf_op jit(solution)/shard_map/forward_1/pallas_call | solution.py:320
  166.6 36.2 %forward_1.3 = (bf16[8,2,2,32,768]{4,3,2,1,0:T(8,128)(2,1)}, bf16[2048,768]{1,0:T(8,128)(2,1)}, bf16[2048,2304]{1,0:T(8,128)(2,1)}, f32[2048,768]{1,0:T(8,128)},...) custom-call(s32[4]{0:T(128)} %counts.7, ...), custom_call_target="tpu_custom_call", output_to_operand_aliasing={{1}: (9, {}), {2}: (10, {}), {3}: (11, {}), {4}: (12, {}), ... | custom-call | flops 14495514624 | bytes 31457280 | tf_op jit(solution)/shard_map/forward_1/pallas_call | solution.py:320
  202.8 31.7 %mlp_back_1.1 = (bf16[2048,768]{1,0:T(8,128)(2,1)}, bf16[2048,3072]{1,0:T(8,128)(2,1)}, f32[2048,768]{1,0:T(8,128)}, f32[1,3072]{1,0:T(1,128)}, f32[1,768]{1,0:T(1,128)}, /*index=5*/f32[1,768]{1,0:T(1,128)}) custom-call(bf16[8,4,2,32,768]{4,3,2,1,0:T(8,128)(2,1)} %all-to-all-done.4.g, bf16[2048,3072]{1,0:T(8,128)(2,1)} %get-tuple-element.103.slope, ...), custom_call_target="tpu_custom_call" | custom-call | flops 19327352832 | bytes 25165824 | tf_op jit(solution)/shard_map/mlp_back_1/pallas_call | solution.py:352
  234.5 41.3 %attention_back_1.1 = (bf16[8,4,2,32,768]{4,3,2,1,0:T(8,128)(2,1)}, bf16[2048,2304]{1,0:T(8,128)(2,1)}, f32[1,768]{1,0:T(1,128)}, f32[1,768]{1,0:T(1,128)}) custom-call(bf16[8,4,2,32,768]{4,3,2,1,0:T(8,128)(2,1)} %pad_maximum_fusion.2.x, f32[2048,768]{1,0:T(8,128)} %get-tuple-element.105.mid, bf16[2048,2304]{1,0:T(8,128)(2,1)} %get-tuple-element.106.triple, ...), custom_call_target="tpu_custom_call" | custom-call | flops 17716740096 | bytes 62914560 | tf_op jit(solution)/shard_map/attention_back_1/pallas_call | solution.py:379
  275.8 17.4 %attention_weights.3 = (bf16[4,384,768]{2,1,0:T(8,128)(2,1)}, bf16[4,384,768]{2,1,0:T(8,128)(2,1)}) custom-call(s32[1]{0:T(128)} %bitcast.8.core, bf16[2048,768]{1,0:T(8,128)(2,1)} %get-tuple-element.133.normed, bf16[2048,2304]{1,0:T(8,128)(2,1)} %get-tuple-element.134.triple, bf16[2048,768]{1,0:T(8,128)(2,1)} %get-tuple-element.109.attended, ...), custom_call_target="tpu_custom_call" | custom-call | flops 9663676416 | bytes 25165824 | tf_op jit(solution)/shard_map/attention_weights/pallas_call | solution.py:476
  293.6 25.4 %all_to_all.91 = bf16[8,2,2,32,768]{4,3,2,1,0:T(8,128)(2,1)} all-to-all(bf16[8,2,2,32,768]{4,3,2,1,0:T(8,128)(2,1)} %get-tuple-element.102), channel_id=1, replica_groups=mesh['clip'=4,'frame'=8] {'frame'}, dimensions={0} | all-to-all | bytes 3145728 | tf_op jit(solution)/shard_map/all_to_all | solution.py:529
  327.1 17.4 %all-to-all-done.1 = bf16[8,2,2,32,768]{4,3,2,1,0:T(8,128)(2,1)} async-done(((bf16[8,2,2,32,768]{4,3,2,1,0:T(8,128)(2,1)}), bf16[8,2,2,32,768]{4,3,2,1,0:T(8,128)(2,1)}, u32[]{:S(2)}, u32[]{:S(2)}) %all-to-all-start.1) | async-done | bytes 1572896 | tf_op jit(solution)/shard_map/all_to_all | solution.py:529
  349.0 26.1 %mlp_weights.3 = (bf16[4,384,768]{2,1,0:T(8,128)(2,1)}, bf16[4,384,768]{2,1,0:T(8,128)(2,1)}, bf16[4,384,768]{2,1,0:T(8,128)(2,1)}, bf16[4,384,768]{2,1,0:T(8,128)(2,1)}) custom-call(s32[1]{0:T(128)} %bitcast.8.core, bf16[2048,3072]{1,0:T(8,128)(2,1)} %get-tuple-element.145.active, bf16[2048,768]{1,0:T(8,128)(2,1)} %get-tuple-element.146.grad, ...), custom_call_target="tpu_custom_call" | custom-call | flops 19327352832 | bytes 31457280 | tf_op jit(solution)/shard_map/mlp_weights/pallas_call | solution.py:452
  376.1 4.6 all-to-all-start.5
  391.1 27.5 %all-to-all-done.5.g = bf16[8,4,2,32,768]{4,3,2,1,0:T(8,128)(2,1)} async-done(((bf16[8,4,2,32,768]{4,3,2,1,0:T(8,128)(2,1)}), bf16[8,4,2,32,768]{4,3,2,1,0:T(8,128)(2,1)}, u32[]{:S(2)}, u32[]{:S(2)}) %all-to-all-start.5) | async-done | bytes 3145760 | tf_op jit(solution)/shard_map/all_to_all | solution.py:529
  418.5 4.9 all-to-all-start.10
  423.4 31.6 %mlp_back_0.1 = (bf16[2048,768]{1,0:T(8,128)(2,1)}, bf16[2048,3072]{1,0:T(8,128)(2,1)}, f32[2048,768]{1,0:T(8,128)}, f32[1,3072]{1,0:T(1,128)}, f32[1,768]{1,0:T(1,128)}, /*index=5*/f32[1,768]{1,0:T(1,128)}) custom-call(bf16[8,4,2,32,768]{4,3,2,1,0:T(8,128)(2,1)} %all-to-all-done.5.g, bf16[2048,3072]{1,0:T(8,128)(2,1)} %get-tuple-element.111.slope, ...), custom_call_target="tpu_custom_call" | custom-call | flops 19327352832 | bytes 25165824 | tf_op jit(solution)/shard_map/mlp_back_0/pallas_call | solution.py:352
  455.0 5.4 all-to-all-start.15
  460.4 40.9 %attention_back_0.1 = (bf16[2048,768]{1,0:T(8,128)(2,1)}, bf16[2048,2304]{1,0:T(8,128)(2,1)}, f32[1,768]{1,0:T(1,128)}, f32[1,768]{1,0:T(1,128)}) custom-call(bf16[2048,768]{1,0:T(8,128)(2,1)} %bitcast.34, f32[2048,768]{1,0:T(8,128)} %get-tuple-element.113.mid, bf16[2048,2304]{1,0:T(8,128)(2,1)} %get-tuple-element.114.triple, ...), custom_call_target="tpu_custom_call" | custom-call | flops 17716740096 | bytes 62914560 | tf_op jit(solution)/shard_map/attention_back_0/pallas_call | solution.py:379
  501.3 17.4 %attention_weights.2 = (bf16[4,384,768]{2,1,0:T(8,128)(2,1)}, bf16[4,384,768]{2,1,0:T(8,128)(2,1)}) custom-call(s32[1]{0:T(128)} %bitcast.8.core, bf16[2048,768]{1,0:T(8,128)(2,1)} %get-tuple-element.129.normed, bf16[2048,2304]{1,0:T(8,128)(2,1)} %get-tuple-element.130.triple, bf16[2048,768]{1,0:T(8,128)(2,1)} %get-tuple-element.117.attended, ...), custom_call_target="tpu_custom_call" | custom-call | flops 9663676416 | bytes 25165824 | tf_op jit(solution)/shard_map/attention_weights/pallas_call | solution.py:476
  519.6 5.2 all-to-all-start.11
  528.5 12.9 %all-to-all-done.11 = bf16[4,96,768]{2,1,0:T(8,128)(2,1)S(1)} async-done(((bf16[4,96,768]{2,1,0:T(8,128)(2,1)}), bf16[4,96,768]{2,1,0:T(8,128)(2,1)S(1)}, u32[]{:S(2)}, u32[]{:S(2)}) %all-to-all-start.11) | async-done | bytes 589856 | tf_op jit(solution)/shard_map/all_to_all | solution.py:513
  545.9 26.6 %mlp_weights.2 = (bf16[4,384,768]{2,1,0:T(8,128)(2,1)}, bf16[4,384,768]{2,1,0:T(8,128)(2,1)}, bf16[4,384,768]{2,1,0:T(8,128)(2,1)}, bf16[4,384,768]{2,1,0:T(8,128)(2,1)}) custom-call(s32[1]{0:T(128)} %bitcast.8.core, bf16[2048,3072]{1,0:T(8,128)(2,1)} %get-tuple-element.137.active, bf16[2048,768]{1,0:T(8,128)(2,1)} %get-tuple-element.138.grad, ...), custom_call_target="tpu_custom_call" | custom-call | flops 19327352832 | bytes 31457280 | tf_op jit(solution)/shard_map/mlp_weights/pallas_call | solution.py:452
  584.1 26.0 %all-to-all-done.16 = bf16[4,192,768]{2,1,0:T(8,128)(2,1)S(1)} async-done(((bf16[4,192,768]{2,1,0:T(8,128)(2,1)}), bf16[4,192,768]{2,1,0:T(8,128)(2,1)S(1)}, u32[]{:S(2)}, u32[]{:S(2)}) %all-to-all-start.16) | async-done | bytes 1179680 | tf_op jit(solution)/shard_map/all_to_all | solution.py:512
  621.4 8.5 %all-to-all-done.7 = bf16[4,96,768]{2,1,0:T(8,128)(2,1)} async-done(((bf16[4,96,768]{2,1,0:T(8,128)(2,1)}), bf16[4,96,768]{2,1,0:T(8,128)(2,1)}, u32[]{:S(2)}, u32[]{:S(2)}) %all-to-all-start.7) | async-done | bytes 589856 | tf_op jit(solution)/shard_map/all_to_all | solution.py:512
  629.9 5.0 all-to-all-start.12
  636.1 51.6 %all-to-all-done.12 = bf16[4,768,768]{2,1,0:T(8,128)(2,1)} async-done(((bf16[4,768,768]{2,1,0:T(8,128)(2,1)}), bf16[4,768,768]{2,1,0:T(8,128)(2,1)}, u32[]{:S(2)}, u32[]{:S(2)}) %all-to-all-start.12) | async-done | bytes 4718624 | tf_op jit(solution)/shard_map/all_to_all | solution.py:506
  696.3 11.0 %all-to-all-done.8 = bf16[4,96,768]{2,1,0:T(8,128)(2,1)S(1)} async-done(((bf16[4,96,768]{2,1,0:T(8,128)(2,1)}), bf16[4,96,768]{2,1,0:T(8,128)(2,1)S(1)}, u32[]{:S(2)}, u32[]{:S(2)}) %all-to-all-start.8) | async-done | bytes 589856 | tf_op jit(solution)/shard_map/all_to_all | solution.py:513
  712.0 27.7 %all-to-all-done.13 = bf16[4,192,768]{2,1,0:T(8,128)(2,1)S(1)} async-done(((bf16[4,192,768]{2,1,0:T(8,128)(2,1)}), bf16[4,192,768]{2,1,0:T(8,128)(2,1)S(1)}, u32[]{:S(2)}, u32[]{:S(2)}) %all-to-all-start.13) | async-done | bytes 1179680 | tf_op jit(solution)/shard_map/all_to_all | solution.py:512
  745.2 27.1 %all-to-all-done.17 = bf16[4,192,768]{2,1,0:T(8,128)(2,1)S(1)} async-done(((bf16[4,192,768]{2,1,0:T(8,128)(2,1)}), bf16[4,192,768]{2,1,0:T(8,128)(2,1)S(1)}, u32[]{:S(2)}, u32[]{:S(2)}) %all-to-all-start.17) | async-done | bytes 1179680 | tf_op jit(solution)/shard_map/all_to_all | solution.py:513
  785.2 23.4 %all-reduce = f32[8,2,768]{2,1,0:T(2,128)S(1)} all-reduce(f32[8,2,768]{2,1,0:T(2,128)S(1)} %pad_maximum_fusion.3), channel_id=2, replica_groups=mesh['clip'=4,'frame'=8] {'frame'}, use_global_device_ids=true, to_apply=%region_0.1.clone | all-reduce | flops 12288 | bytes 98304
  809.2 12.7 %psum.7 = f32[2,768]{1,0:T(2,128)S(1)} all-reduce(f32[2,768]{1,0:T(2,128)S(1)} %dynamic-slice_bitcast_fusion), channel_id=1, replica_groups=mesh['clip'=4,'frame'=8] {'clip'}, use_global_device_ids=true, to_apply=%region_1.2 | all-reduce | flops 1536 | bytes 12288 | tf_op jit(solution)/shard_map/psum | solution.py:606
  (152 shorter events, 112.2 us)
Async XLA Ops:
  99.1 29.4 %copy-start = (bf16[8,2,2,32,768]{4,3,2,1,0:T(8,128)(2,1)}, bf16[8,2,2,32,768]{4,3,2,1,0:T(8,128)(2,1)S(1)}, u32[]{:S(2)}) copy-start(bf16[8,2,2,32,768]{4,3,2,1,0:T(8,128)(2,1)S(1)} %all_to_all.90.x) | copy-start | bytes 4718596
  99.1 24.5 %all-to-all-start = ((bf16[8,2,2,32,768]{4,3,2,1,0:T(8,128)(2,1)}), bf16[8,2,2,32,768]{4,3,2,1,0:T(8,128)(2,1)S(1)}, u32[]{:S(2)}, u32[]{:S(2)}) async-start(bf16[8,2,2,32,768]{4,3,2,1,0:T(8,128)(2,1)} %get-tuple-element.81), calls=%async_computation | async-start | bytes 3145728 | tf_op jit(solution)/shard_map/all_to_all | solution.py:529
  123.7 4.9 copy-start.1
  123.7 79.1 %all-to-all-start.4 = ((bf16[8,4,2,32,768]{4,3,2,1,0:T(8,128)(2,1)}), bf16[8,4,2,32,768]{4,3,2,1,0:T(8,128)(2,1)}, u32[]{:S(2)}, u32[]{:S(2)}) async-start(bf16[8,4,2,32,768]{4,3,2,1,0:T(8,128)(2,1)} %bitcast.31), calls=%async_computation.4 | async-start | bytes 6291456 | tf_op jit(solution)/shard_map/all_to_all | solution.py:529
  293.2 30.3 %collective-permute-start.1 = (bf16[4,384,768]{2,1,0:T(8,128)(2,1)}, bf16[4,384,768]{2,1,0:T(8,128)(2,1)}, u32[]{:S(2)}, u32[]{:S(2)}) collective-permute-start(bf16[4,384,768]{2,1,0:T(8,128)(2,1)} %get-tuple-element.136), channel_id=1, source_target_pairs={{0,1},{1,0},{2,3},{3,2},{4,5},{5,4},{6,7},{7,6},{8,9},{9,8},{10,11... | collective-permute-start | bytes 7077896 | tf_op jit(solution)/shard_map/ppermute | solution.py:500
  293.6 29.9 %copy-start.9 = (bf16[4,384,768]{2,1,0:T(8,128)(2,1)S(1)}, bf16[4,384,768]{2,1,0:T(8,128)(2,1)}, u32[]{:S(2)}) copy-start(bf16[4,384,768]{2,1,0:T(8,128)(2,1)} %get-tuple-element.135) | copy-start | bytes 7077892
  319.0 25.5 %all-to-all-start.1 = ((bf16[8,2,2,32,768]{4,3,2,1,0:T(8,128)(2,1)}), bf16[8,2,2,32,768]{4,3,2,1,0:T(8,128)(2,1)}, u32[]{:S(2)}, u32[]{:S(2)}) async-start(bf16[8,2,2,32,768]{4,3,2,1,0:T(8,128)(2,1)} %get-tuple-element.82), calls=%async_computation.1 | async-start | bytes 3145728 | tf_op jit(solution)/shard_map/all_to_all | solution.py:529
  344.5 31.5 %all-to-all-start.9 = ((bf16[4,384,768]{2,1,0:T(8,128)(2,1)}), bf16[4,384,768]{2,1,0:T(8,128)(2,1)}, u32[]{:S(2)}, u32[]{:S(2)}) async-start(bf16[4,384,768]{2,1,0:T(8,128)(2,1)} %add_convert_fusion.4), calls=%async_computation.9 | async-start | bytes 4718592 | tf_op jit(solution)/shard_map/all_to_all | solution.py:506
  375.1 5.5 collective-permute-start.4
  375.1 8.2 collective-permute-start.5
  376.1 4.6 copy-start.7
  376.1 42.5 %all-to-all-start.5 = ((bf16[8,4,2,32,768]{4,3,2,1,0:T(8,128)(2,1)}), bf16[8,4,2,32,768]{4,3,2,1,0:T(8,128)(2,1)}, u32[]{:S(2)}, u32[]{:S(2)}) async-start(bf16[8,4,2,32,768]{4,3,2,1,0:T(8,128)(2,1)} %get-tuple-element.110), calls=%async_computation.5 | async-start | bytes 6291456 | tf_op jit(solution)/shard_map/all_to_all | solution.py:529
  418.5 36.5 %all-to-all-start.10 = ((bf16[4,96,768]{2,1,0:T(8,128)(2,1)}), bf16[4,96,768]{2,1,0:T(8,128)(2,1)S(1)}, u32[]{:S(2)}, u32[]{:S(2)}) async-start(bf16[4,96,768]{2,1,0:T(8,128)(2,1)} %bitcast.11), calls=%async_computation.10 | async-start | bytes 1179648 | tf_op jit(solution)/shard_map/all_to_all | solution.py:512
  455.0 63.8 %all-to-all-start.15 = ((bf16[4,768,768]{2,1,0:T(8,128)(2,1)}), bf16[4,768,768]{2,1,0:T(8,128)(2,1)}, u32[]{:S(2)}, u32[]{:S(2)}) async-start(bf16[4,768,768]{2,1,0:T(8,128)(2,1)} %pad_maximum_fusion.1), calls=%async_computation.15 | async-start | bytes 9437184 | tf_op jit(solution)/shard_map/all_to_all | solution.py:506
  518.7 6.2 copy-start.8
  518.7 6.2 collective-permute-start
  519.6 21.8 %all-to-all-start.11 = ((bf16[4,96,768]{2,1,0:T(8,128)(2,1)}), bf16[4,96,768]{2,1,0:T(8,128)(2,1)S(1)}, u32[]{:S(2)}, u32[]{:S(2)}) async-start(bf16[4,96,768]{2,1,0:T(8,128)(2,1)} %broadcast_in_dim.9), calls=%async_computation.11 | async-start | bytes 1179648 | tf_op jit(solution)/shard_map/all_to_all | solution.py:513
  541.4 31.1 %copy-start.10 = (bf16[4,96,768]{2,1,0:T(8,128)(2,1)}, bf16[4,96,768]{2,1,0:T(8,128)(2,1)S(1)}, u32[]{:S(2)}) copy-start(bf16[4,96,768]{2,1,0:T(8,128)(2,1)S(1)} %all-to-all-done.11) | copy-start | bytes 1769476
  541.4 36.0 %all-to-all-start.6 = ((bf16[4,384,768]{2,1,0:T(8,128)(2,1)}), bf16[4,384,768]{2,1,0:T(8,128)(2,1)}, u32[]{:S(2)}, u32[]{:S(2)}) async-start(bf16[4,384,768]{2,1,0:T(8,128)(2,1)} %add_convert_fusion.5), calls=%async_computation.6 | async-start | bytes 4718592 | tf_op jit(solution)/shard_map/all_to_all | solution.py:506
  572.5 41.8 %collective-permute-start.2 = (bf16[4,384,768]{2,1,0:T(8,128)(2,1)}, bf16[4,384,768]{2,1,0:T(8,128)(2,1)}, u32[]{:S(2)}, u32[]{:S(2)}) collective-permute-start(bf16[4,384,768]{2,1,0:T(8,128)(2,1)} %get-tuple-element.142), channel_id=1, source_target_pairs={{0,1},{1,0},{2,3},{3,2},{4,5},{5,4},{6,7},{7,6},{8,9},{9,8},{10,11... | collective-permute-start | bytes 7077896 | tf_op jit(solution)/shard_map/ppermute | solution.py:500
  572.6 44.1 %collective-permute-start.3 = (bf16[4,384,768]{2,1,0:T(8,128)(2,1)}, bf16[4,384,768]{2,1,0:T(8,128)(2,1)}, u32[]{:S(2)}, u32[]{:S(2)}) collective-permute-start(bf16[4,384,768]{2,1,0:T(8,128)(2,1)} %get-tuple-element.144), channel_id=1, source_target_pairs={{0,1},{1,0},{2,3},{3,2},{4,5},{5,4},{6,7},{7,6},{8,9},{9,8},{10,11... | collective-permute-start | bytes 7077896 | tf_op jit(solution)/shard_map/ppermute | solution.py:500
  577.5 36.9 %copy-start.5 = (bf16[4,384,768]{2,1,0:T(8,128)(2,1)S(1)}, bf16[4,384,768]{2,1,0:T(8,128)(2,1)}, u32[]{:S(2)}) copy-start(bf16[4,384,768]{2,1,0:T(8,128)(2,1)} %get-tuple-element.141) | copy-start | bytes 7077892
  577.5 32.7 %all-to-all-start.16 = ((bf16[4,192,768]{2,1,0:T(8,128)(2,1)}), bf16[4,192,768]{2,1,0:T(8,128)(2,1)S(1)}, u32[]{:S(2)}, u32[]{:S(2)}) async-start(bf16[4,192,768]{2,1,0:T(8,128)(2,1)} %bitcast.16), calls=%async_computation.16 | async-start | bytes 2359296 | tf_op jit(solution)/shard_map/all_to_all | solution.py:512
  610.1 19.8 %all-to-all-start.7 = ((bf16[4,96,768]{2,1,0:T(8,128)(2,1)}), bf16[4,96,768]{2,1,0:T(8,128)(2,1)}, u32[]{:S(2)}, u32[]{:S(2)}) async-start(bf16[4,96,768]{2,1,0:T(8,128)(2,1)} %bitcast.41), calls=%async_computation.7 | async-start | bytes 1179648 | tf_op jit(solution)/shard_map/all_to_all | solution.py:512
  629.9 57.7 %all-to-all-start.12 = ((bf16[4,768,768]{2,1,0:T(8,128)(2,1)}), bf16[4,768,768]{2,1,0:T(8,128)(2,1)}, u32[]{:S(2)}, u32[]{:S(2)}) async-start(bf16[4,768,768]{2,1,0:T(8,128)(2,1)} %pad_maximum_fusion), calls=%async_computation.12 | async-start | bytes 9437184 | tf_op jit(solution)/shard_map/all_to_all | solution.py:506
  688.5 18.9 %all-to-all-start.8 = ((bf16[4,96,768]{2,1,0:T(8,128)(2,1)}), bf16[4,96,768]{2,1,0:T(8,128)(2,1)S(1)}, u32[]{:S(2)}, u32[]{:S(2)}) async-start(bf16[4,96,768]{2,1,0:T(8,128)(2,1)} %broadcast_in_dim.8), calls=%async_computation.8 | async-start | bytes 1179648 | tf_op jit(solution)/shard_map/all_to_all | solution.py:513
  708.2 31.5 %all-to-all-start.13 = ((bf16[4,192,768]{2,1,0:T(8,128)(2,1)}), bf16[4,192,768]{2,1,0:T(8,128)(2,1)S(1)}, u32[]{:S(2)}, u32[]{:S(2)}) async-start(bf16[4,192,768]{2,1,0:T(8,128)(2,1)} %bitcast.13), calls=%async_computation.13 | async-start | bytes 2359296 | tf_op jit(solution)/shard_map/all_to_all | solution.py:512
  711.7 32.6 %copy-start.23 = (u32[32]{0:T(128)S(1)}, u32[32]{0:T(128)}, u32[]{:S(2)}) copy-start(u32[32]{0:T(128)} %constant.31) | copy-start | bytes 388
  740.8 31.5 %all-to-all-start.17 = ((bf16[4,192,768]{2,1,0:T(8,128)(2,1)}), bf16[4,192,768]{2,1,0:T(8,128)(2,1)S(1)}, u32[]{:S(2)}, u32[]{:S(2)}) async-start(bf16[4,192,768]{2,1,0:T(8,128)(2,1)} %broadcast_in_dim.11), calls=%async_computation.17 | async-start | bytes 2359296 | tf_op jit(solution)/shard_map/all_to_all | solution.py:513
  773.7 56.3 %all-to-all-start.14 = ((bf16[4,192,768]{2,1,0:T(8,128)(2,1)}), bf16[4,192,768]{2,1,0:T(8,128)(2,1)}, u32[]{:S(2)}, u32[]{:S(2)}) async-start(bf16[4,192,768]{2,1,0:T(8,128)(2,1)} %broadcast_in_dim.10), calls=%async_computation.14 | async-start | bytes 2359296 | tf_op jit(solution)/shard_map/all_to_all | solution.py:513
  778.1 3.7 copy-start.15
  783.9 42.0 %copy-start.12 = (bf16[4,96,768]{2,1,0:T(8,128)(2,1)S(1)}, bf16[4,96,768]{2,1,0:T(8,128)(2,1)}, u32[]{:S(2)}) copy-start(bf16[4,96,768]{2,1,0:T(8,128)(2,1)} %copy-done.11) | copy-start | bytes 1769476
  (16 other events, 39.4 us)

commit v2 on v1

v2 whole, which is shorter than its diff:
```python
import functools

import jax
import jax.numpy as jnp
from jax import lax
from jax.experimental import pallas as pl
from jax.experimental.pallas import tpu as pltpu
from jax.sharding import PartitionSpec as P

HEAD_DIM = 64
TUBE = 16
PAIR = 2 * HEAD_DIM
EPSILON = 1e-05
HALF_ROOT = 0.7071067811865476
BELL_PEAK = 0.3989422804014327
LOW = jnp.bfloat16
WIDE = jnp.float32
VMEM_BYTES = 63 * 1024 * 1024
SMALL_ROWS = 16


def dot(left, right, left_dim=1, right_dim=0):
    return lax.dot_general(
        left, right, (((left_dim,), (right_dim,)), ((), ())), preferred_element_type=WIDE
    )


def normalize(x):
    center = x - jnp.mean(x, axis=-1, keepdims=True)
    scale = lax.rsqrt(jnp.mean(center * center, axis=-1, keepdims=True) + EPSILON)
    return center * scale, scale


def normalize_back(n, scale, gain, grad):
    e = grad * gain
    return scale * (
        e - jnp.mean(e, axis=-1, keepdims=True) - n * jnp.mean(e * n, axis=-1, keepdims=True)
    )


def chunks(total, size):
    return [slice(start, start + size) for start in range(0, total, size)]


def split_heads(first, value):
    zero = jnp.zeros_like(value)
    return jnp.where(first, value, zero), jnp.where(first, zero, value)


def load_window(ref, layout, window):
    if layout == "tokens":
        return ref[0, window]
    if layout == "frames":
        block = ref[:, 0, window]
    else:
        block = ref[:, 0, :, window * TUBE : (window + 1) * TUBE, :]
    return block.reshape(-1, block.shape[-1])


def load_rows(ref, layout, windows):
    if layout == "rows":
        return ref[...]
    return jnp.concatenate([load_window(ref, layout, w) for w in range(windows)], axis=0)


def store_window(ref, layout, window, value):
    if layout == "tokens":
        ref[0, window] = value
    elif layout == "frames":
        ref[:, 0, window] = value.reshape(ref.shape[0], -1, ref.shape[-1])
    else:
        tube = slice(window * TUBE, (window + 1) * TUBE)
        ref[:, 0, :, tube, :] = value.reshape(ref.shape[0], -1, TUBE, ref.shape[-1])


def store_rows(ref, layout, windows, value):
    length = value.shape[0] // windows
    for w in range(windows):
        store_window(ref, layout, w, value[w * length : (w + 1) * length])


def forward_kernel(dims, counts, x, *refs):
    block, windows, length, width, hidden, n_alias, first_clip, passes = dims
    if block == 0:
        cotangent, refs = refs[0], refs[1:]
    gain, shift, w_in, w_out, w_expand, b_expand, w_reduce = refs[:7]
    refs = refs[7 + n_alias :]
    if passes:
        refs = refs[1:]
    if block == 0:
        out, *refs = refs
    normed_o, triple_o, recip_o, raised_o, attended_o, middle_o, normed2_o, active_o, slope_o, extra_o = refs
    stream = load_rows(x, ("tokens", "tubes")[block], windows)
    if block == 0:
        for w in range(windows):
            store_window(extra_o, "frames", w, load_window(cotangent, "tokens", w))
    else:
        extra_o[...] = stream
    stream = stream.astype(WIDE)
    n, unused = normalize(stream)
    normed_o[...] = (n * gain[block, 0] + shift[block, 0]).astype(LOW)
    for c in chunks(3 * width, width):
        triple_o[:, c] = dot(normed_o[...], w_in[:, c]).astype(LOW)
    first = lax.broadcasted_iota(jnp.int32, (length, PAIR), 1) < HEAD_DIM
    ones_a, ones_b = split_heads(first, jnp.ones((length, PAIR), LOW))
    if block == 1:
        key = lax.broadcasted_iota(jnp.int32, (1, length), 1)
        kept = key // TUBE < counts[first_clip + pl.program_id(0)]
        bias = jnp.where(kept, 0.0, -1e30).astype(WIDE)
    for w in range(windows):
        span = slice(w * length, (w + 1) * length)
        for p, c in enumerate(chunks(width, PAIR)):
            queries = triple_o[span, c] * LOW(HEAD_DIM**-0.5)
            keys = triple_o[span, c.start + width : c.stop + width]
            values = triple_o[span, c.start + 2 * width : c.stop + 2 * width]
            raised = []
            for q in split_heads(first, queries):
                scores = dot(q, keys, 1, 1)
                if block == 1:
                    scores = scores + bias
                raised.append(
                    jnp.exp(scores - jnp.max(scores, axis=1, keepdims=True)).astype(LOW)
                )
            raised = jnp.concatenate(raised, axis=1)
            raised_o[w, p] = raised
            values_a, values_b = split_heads(first, values)
            sums = dot(
                raised,
                jnp.concatenate(
                    [
                        jnp.concatenate([values_a, ones_a], axis=1),
                        jnp.concatenate([values_b, ones_b], axis=1),
                    ],
                    axis=0,
                ),
            )
            recip = 1.0 / sums[:, PAIR:]
            recip_o[span, c] = recip
            attended_o[span, c] = (sums[:, :PAIR] * recip).astype(LOW)
    middle = stream + dot(attended_o[...], w_out[...])
    middle_o[...] = middle
    n, unused = normalize(middle)
    normed2_o[...] = (n * gain[block, 1] + shift[block, 1]).astype(LOW)
    total = middle
    for c in chunks(hidden, 512):
        pre = dot(normed2_o[...], w_expand[:, c]) + b_expand[block : block + 1, c]
        below = 0.5 + 0.5 * lax.erf(pre * HALF_ROOT)
        active = (pre * below).astype(LOW)
        active_o[:, c] = active
        slope_o[:, c] = (below + pre * (BELL_PEAK * jnp.exp(-0.5 * pre * pre))).astype(LOW)
        if block == 0:
            total = total + dot(active, w_reduce[c, :])
    if block == 0:
        store_rows(out, "frames", windows, total.astype(LOW))


def output_kernel(windows, active, middle, w_reduce, *refs):
    total = middle[...] + dot(active[...], w_reduce[...])
    store_rows(refs[-1], "tubes", windows, total.astype(LOW))


def mlp_back_kernel(dims, *refs):
    block, windows, width, hidden = dims
    g, slope, middle, gain, w_expand, w_reduce = refs[:6]
    rows_o, pre_o, mid_o, bias_o, gain_o, shift_o = refs[-6:]
    grad = load_rows(g, ("frames", "tubes")[block], windows)
    rows_o[...] = grad

    @pl.when(pl.program_id(0) == 0)
    def _():
        bias_o[...] = jnp.zeros_like(bias_o)
        gain_o[...] = jnp.zeros_like(gain_o)
        shift_o[...] = jnp.zeros_like(shift_o)

    total = None
    for c in chunks(hidden, 512):
        pre = (dot(grad, w_reduce[c, :], 1, 1) * slope[:, c].astype(WIDE)).astype(LOW)
        pre_o[:, c] = pre
        bias_o[:, c] += jnp.sum(pre.astype(WIDE), axis=0, keepdims=True)
        part = dot(pre, w_expand[:, c], 1, 1)
        total = part if total is None else total + part
    n, scale = normalize(middle[...])
    gain_o[...] += jnp.sum(total * n, axis=0, keepdims=True)
    shift_o[...] += jnp.sum(total, axis=0, keepdims=True)
    mid_o[...] = grad.astype(WIDE) + normalize_back(n, scale, gain[block, 1], total)


def attention_back_kernel(dims, *refs):
    block, windows, length, width = dims
    mid, triple, recip, raised, attended, w_out = refs[:6]
    if block == 0:
        triple_o, grad_s = refs[-2:]
    else:
        triple_o, grad_s = refs[-5], refs[-1]
    grad_s[...] = dot(mid[...].astype(LOW), w_out[...], 1, 1).astype(LOW)
    first = lax.broadcasted_iota(jnp.int32, (length, PAIR), 1) < HEAD_DIM
    minus = jnp.full((length, PAIR), -1.0, LOW)
    root = HEAD_DIM**-0.5
    for w in range(windows):
        span = slice(w * length, (w + 1) * length)
        for p, c in enumerate(chunks(width, PAIR)):
            c_keys = slice(c.start + width, c.stop + width)
            c_values = slice(c.start + 2 * width, c.stop + 2 * width)
            grad = grad_s[span, c]
            grad_wide = grad.astype(WIDE)
            share = recip[span, c]
            inner = (grad_wide * attended[span, c].astype(WIDE)).astype(LOW)
            grad_scaled = (grad_wide * share).astype(LOW)
            queries = (triple[span, c].astype(WIDE) * (share * root)).astype(LOW)
            keys = triple[span, c_keys] * LOW(root)
            values = jnp.concatenate([triple[span, c_values], minus], axis=1)
            scores = []
            for i, (a, b) in enumerate(zip(split_heads(first, grad), split_heads(first, inner))):
                delta = dot(jnp.concatenate([a, b], axis=1), values, 1, 1)
                e = raised[w, p, :, i * length : (i + 1) * length]
                scores.append((e.astype(WIDE) * delta).astype(LOW))
            grad_q = (
                dot(
                    jnp.concatenate(scores, axis=1),
                    jnp.concatenate(split_heads(first, keys), axis=0),
                )
                * share
            )
            grad_k = dot(
                jnp.concatenate(scores, axis=0),
                jnp.concatenate(split_heads(first, queries), axis=0),
                0,
                0,
            )
            grad_v = dot(
                jnp.concatenate([raised[w, p, :, :length], raised[w, p, :, length:]], axis=0),
                jnp.concatenate(split_heads(first, grad_scaled), axis=0),
                0,
                0,
            )
            triple_o[span, c] = grad_q.astype(LOW)
            triple_o[span, c_keys] = grad_k.astype(LOW)
            triple_o[span, c_values] = grad_v.astype(LOW)
    if block == 1:
        x, gain, w_in = refs[6:9]
        stream_back(block, windows, "rows", "tubes", x, mid, triple_o, gain, w_in, *refs[-4:-1])


def stream_back(block, windows, x_layout, layout, x, mid, triple, gain, w_in, gain_o, shift_o, out):
    @pl.when(pl.program_id(0) == 0)
    def _():
        gain_o[...] = jnp.zeros_like(gain_o)
        shift_o[...] = jnp.zeros_like(shift_o)

    total = dot(triple[...], w_in[...], 1, 1)
    n, scale = normalize(load_rows(x, x_layout, windows).astype(WIDE))
    gain_o[...] += jnp.sum(total * n, axis=0, keepdims=True)
    shift_o[...] += jnp.sum(total, axis=0, keepdims=True)
    grad_x = (mid[...] + normalize_back(n, scale, gain[block, 0], total)).astype(LOW)
    store_rows(out, layout, windows, grad_x)


def finish_kernel(windows, x, mid, triple, gain, w_in, mixed, *refs):
    gain_o, shift_o, out, mixed_o = refs[-4:]
    stream_back(0, windows, "tokens", "tokens", x, mid, triple, gain, w_in, gain_o, shift_o, out)
    for w in range(windows):
        store_window(mixed_o, "tokens", w, load_window(mixed, "frames", w))


def split_rows(value, place, send, keep):
    value = value.astype(LOW)
    pairs, length = keep.shape[0], keep.shape[1]
    same = place % 2 == 0
    for p in range(pairs):
        low = value[2 * p * length : (2 * p + 1) * length]
        high = value[(2 * p + 1) * length : (2 * p + 2) * length]
        slot = (place // 2 % pairs) ^ p
        keep[slot] = jnp.where(same, low, high)
        send[slot] = jnp.where(same, high, low)


def outer_kernel(has_last, is_split, place, left, right, *refs):
    place = place[0]
    step = pl.program_id(0)
    outs = refs[-2:] if is_split else refs[-1:]

    def store(value):
        if is_split:
            split_rows(value, place, *outs)
        else:
            outs[0][...] = value.astype(LOW).reshape(outs[0].shape)

    if not has_last:
        store(dot(left[...], right[...], 0, 0))
        return
    last = pl.num_programs(0) - 1

    @pl.when(step < last)
    def _():
        store(dot(left[...], right[...], 0, 0))

    @pl.when(step == last)
    def _():
        store(dot(refs[0][...], refs[1][...].astype(LOW), 0, 0))


def whole(shape):
    return pl.BlockSpec(shape, lambda i: (0,) * len(shape), pipeline_mode=pl.Buffered(1))


def layer(shape, block):
    return pl.BlockSpec(
        (None,) + shape, lambda i: (block,) + (0,) * len(shape), pipeline_mode=pl.Buffered(1)
    )


def clip_spec(shape, first=0):
    if len(shape) == 2:
        return pl.BlockSpec(shape, lambda i: (i + first, 0))
    if len(shape) == 3:
        return pl.BlockSpec((1,) + shape, lambda i: (i + first, 0, 0, 0))
    return pl.BlockSpec(
        (shape[0], 1) + shape[1:], lambda i: (0, i + first) + (0,) * (len(shape) - 1)
    )


def all_clips(shape, clips):
    if len(shape) == 2:
        return (clips * shape[0], shape[1])
    if len(shape) == 3:
        return (clips,) + shape
    return (shape[0], clips) + shape[1:]


ANY = pl.BlockSpec(memory_space=pl.ANY)
SCALARS = pl.BlockSpec(memory_space=pltpu.SMEM)


def params():
    return pltpu.CompilerParams(vmem_limit_bytes=VMEM_BYTES)


def cost(micros):
    return pl.CostEstimate(
        flops=int(micros * 350000000), bytes_accessed=int(micros * 1050000), transcendentals=0
    )


def sizes(weights, shapes):
    width, hidden = weights[4].shape[1:]
    clips, windows, length, parts = shapes
    return clips, windows, length, parts, windows * length, width, hidden


def forward(block, counts, x, cotangent, weights, saved, first, shapes, through=None):
    gain, shift, w_in, w_out, w_expand, b_expand, w_reduce = weights
    clips, windows, length, parts, rows, width, hidden = sizes(weights, shapes)
    steps = clips // 2
    travel = (parts, windows, length // parts, width)
    raised = (windows, width // PAIR, length, 2 * length)
    kept = [
        (rows, width), (rows, 3 * width), (rows, width), raised, (rows, width),
        (rows, width), (rows, width), (rows, hidden), (rows, hidden),
        travel if block == 0 else (rows, width),
    ]
    types = [LOW, LOW, WIDE, LOW, LOW, WIDE, LOW, LOW, LOW, LOW]
    specs, outs = [], []
    for index, (shape, kind) in enumerate(zip(kept, types)):
        if index == 3:
            specs.append(pl.BlockSpec(shape, lambda i: (i + first, 0, 0, 0)))
            outs.append(jax.ShapeDtypeStruct((clips * windows,) + shape[1:], kind))
        else:
            specs.append(clip_spec(shape, first))
            outs.append(jax.ShapeDtypeStruct(all_clips(shape, clips), kind))
    if block == 0:
        specs = [clip_spec(travel)] + specs
        outs = [jax.ShapeDtypeStruct(all_clips(travel, steps), LOW)] + outs
        ins = [counts, x, cotangent]
        in_specs = [SCALARS] + [clip_spec(v.shape[1:], first) for v in ins[1:]]
    else:
        ins = [counts, x]
        in_specs = [SCALARS, clip_spec(travel)]
    alias = [] if saved is None else list(saved)
    base = 1 if block == 0 else 0
    if through is not None:
        specs = [ANY] + specs
        outs = [jax.ShapeDtypeStruct(through.shape, through.dtype)] + outs
        alias = [through] + alias
    ins += weights
    in_specs += [
        whole(gain.shape),
        whole(shift.shape),
        layer(w_in.shape[1:], block),
        layer(w_out.shape[1:], block),
        layer(w_expand.shape[1:], block),
        whole(b_expand.shape),
        layer(w_reduce.shape[1:], block),
    ]
    dims = (block, windows, length, width, hidden, len(alias), first, through is not None)
    got = pl.pallas_call(
        functools.partial(forward_kernel, dims),
        grid=(steps,),
        in_specs=in_specs + [ANY] * len(alias),
        out_specs=specs,
        out_shape=outs,
        input_output_aliases={len(ins) + i: base + i for i in range(len(alias))},
        compiler_params=params(),
        cost_estimate=cost(36 if block == 0 else 30),
        name=f"forward_{block}",
    )(*ins, *alias)
    if block == 0 or through is not None:
        return got[0], got[1:]
    return got


def output(active, middle, weights, shapes, through):
    clips, windows, length, parts, rows, width, hidden = sizes(weights, shapes)
    travel = (parts, windows, length // parts, width)
    return pl.pallas_call(
        functools.partial(output_kernel, windows),
        grid=(clips,),
        in_specs=[
            clip_spec((rows, hidden)),
            clip_spec((rows, width)),
            layer(weights[6].shape[1:], 1),
        ]
        + [ANY],
        out_specs=[ANY, clip_spec(travel)],
        out_shape=[
            jax.ShapeDtypeStruct(through.shape, through.dtype),
            jax.ShapeDtypeStruct(all_clips(travel, clips), LOW),
        ],
        input_output_aliases={3: 0},
        compiler_params=params(),
        cost_estimate=cost(14),
        name="output",
    )(active, middle, weights[6], through)


def mlp_back(block, g, slope, middle, weights, shapes, through=()):
    gain, shift, w_in, w_out, w_expand, b_expand, w_reduce = weights
    clips, windows, length, parts, rows, width, hidden = sizes(weights, shapes)
    travel = (parts, windows, length // parts, width)
    kinds = [
        ((rows, width), LOW), ((rows, hidden), LOW), ((rows, width), WIDE),
        ((1, hidden), WIDE), ((1, width), WIDE), ((1, width), WIDE),
    ]
    return pl.pallas_call(
        functools.partial(mlp_back_kernel, (block, windows, width, hidden)),
        grid=(clips,),
        in_specs=[
            clip_spec(travel),
            clip_spec((rows, hidden)),
            clip_spec((rows, width)),
            whole(gain.shape),
            layer(w_expand.shape[1:], block),
            layer(w_reduce.shape[1:], block),
        ]
        + [ANY] * len(through),
        out_specs=[ANY] * len(through)
        + [clip_spec(s) for s, unused in kinds[:3]]
        + [pl.BlockSpec(s, lambda i: (0, 0)) for s, unused in kinds[3:]],
        out_shape=[jax.ShapeDtypeStruct(v.shape, v.dtype) for v in through]
        + [jax.ShapeDtypeStruct(all_clips(s, clips), k) for s, k in kinds[:3]]
        + [jax.ShapeDtypeStruct(s, k) for s, k in kinds[3:]],
        input_output_aliases={6 + i: i for i in range(len(through))},
        compiler_params=params(),
        cost_estimate=cost(100),
        name=f"mlp_back_{block}",
    )(g, slope, middle, gain, w_expand, w_reduce, *through)


def attention_back(block, x, mid, triple, recip, raised, attended, weights, shapes, after=()):
    gain, shift, w_in, w_out, w_expand, b_expand, w_reduce = weights
    clips, windows, length, parts, rows, width, hidden = sizes(weights, shapes)
    travel = (parts, windows, length // parts, width)
    ins = [mid, triple, recip, raised, attended, w_out]
    in_specs = [
        clip_spec((rows, width)),
        clip_spec((rows, 3 * width)),
        clip_spec((rows, width)),
        pl.BlockSpec((windows,) + raised.shape[1:], lambda i: (i, 0, 0, 0)),
        clip_spec((rows, width)),
        layer(w_out.shape[1:], block),
    ]
    out_specs = [clip_spec((rows, 3 * width))]
    out_shape = [jax.ShapeDtypeStruct((clips * rows, 3 * width), LOW)]
    if block == 1:
        ins += [x, gain, w_in]
        in_specs += [clip_spec((rows, width)), whole(gain.shape), layer(w_in.shape[1:], block)]
        out_specs += [pl.BlockSpec((1, width), lambda i: (0, 0))] * 2 + [clip_spec(travel)]
        out_shape += [jax.ShapeDtypeStruct((1, width), WIDE)] * 2
        out_shape += [jax.ShapeDtypeStruct(all_clips(travel, clips), LOW)]
    return pl.pallas_call(
        functools.partial(attention_back_kernel, (block, windows, length, width)),
        grid=(clips,),
        in_specs=in_specs + [ANY] * len(after),
        out_specs=out_specs,
        out_shape=out_shape,
        scratch_shapes=[pltpu.VMEM((rows, width), LOW)],
        compiler_params=params(),
        cost_estimate=cost(42 if block else 30),
        name=f"attention_back_{block}",
    )(*ins, *after)


def finish(x, mid, triple, mixed, weights, shapes, through, after=()):
    gain, shift, w_in, w_out, w_expand, b_expand, w_reduce = weights
    clips, windows, length, parts, rows, width, hidden = sizes(weights, shapes)
    travel = (parts, windows, length // parts, width)
    tokens = (windows, length, width)
    sums = jax.ShapeDtypeStruct((1, width), WIDE)
    sums_spec = pl.BlockSpec((1, width), lambda i: (0, 0))
    return pl.pallas_call(
        functools.partial(finish_kernel, windows),
        grid=(clips,),
        in_specs=[
            clip_spec(tokens),
            clip_spec((rows, width)),
            clip_spec((rows, 3 * width)),
            whole(gain.shape),
            layer(w_in.shape[1:], 0),
            clip_spec(travel),
            ANY,
        ]
        + [ANY] * len(after),
        out_specs=[ANY, sums_spec, sums_spec, clip_spec(tokens), clip_spec(tokens)],
        out_shape=[jax.ShapeDtypeStruct(through.shape, through.dtype), sums, sums]
        + [jax.ShapeDtypeStruct(all_clips(tokens, clips), LOW)] * 2,
        input_output_aliases={6: 0},
        compiler_params=params(),
        cost_estimate=cost(15),
        name="finish",
    )(x, mid, triple, gain, w_in, mixed, through, *after)


def outer_rows(place, active, grad, parts, is_split, into=None, after=()):
    total, width = grad.shape
    hidden = active.shape[1]
    steps = hidden // width
    group = parts // steps
    rows = hidden // parts
    if is_split:
        half = group // 2
        spec = pl.BlockSpec((half, rows, width), lambda i, place: (i ^ (place[0] // 2 // half), 0, 0))
        shape = jax.ShapeDtypeStruct((parts // 2, rows, width), LOW)
    else:
        spec = pl.BlockSpec((group, rows, width), lambda i, place: (i, 0, 0))
        shape = jax.ShapeDtypeStruct(into.shape, LOW)
    alias = [] if into is None else [into]
    arrays = 2 if is_split else 1
    return pl.pallas_call(
        functools.partial(outer_kernel, False, is_split),
        grid_spec=pltpu.PrefetchScalarGridSpec(
            num_scalar_prefetch=1,
            grid=(steps,),
            in_specs=[
                pl.BlockSpec((total, width), lambda i, place: (0, i)),
                pl.BlockSpec(
                    (total, width), lambda i, place: (0, 0), pipeline_mode=pl.Buffered(1)
                ),
            ]
            + [ANY] * (len(alias) + len(after)),
            out_specs=[spec] * arrays,
        ),
        out_shape=[shape] * arrays,
        input_output_aliases={3: 0} if alias else {},
        compiler_params=params(),
        cost_estimate=cost(14),
        name="outer_rows",
    )(place, active, grad, *alias, *after)


def outer_columns(place, left, right, last, parts, is_split, after=(), skip=0):
    total, width = left.shape
    steps = right.shape[1] // width
    blocks = steps + (1 if last else 0)
    ins = [place, left, right, *last]
    in_specs = [
        SCALARS,
        whole((total, width)),
        pl.BlockSpec((total, width), lambda i: (0, jnp.minimum(i, steps - 1))),
    ]
    in_specs += [whole((total, width))] * len(last)
    owners, arrays = (parts // 2, 2) if is_split else (parts, 1)
    spec = pl.BlockSpec((owners, width // parts, width), lambda i: (0, i + skip, 0))
    shape = jax.ShapeDtypeStruct((owners, (blocks + skip) * width // parts, width), LOW)
    return pl.pallas_call(
        functools.partial(outer_kernel, bool(last), is_split),
        grid=(blocks,),
        in_specs=in_specs + [ANY] * len(after),
        out_specs=[spec] * arrays,
        out_shape=[shape] * arrays,
        compiler_params=params(),
        cost_estimate=cost(4 * blocks),
        name="outer_columns",
    )(*ins, *after)


def add_all(values):
    total = values[0].astype(WIDE)
    for value in values[1:]:
        total = total + value.astype(WIDE)
    return total.astype(LOW)


def swap(value, axis, offset):
    return lax.ppermute(
        value, axis, [(i, i ^ offset) for i in range(lax.axis_size(axis))]
    )


def sum_frames(send, keep, reverse):
    bits = (lax.axis_size("frame") // 2).bit_length() - 1
    shape = (2,) * bits + keep.shape[1:]
    terms = [keep.reshape(shape), swap(send, "frame", 1).reshape(shape)]
    order = list(range(1, bits + 1))
    if reverse:
        order = order[::-1]
    left = list(range(bits, 0, -1))
    for bit in order:
        axis = left.index(bit)
        left.remove(bit)
        far = add_all([lax.index_in_dim(t, 1, axis, keepdims=False) for t in terms])
        yield far
        terms = [lax.index_in_dim(t, 0, axis, keepdims=False) for t in terms]
        terms.append(swap(far, "frame", 1 << bit))
    yield add_all(terms)


def last_of(steps):
    for value in steps:
        pass
    return value


def sum_clips(total, small):
    size = lax.axis_size("clip")
    rows = -(-total.shape[0] // (16 * size)) * 16
    blocks = jnp.pad(total, ((0, rows * size - total.shape[0]), (0, 0)))
    blocks = blocks.reshape(size, rows, total.shape[1])
    sent = blocks
    if small is not None:
        small = jnp.broadcast_to(small[None], (size,) + small.shape)
        sent = jnp.concatenate([blocks, small], axis=1)
    got = lax.all_to_all(sent, "clip", 0, 0)
    mine = add_all([v[:rows] for v in got])
    if small is not None:
        small = jnp.sum(got[:, rows:].astype(WIDE), axis=0)
    everything = lax.all_to_all(jnp.broadcast_to(mine[None], blocks.shape), "clip", 0, 0)
    return everything.reshape(size * rows, -1), small


def gather_kernel(block, plan, n_in, n_outs, *refs):
    sources, outs = refs[: len(plan)], refs[n_in : n_in + n_outs]
    for source, group in zip(sources, plan):
        width = source.shape[1]
        start = 0
        for out, columns in group:
            length = outs[out].shape[1]
            for c in range(columns):
                outs[out][0, :, c * width : (c + 1) * width] = source[
                    start : start + length, :
                ].astype(WIDE)
                start += length


def gather(block, sources, plan, outs, through):
    filled = not isinstance(outs[0], jax.ShapeDtypeStruct)
    extra = list(outs) if filled else []
    passed = [] if through is None else [through]
    specs = [
        pl.BlockSpec((1,) + v.shape[1:], lambda i: (block, 0, 0)) for v in outs
    ]
    ins = [*sources, *extra, *passed]
    aliases = {len(sources) + i: i for i in range(len(extra))}
    if passed:
        aliases[len(ins) - 1] = len(outs)
    return pl.pallas_call(
        functools.partial(gather_kernel, block, plan, len(ins), len(outs)),
        grid=(1,),
        in_specs=[whole(v.shape) for v in sources] + [ANY] * (len(extra) + len(passed)),
        out_specs=specs + [ANY] * len(passed),
        out_shape=[jax.ShapeDtypeStruct(v.shape, v.dtype) for v in [*outs, *passed]],
        input_output_aliases=aliases,
        compiler_params=params(),
        cost_estimate=cost(4),
        name="gather",
    )(*ins)


def exchange(value):
    return lax.all_to_all(value, "frame", 0, 0)


def local(
    tokens,
    frame_counts,
    norm_gain,
    norm_bias,
    project_in,
    project_out,
    expand_weight,
    expand_bias,
    reduce_weight,
    cotangent,
):
    clips, frames, length, width = tokens.shape
    hidden = expand_weight.shape[2]
    parts = lax.axis_size("frame")
    part = width // parts
    shapes = (clips, frames, length, parts)
    half = clips // 2
    weights = (
        norm_gain, norm_bias, project_in, project_out, expand_weight, expand_bias, reduce_weight
    )
    place = lax.axis_index("frame").astype(jnp.int32).reshape(1)

    out, saved0 = forward(0, frame_counts, tokens, cotangent, weights, None, 0, shapes)
    boundary_a = exchange(out)
    out, saved0 = forward(0, frame_counts, tokens, cotangent, weights, saved0, half, shapes)
    boundary_b = exchange(out)
    cotangent_tubes, saved1 = forward(
        1, frame_counts, boundary_a, None, weights, None, 0, shapes, saved0[9]
    )
    cotangent_tubes = exchange(cotangent_tubes)
    saved1 = forward(1, frame_counts, boundary_b, None, weights, saved1, half, shapes)

    def scatter(value):
        return lax.psum_scatter(value, "frame", scatter_dimension=0, tiled=True)[0]

    normed, triple, recip, raised, attended, middle, normed2, active, slope, stream = saved1
    rows1, pre, mid, bias1, gain12, shift12 = mlp_back(
        1, cotangent_tubes, slope, middle, weights, shapes
    )
    columns = hidden // width
    (mlp1,) = outer_columns(place, normed2, pre, [], parts, False, [], columns)
    (mlp1,) = outer_rows(place, active, rows1, parts, False, mlp1)
    mlp1_scattered = scatter(mlp1)
    grad_triple, gain11, shift11, grad_boundary = attention_back(
        1, stream, mid, triple, recip, raised, attended, weights, shapes, [mlp1]
    )
    grad_boundary = exchange(grad_boundary)
    (attention1,) = outer_columns(
        place, normed, grad_triple, [attended, mid], parts, False
    )
    attention1, mixed = output(active, middle, weights, shapes, attention1)
    attention1_scattered = scatter(attention1)

    normed, triple, recip, raised, attended, middle, normed2, active, slope = saved0[:9]
    mixed, rows0, pre, mid, bias0, gain02, shift02 = mlp_back(
        0, grad_boundary, slope, middle, weights, shapes, [mixed]
    )
    mixed = exchange(mixed)
    mlp1_sum, attention1_sum = lax.psum((mlp1_scattered, attention1_scattered), "clip")
    reduce0 = outer_rows(place, active, rows0, parts, True, None, [mlp1_scattered])
    expand0 = outer_columns(place, normed2, pre, [], parts, True, [reduce0[0]])
    (grad_triple,) = attention_back(
        0, None, mid, triple, recip, raised, attended, weights, shapes, [expand0[0]]
    )
    steps_c, steps_d = sum_frames(*reduce0, False), sum_frames(*expand0, True)
    sent = [next(steps_c), next(steps_d)]
    attention0 = outer_columns(
        place, normed, grad_triple, [attended, mid], parts, True, [*sent, attention1_scattered]
    )
    send, gain01, shift01, grad_tokens, mixed = finish(
        tokens, mid, grad_triple, mixed, weights, shapes, attention0[0]
    )
    cut = send.shape[1] // 2
    steps_a = sum_frames(send[:, :cut], attention0[1][:, :cut], False)
    steps_b = sum_frames(send[:, cut:], attention0[1][:, cut:], True)

    def by_owner(*values):
        return jnp.concatenate([v.reshape(parts, -1) for v in values], axis=1)

    small = by_owner(
        gain01, gain02, shift01, shift02, bias0, gain11, gain12, shift11, shift12, bias1
    ).astype(LOW)
    count = small.shape[1]
    small = jnp.pad(small, ((0, 0), (0, SMALL_ROWS * width - count)))
    small = add_all(list(exchange(small.reshape(parts, SMALL_ROWS, width))))
    last = jnp.concatenate([last_of(steps_a), last_of(steps_b)], axis=0)
    outs = [
        (2, hidden // parts, width),
        (2, part, hidden),
        (2, part, 3 * width),
        (2, part, width),
    ]
    outs = [jax.ShapeDtypeStruct(v, WIDE) for v in outs]
    mlp_plan = ((0, 1), (1, columns))
    attention_plan = ((2, 3), (3, 1))
    mlp0_sum = jnp.concatenate([last_of(steps_c), last_of(steps_d)], axis=0)
    outs = gather(1, [mlp1_sum, attention1_sum], (mlp_plan, attention_plan), outs, mlp0_sum)
    *outs, mlp0_sum = outs
    mlp0_sum, unused = sum_clips(mlp0_sum, None)
    attention0_sum, small = sum_clips(last, small)
    small = small.reshape(-1)[:count].reshape(2, -1)
    grad_reduce, grad_expand, grad_in, grad_out = gather(
        0, [mlp0_sum, attention0_sum], (mlp_plan, attention_plan), outs, None
    )
    return (
        mixed,
        grad_tokens,
        small[:, : 2 * part].reshape(2, 2, part),
        small[:, 2 * part : 4 * part].reshape(2, 2, part),
        grad_in,
        grad_out,
        grad_expand,
        small[:, 4 * part :],
        grad_reduce,
    )


def solution(mesh):
    in_specs = (
        P("clip", "frame", None, None),
        P("clip"),
        P(),
        P(),
        P(),
        P(),
        P(),
        P(),
        P(),
        P("clip", "frame", None, None),
    )
    out_specs = (
        P("clip", "frame", None, None),
        P("clip", "frame", None, None),
        P(None, None, "frame"),
        P(None, None, "frame"),
        P(None, "frame", None),
        P(None, "frame", None),
        P(None, "frame", None),
        P(None, "frame"),
        P(None, "frame", None),
    )
    return jax.shard_map(local, mesh=mesh, in_specs=in_specs, out_specs=out_specs, check_vma=False)
```

time: 845 us -> 663 us (0.78)
  blocking collectives: 87.7 us -> 0 us
  waiting for transfers between devices: 228 us -> 144 us
  Pallas kernels: 377 us -> 401 us
  other arithmetic: 48.8 us -> 24.9 us
  between operations: 1.58 us -> 14.6 us
  starting transfers between devices: 71 us -> 58.7 us
  local copies, waits for them, and re-layouts: 21.4 us -> 10.3 us
    all_to_all x12 -> x4, waiting for transfers between devices: 165 us -> 76.2 us  [the longest x2 41.3 us: sum_clips(): lax.all_to_all(jnp.broadcast_to(mine[None], blocks.shape), 'clip', 0, 0)]
    all_to_all x2 -> x0, blocking collectives: 51.5 us -> none  [exchange(): return lax.all_to_all(value, 'frame', 0, 0)]
    all_to_all x12 -> x4, starting transfers between devices: 52 us -> 17.1 us  [the longest x2 9.36 us: sum_clips(): got = lax.all_to_all(sent, 'clip', 0, 0)]
    pallas_call x12 -> x18, Pallas kernels: 377 us -> 401 us  [the longest x4 129 us: forward(): pl.pallas_call(functools.partial(forward_kernel, dims), grid=(steps,), in...]
    unnamed x1 -> x0, blocking collectives: 23.4 us -> none
    all_to_all x4 -> x6, waiting for transfers between devices: 62 us -> 42.4 us  [exchange(): return lax.all_to_all(value, 'frame', 0, 0)]
    ppermute x6 -> x12, waiting for transfers between devices: 0.36 us -> 18.2 us  [swap(): lax.ppermute(value, axis, [(i, i ^ offset) for i in range(lax.axis_size(a...]
    reduce_sum x8 -> x1, other arithmetic: 16.5 us -> 0.02 us  [sum_clips(): small = jnp.sum(got[:, rows:].astype(WIDE), axis=0)]
  transfers between devices with their start and end apart: 22 -> 25, of which waited for: 12 -> 10; matrix products, arithmetic and copies ran while one was open for 7% -> 5% of each run, Pallas kernels for 26% -> 44%
where the time goes in v2:
time: 663 us; the launch traced here: 654 us
  Pallas kernels  401 us (60%)
  waiting for transfers between devices  144 us (22%)
  starting transfers between devices  58.7 us (9%)
  other arithmetic  24.9 us (4%)
  between operations  14.6 us (2%)
  local copies, waits for them, and re-layouts  10.3 us (2%)
    pallas_call x4, Pallas kernels, forward(): pl.pallas_call(functools.partial(forward_kernel, dims), grid=(steps,), in...  129 us
    pallas_call x2, Pallas kernels, attention_back(): pl.pallas_call(functools.partial(attention_back_kernel, (block, windows,...  77.5 us
    pallas_call x4, Pallas kernels, outer_columns(): pl.pallas_call(functools.partial(outer_kernel, bool(last), is_split), gri...  64.3 us
    pallas_call x2, Pallas kernels, mlp_back(): pl.pallas_call(functools.partial(mlp_back_kernel, (block, windows, width,...  63.5 us
    all_to_all x6, waiting for transfers between devices, exchange(): return lax.all_to_all(value, 'frame', 0, 0)  42.4 us
    all_to_all x2, waiting for transfers between devices, sum_clips(): lax.all_to_all(jnp.broadcast_to(mine[None], blocks.shape), 'clip', 0, 0)  41.3 us
    all_to_all x2, waiting for transfers between devices, sum_clips(): got = lax.all_to_all(sent, 'clip', 0, 0)  34.9 us
    pallas_call x2, Pallas kernels, outer_rows(): pl.pallas_call(functools.partial(outer_kernel, False, is_split), grid_spe...  29.5 us
  transfers between devices with their start and end apart: 25, of which 10 were waited for; matrix products, arithmetic and copies ran while one was open for 5% of the time, Pallas kernels for 44%

profile of v2, /device:TPU:0, one launch (start us, length us, event | category | flops | bytes accessed | tf_op | source)
XLA Modules:
  0.0 653.8 jit_solution(662211042893694286)
XLA Ops:
  7.2 36.4 %forward_0.2 = (bf16[8,2,2,32,768]{4,3,2,1,0:T(8,128)(2,1)}, bf16[2048,768]{1,0:T(8,128)(2,1)}, bf16[2048,2304]{1,0:T(8,128)(2,1)}, f32[2048,768]{1,0:T(8,128)},...) custom-call(s32[4]{0:T(128)} %counts.7, ...), custom_call_target="tpu_custom_call" | custom-call | flops 12600000512 | bytes 37800000 | tf_op jit(solution)/shard_map/forward_0/pallas_call | solution.py:395
  43.6 5.4 all-to-all-start
  49.1 36.5 %forward_0.3 = (bf16[8,2,2,32,768]{4,3,2,1,0:T(8,128)(2,1)}, bf16[2048,768]{1,0:T(8,128)(2,1)}, bf16[2048,2304]{1,0:T(8,128)(2,1)}, f32[2048,768]{1,0:T(8,128)},...) custom-call(s32[4]{0:T(128)} %counts.7, ...), custom_call_target="tpu_custom_call", output_to_operand_aliasing={{1}: (10, {}), {2}: (11, {}), {3}: (12, {}), {4}: (13, {}),... | custom-call | flops 12600000512 | bytes 37800000 | tf_op jit(solution)/shard_map/forward_0/pallas_call | solution.py:395
  85.6 4.7 all-to-all-start.2
  90.3 27.9 %forward_1.2 = (bf16[8,4,2,32,768]{4,3,2,1,0:T(8,128)(2,1)}, bf16[2048,768]{1,0:T(8,128)(2,1)}, bf16[2048,2304]{1,0:T(8,128)(2,1)}, f32[2048,768]{1,0:T(8,128)},...) custom-call(s32[4]{0:T(128)} %counts.7, ...), custom_call_target="tpu_custom_call", output_to_operand_aliasing={{0}: (9, {})} | custom-call | flops 10499999744 | bytes 31500000 | tf_op jit(solution)/shard_map/forward_1/pallas_call | solution.py:395
  118.2 4.5 all-to-all-start.1
  122.9 27.9 %forward_1.3 = (bf16[2048,768]{1,0:T(8,128)(2,1)}, bf16[2048,2304]{1,0:T(8,128)(2,1)}, f32[2048,768]{1,0:T(8,128)}, bf16[8,6,256,512]{3,2,1,0:T(8,128)(2,1)}, bf...) custom-call(s32[4]{0:T(128)} %counts.7, ...), custom_call_target="tpu_custom_call", output_to_operand_aliasing={{0}: (9, {}), {1}: (10, {}), {2}: (11, {}), {3}: (12, {}), ... | custom-call | flops 10499999744 | bytes 31500000 | tf_op jit(solution)/shard_map/forward_1/pallas_call | solution.py:395
  150.8 9.8 %all-to-all-done.1.refs_0_ = bf16[8,4,2,32,768]{4,3,2,1,0:T(8,128)(2,1)} async-done(((bf16[8,4,2,32,768]{4,3,2,1,0:T(8,128)(2,1)}), bf16[8,4,2,32,768]{4,3,2,1,0:T(8,128)(2,1)}, u32[]{:S(2)}, u32[]{:S(2)}) %all-to-all-start.1) | async-done | bytes 3145760 | tf_op jit(solution)/shard_map/all_to_all | solution.py:688
  160.6 31.9 %mlp_back_1.1 = (bf16[2048,768]{1,0:T(8,128)(2,1)}, bf16[2048,3072]{1,0:T(8,128)(2,1)}, f32[2048,768]{1,0:T(8,128)}, f32[1,3072]{1,0:T(1,128)}, f32[1,768]{1,0:T(1,128)}, /*index=5*/f32[1,768]{1,0:T(1,128)}) custom-call(bf16[8,4,2,32,768]{4,3,2,1,0:T(8,128)(2,1)} %all-to-all-done.1.refs_0_, bf16[2048,3072]{1,0:T(8,128)(2,1)} %get-tuple-element.115.refs_1_, ...), custom_call_target="tpu_custom_call" | custom-call | flops 35000000512 | bytes 105000000 | tf_op jit(solution)/shard_map/mlp_back_1/pallas_call | solution.py:443
  192.5 14.6 %outer_columns.4.refs_0_ = bf16[8,768,768]{2,1,0:T(8,128)(2,1)} custom-call(s32[1]{0:T(128)} %bitcast.place, bf16[2048,768]{1,0:T(8,128)(2,1)} %get-tuple-element.125.left, bf16[2048,3072]{1,0:T(8,128)(2,1)} %get-tuple-element.126.right), custom_call_target="tpu_custom_call" | custom-call | flops 5600000000 | bytes 16800000 | tf_op jit(solution)/shard_map/outer_columns/pallas_call | solution.py:583
  207.1 14.5 %outer_rows.2.refs_9_ = bf16[8,768,768]{2,1,0:T(8,128)(2,1)} custom-call(s32[1]{0:T(128)} %bitcast.place, bf16[2048,3072]{1,0:T(8,128)(2,1)} %get-tuple-element.123.left.active, bf16[2048,768]{1,0:T(8,128)(2,1)} %get-tuple-element.124.right, bf16[8,768,768]{2,1,0:T(8,128)(2,1)} %outer_columns.4.refs_0_), custom_call_target="tpu_custom_call", output_to_operand_aliasing={{}: (3, {})} | custom-call | flops 4899999744 | bytes 14700000 | tf_op jit(solution)/shard_map/outer_rows/pallas_call | solution.py:547
  221.6 46.6 %attention_back_1.1 = (bf16[2048,2304]{1,0:T(8,128)(2,1)}, f32[1,768]{1,0:T(1,128)}, f32[1,768]{1,0:T(1,128)}, bf16[8,4,2,32,768]{4,3,2,1,0:T(8,128)(2,1)}) custom-call(f32[2048,768]{1,0:T(8,128)} %get-tuple-element.117.refs_0_.refs_1_, bf16[2048,2304]{1,0:T(8,128)(2,1)} %get-tuple-element.118.refs_1_, f32[2048,768]{1,0:T(8,128)} %get-tuple-element.119.refs_2_, ...), custom_call_target="tpu_custom_call" | custom-call | flops 14700000256 | bytes 44100000 | tf_op jit(solution)/shard_map/attention_back_1/pallas_call | solution.py:489
  268.2 4.5 all-to-all-start.3
  272.7 17.7 %outer_columns.5.refs_0_ = bf16[8,384,768]{2,1,0:T(8,128)(2,1)} custom-call(s32[1]{0:T(128)} %bitcast.place, bf16[2048,768]{1,0:T(8,128)(2,1)} %get-tuple-element.130.left, bf16[2048,2304]{1,0:T(8,128)(2,1)} %get-tuple-element.131.right, bf16[2048,768]{1,0:T(8,128)(2,1)} %get-tuple-element.121.refs_4_.refs_0_, f32[2048,768]{1,0:T(8,128)} %get-tuple-element.117.refs_0_.refs_1_), custom_call_target="tpu_custom_call" | custom-call | flops 5600000000 | bytes 16800000 | tf_op jit(solution)/shard_map/outer_columns/pallas_call | solution.py:583
  290.5 15.2 %output.1 = (bf16[8,384,768]{2,1,0:T(8,128)(2,1)}, bf16[8,4,2,32,768]{4,3,2,1,0:T(8,128)(2,1)}) custom-call(bf16[2048,3072]{1,0:T(8,128)(2,1)} %get-tuple-element.123.left.active, f32[2048,768]{1,0:T(8,128)} %get-tuple-element.116.refs_2_.middle, bf16[2,3072,768]{2,1,0:T(8,128)(2,1)} %refs_5_.14, ...), custom_call_target="tpu_custom_call", output_to_operand_aliasing={{0}: (3, {})} | custom-call | flops 4899999744 | bytes 14700000 | tf_op jit(solution)/shard_map/output/pallas_call | solution.py:414
  305.7 17.5 %all-to-all-done.3.refs_0_ = bf16[8,4,2,32,768]{4,3,2,1,0:T(8,128)(2,1)} async-done(((bf16[8,4,2,32,768]{4,3,2,1,0:T(8,128)(2,1)}), bf16[8,4,2,32,768]{4,3,2,1,0:T(8,128)(2,1)}, u32[]{:S(2)}, u32[]{:S(2)}) %all-to-all-start.3) | async-done | bytes 3145760 | tf_op jit(solution)/shard_map/all_to_all | solution.py:688
  323.2 31.7 %mlp_back_0.1 = (bf16[8,4,2,32,768]{4,3,2,1,0:T(8,128)(2,1)}, bf16[2048,768]{1,0:T(8,128)(2,1)}, bf16[2048,3072]{1,0:T(8,128)(2,1)}, f32[2048,768]{1,0:T(8,128)}...) custom-call(bf16[8,4,2,32,768]{4,3,2,1,0:T(8,128)(2,1)} %all-to-all-done.3.refs_0_, ...), custom_call_target="tpu_custom_call", output_to_operand_aliasing={{0}: (6, {})} | custom-call | flops 35000000512 | bytes 105000000 | tf_op jit(solution)/shard_map/mlp_back_0/pallas_call | solution.py:443
  354.9 14.9 %outer_rows.3 = (bf16[4,384,768]{2,1,0:T(8,128)(2,1)}, bf16[4,384,768]{2,1,0:T(8,128)(2,1)}) custom-call(s32[1]{0:T(128)} %bitcast.place, bf16[2048,3072]{1,0:T(8,128)(2,1)} %get-tuple-element.140.left, bf16[2048,768]{1,0:T(8,128)(2,1)} %get-tuple-element.141.right, bf16[768,768]{1,0:T(8,128)(2,1)} %bitcast.73), custom_call_target="tpu_custom_call" | custom-call | flops 4899999744 | bytes 14700000 | tf_op jit(solution)/shard_map/outer_rows/pallas_call | solution.py:547
  369.8 14.6 %outer_columns.6 = (bf16[4,384,768]{2,1,0:T(8,128)(2,1)}, bf16[4,384,768]{2,1,0:T(8,128)(2,1)}) custom-call(s32[1]{0:T(128)} %bitcast.place, bf16[2048,768]{1,0:T(8,128)(2,1)} %get-tuple-element.138.left, bf16[2048,3072]{1,0:T(8,128)(2,1)} %get-tuple-element.139.right, bf16[4,384,768]{2,1,0:T(8,128)(2,1)} %get-tuple-element.142.refs_0_), custom_call_target="tpu_custom_call" | custom-call | flops 5600000000 | bytes 16800000 | tf_op jit(solution)/shard_map/outer_columns/pallas_call | solution.py:583
  384.9 4.4 all-to-all-start.4
  389.4 30.9 %attention_back_0.1.right.triple = bf16[2048,2304]{1,0:T(8,128)(2,1)} custom-call(f32[2048,768]{1,0:T(8,128)} %get-tuple-element.133.refs_0_.refs_1_.mid, bf16[2048,2304]{1,0:T(8,128)(2,1)} %get-tuple-element.134.refs_1_, f32[2048,768]{1,0:T(8,128)} %get-tuple-element.135.refs_2_, bf16[8,6,256,512]{3,2,1,0:T(8,128)(2,1)} %get-tuple-element.136.refs_3_, ...), custom_call_target="tpu_custom_call" | custom-call | flops 10499999744 | bytes 31500000 | tf_op jit(solution)/shard_map/attention_back_0/pallas_call | solution.py:489
  426.0 17.4 %outer_columns.7 = (bf16[4,384,768]{2,1,0:T(8,128)(2,1)}, bf16[4,384,768]{2,1,0:T(8,128)(2,1)}) custom-call(s32[1]{0:T(128)} %bitcast.place, bf16[2048,768]{1,0:T(8,128)(2,1)} %get-tuple-element.145.left, bf16[2048,2304]{1,0:T(8,128)(2,1)} %attention_back_0.1.right.triple, bf16[2048,768]{1,0:T(8,128)(2,1)} %get-tuple-element.137.refs_4_.refs_0_, ...), custom_call_target="tpu_custom_call" | custom-call | flops 5600000000 | bytes 16800000 | tf_op jit(solution)/shard_map/outer_columns/pallas_call | solution.py:583
  443.3 16.2 %finish.1 = (bf16[4,384,768]{2,1,0:T(8,128)(2,1)}, f32[1,768]{1,0:T(1,128)}, f32[1,768]{1,0:T(1,128)}, bf16[4,2,256,768]{3,2,1,0:T(8,128)(2,1)}, bf16[4,2,256,768]{3,2,1,0:T(8,128)(2,1)}) custom-call(bf16[4,2,256,768]{3,2,1,0:T(8,128)(2,1)} %x.7, f32[2048,768]{1,0:T(8,128)} %get-tuple-element.133.refs_0_.refs_1_.mid, ...), custom_call_target="tpu_custom_call", output_to_operand_aliasing={{0}: (6, {})} | custom-call | flops 5249999872 | bytes 15750000 | tf_op jit(solution)/shard_map/finish/pallas_call | solution.py:509
  481.8 15.1 %all-to-all-done.5 = bf16[8,16,768]{2,1,0:T(8,128)(2,1)} async-done(((bf16[8,16,768]{2,1,0:T(8,128)(2,1)}), bf16[8,16,768]{2,1,0:T(8,128)(2,1)}, u32[]{:S(2)}, u32[]{:S(2)}) %all-to-all-start.5) | async-done | bytes 196640 | tf_op jit(solution)/shard_map/all_to_all | solution.py:688
  501.5 5.6 collective-permute-done.6
  515.1 12.6 %collective-permute-done.7 = bf16[192,768]{1,0:T(8,128)(2,1)S(1)} collective-permute-done((bf16[192,768]{1,0:T(8,128)(2,1)S(1)}, bf16[192,768]{1,0:T(8,128)(2,1)S(1)}, u32[]{:S(2)}, u32[]{:S(2)}) %collective-permute-start.7) | collective-permute-done | bytes 294944 | tf_op jit(solution)/shard_map/ppermute | solution.py:603
  531.2 5.8 all-to-all-start.6
  541.6 6.9 %all-reduce.4.cloned.1.call-done = (bf16[768,768]{1,0:T(8,128)(2,1)}, bf16[384,768]{1,0:T(8,128)(2,1)}) async-done(((bf16[768,768]{1,0:T(8,128)(2,1)}, bf16[384,768]{1,0:T(8,128)(2,1)}), (bf16[768,768]{1,0:T(8,128)(2,1)}, bf16[384,768]{1,0:T(8,128)(2,1)})) %all-reduce.4.cloned.1.call-update) | async-done | bytes 1769488 | tf_op jit(solution)/shard_map/psum | solution.py:750
  551.7 6.2 all-to-all-done.6
  561.5 28.7 %all-to-all-done.7 = bf16[4,192,768]{2,1,0:T(8,128)(2,1)S(1)} async-done(((bf16[4,192,768]{2,1,0:T(8,128)(2,1)}), bf16[4,192,768]{2,1,0:T(8,128)(2,1)S(1)}, u32[]{:S(2)}, u32[]{:S(2)}) %all-to-all-start.7) | async-done | bytes 1179680 | tf_op jit(solution)/shard_map/all_to_all | solution.py:641
  594.7 15.2 %all-to-all-done.9 = bf16[4,96,768]{2,1,0:T(8,128)(2,1)S(1)} async-done(((bf16[4,96,768]{2,1,0:T(8,128)(2,1)}), bf16[4,96,768]{2,1,0:T(8,128)(2,1)S(1)}, u32[]{:S(2)}, u32[]{:S(2)}) %all-to-all-start.9) | async-done | bytes 589856 | tf_op jit(solution)/shard_map/all_to_all | solution.py:645
  617.4 26.1 %all-to-all-done.8 = bf16[4,192,768]{2,1,0:T(8,128)(2,1)} async-done(((bf16[4,192,768]{2,1,0:T(8,128)(2,1)}), bf16[4,192,768]{2,1,0:T(8,128)(2,1)}, u32[]{:S(2)}, u32[]{:S(2)}) %all-to-all-start.8) | async-done | bytes 1179680 | tf_op jit(solution)/shard_map/all_to_all | solution.py:645
  (114 shorter events, 71.2 us)
Async XLA Ops:
  43.6 42.0 %all-to-all-start = ((bf16[8,2,2,32,768]{4,3,2,1,0:T(8,128)(2,1)}), bf16[8,2,2,32,768]{4,3,2,1,0:T(8,128)(2,1)}, u32[]{:S(2)}, u32[]{:S(2)}) async-start(bf16[8,2,2,32,768]{4,3,2,1,0:T(8,128)(2,1)} %get-tuple-element.91), calls=%async_computation | async-start | bytes 3145728 | tf_op jit(solution)/shard_map/all_to_all | solution.py:688
  85.6 32.7 %all-to-all-start.2 = ((bf16[8,2,2,32,768]{4,3,2,1,0:T(8,128)(2,1)}), bf16[8,2,2,32,768]{4,3,2,1,0:T(8,128)(2,1)}, u32[]{:S(2)}, u32[]{:S(2)}) async-start(bf16[8,2,2,32,768]{4,3,2,1,0:T(8,128)(2,1)} %get-tuple-element.104), calls=%async_computation.2 | async-start | bytes 3145728 | tf_op jit(solution)/shard_map/all_to_all | solution.py:688
  118.2 42.4 %all-to-all-start.1 = ((bf16[8,4,2,32,768]{4,3,2,1,0:T(8,128)(2,1)}), bf16[8,4,2,32,768]{4,3,2,1,0:T(8,128)(2,1)}, u32[]{:S(2)}, u32[]{:S(2)}) async-start(bf16[8,4,2,32,768]{4,3,2,1,0:T(8,128)(2,1)} %get-tuple-element.103), calls=%async_computation.1 | async-start | bytes 6291456 | tf_op jit(solution)/shard_map/all_to_all | solution.py:688
  122.7 232.1 %reduce-scatter.3.cloned.1.call-start = ((), (), s32[]{:S(2)}) async-start(), calls=%async_computation.12 | async-start | bytes 10616832 | tf_op jit(solution)/shard_map/reduce_scatter | solution.py:725
  268.2 55.0 %all-to-all-start.3 = ((bf16[8,4,2,32,768]{4,3,2,1,0:T(8,128)(2,1)}), bf16[8,4,2,32,768]{4,3,2,1,0:T(8,128)(2,1)}, u32[]{:S(2)}, u32[]{:S(2)}) async-start(bf16[8,4,2,32,768]{4,3,2,1,0:T(8,128)(2,1)} %get-tuple-element.127), calls=%async_computation.3 | async-start | bytes 6291456 | tf_op jit(solution)/shard_map/all_to_all | solution.py:688
  272.7 153.3 %reduce-scatter.5.cloned.1.call-start = ((), (), s32[]{:S(2)}) async-start(), calls=%async_computation.13 | async-start | bytes 5308416 | tf_op jit(solution)/shard_map/reduce_scatter | solution.py:725
  369.8 50.5 %collective-permute-start = (bf16[4,384,768]{2,1,0:T(8,128)(2,1)}, bf16[4,384,768]{2,1,0:T(8,128)(2,1)}, u32[]{:S(2)}, u32[]{:S(2)}) collective-permute-start(bf16[4,384,768]{2,1,0:T(8,128)(2,1)} %get-tuple-element.142.refs_0_), channel_id=1, source_target_pairs={{0,1},{1,0},{2,3},{3,2},{4,5},{5,4},{6,7},{7,6},{8,9},{9,8},{10,11... | collective-permute-start | bytes 7077896 | tf_op jit(solution)/shard_map/ppermute | solution.py:603
  384.4 38.9 %collective-permute-start.1 = (bf16[4,384,768]{2,1,0:T(8,128)(2,1)}, bf16[4,384,768]{2,1,0:T(8,128)(2,1)}, u32[]{:S(2)}, u32[]{:S(2)}) collective-permute-start(bf16[4,384,768]{2,1,0:T(8,128)(2,1)} %get-tuple-element.143.refs_6_), channel_id=1, source_target_pairs={{0,1},{1,0},{2,3},{3,2},{4,5},{5,4},{6,7},{7,6},{8,9},{9,8},{10,11... | collective-permute-start | bytes 7077896 | tf_op jit(solution)/shard_map/ppermute | solution.py:603
  384.9 58.4 %all-to-all-start.4 = ((bf16[8,4,2,32,768]{4,3,2,1,0:T(8,128)(2,1)}), bf16[8,4,2,32,768]{4,3,2,1,0:T(8,128)(2,1)}, u32[]{:S(2)}, u32[]{:S(2)}) async-start(bf16[8,4,2,32,768]{4,3,2,1,0:T(8,128)(2,1)} %get-tuple-element.144), calls=%async_computation.5 | async-start | bytes 6291456 | tf_op jit(solution)/shard_map/all_to_all | solution.py:688
  443.3 105.1 %all-reduce.4.cloned.1.call-start = ((), (), s32[]{:S(2)}) async-start(), calls=%async_computation.14 | async-start | bytes 3538944 | tf_op jit(solution)/shard_map/psum | solution.py:750
  459.6 6.3 copy-start.4
  459.6 6.3 copy-start.10
  459.6 6.3 copy-start.11
  459.6 6.5 copy-start.5
  459.6 6.6 %copy-start = (bf16[2,384,768]{2,1,0:T(8,128)(2,1)S(1)}, bf16[2,384,768]{2,1,0:T(8,128)(2,1)}, u32[]{:S(2)}) copy-start(bf16[2,384,768]{2,1,0:T(8,128)(2,1)} %fusion.refs_2_) | copy-start | bytes 3538948
  459.6 8.1 %copy-start.12 = (f32[1,768]{1,0:T(1,128)S(1)}, f32[1,768]{1,0:T(1,128)}, u32[]{:S(2)}) copy-start(f32[1,768]{1,0:T(1,128)} %get-tuple-element.154) | copy-start | bytes 9220
  459.6 8.1 %copy-start.13 = (f32[1,768]{1,0:T(1,128)S(1)}, f32[1,768]{1,0:T(1,128)}, u32[]{:S(2)}) copy-start(f32[1,768]{1,0:T(1,128)} %get-tuple-element.156) | copy-start | bytes 9220
  463.0 11.2 %collective-permute-start.5 = (bf16[4,192,768]{2,1,0:T(8,128)(2,1)}, bf16[4,192,768]{2,1,0:T(8,128)(2,1)}, u32[]{:S(2)}, u32[]{:S(2)}) collective-permute-start(bf16[4,192,768]{2,1,0:T(8,128)(2,1)} %get-tuple-element.176), channel_id=1, source_target_pairs={{0,1},{1,0},{2,3},{3,2},{4,5},{5,4},{6,7},{7,6},{8,9},{9,8},{10,11... | collective-permute-start | bytes 3538952 | tf_op jit(solution)/shard_map/ppermute | solution.py:603
  463.4 15.0 %collective-permute-start.2 = (bf16[4,192,768]{2,1,0:T(8,128)(2,1)}, bf16[4,192,768]{2,1,0:T(8,128)(2,1)}, u32[]{:S(2)}, u32[]{:S(2)}) collective-permute-start(bf16[4,192,768]{2,1,0:T(8,128)(2,1)} %get-tuple-element.175), channel_id=1, source_target_pairs={{0,1},{1,0},{2,3},{3,2},{4,5},{5,4},{6,7},{7,6},{8,9},{9,8},{10,11... | collective-permute-start | bytes 3538952 | tf_op jit(solution)/shard_map/ppermute | solution.py:603
  463.9 33.9 %collective-permute-start.10 = (bf16[2,384,768]{2,1,0:T(8,128)(2,1)S(1)}, bf16[2,384,768]{2,1,0:T(8,128)(2,1)}, u32[]{:S(2)}, u32[]{:S(2)}) collective-permute-start(bf16[2,384,768]{2,1,0:T(8,128)(2,1)S(1)} %copy-done.1), channel_id=1, source_target_pairs={{0,4},{1,5},{2,6},{3,7},{4,0},{5,1},{6,2},{7,3},{8,12},{9,13},{10,... | collective-permute-start | bytes 3538952 | tf_op jit(solution)/shard_map/ppermute | solution.py:603
  466.2 46.5 %collective-permute-start.8 = (bf16[2,384,768]{2,1,0:T(8,128)(2,1)S(1)}, bf16[2,384,768]{2,1,0:T(8,128)(2,1)}, u32[]{:S(2)}, u32[]{:S(2)}) collective-permute-start(bf16[2,384,768]{2,1,0:T(8,128)(2,1)S(1)} %copy-done), channel_id=1, source_target_pairs={{0,2},{1,3},{2,0},{3,1},{4,6},{5,7},{6,4},{7,5},{8,10},{9,11},{10,... | collective-permute-start | bytes 3538952 | tf_op jit(solution)/shard_map/ppermute | solution.py:603
  468.8 28.1 %all-to-all-start.5 = ((bf16[8,16,768]{2,1,0:T(8,128)(2,1)}), bf16[8,16,768]{2,1,0:T(8,128)(2,1)}, u32[]{:S(2)}, u32[]{:S(2)}) async-start(bf16[8,16,768]{2,1,0:T(8,128)(2,1)} %copy.49), calls=%async_computation.7 | async-start | bytes 393216 | tf_op jit(solution)/shard_map/all_to_all | solution.py:688
  476.4 30.6 %collective-permute-start.6 = (bf16[2,192,768]{2,1,0:T(8,128)(2,1)}, bf16[2,192,768]{2,1,0:T(8,128)(2,1)}, u32[]{:S(2)}, u32[]{:S(2)}) collective-permute-start(bf16[2,192,768]{2,1,0:T(8,128)(2,1)} %add_convert_fusion.3), channel_id=1, source_target_pairs={{0,4},{1,5},{2,6},{3,7},{4,0},{5,1},{6,2},{7,3},{8,12},{9,13},{10,... | collective-permute-start | bytes 1769480 | tf_op jit(solution)/shard_map/ppermute | solution.py:603
  480.3 29.7 %collective-permute-start.3 = (bf16[2,192,768]{2,1,0:T(8,128)(2,1)}, bf16[2,192,768]{2,1,0:T(8,128)(2,1)}, u32[]{:S(2)}, u32[]{:S(2)}) collective-permute-start(bf16[2,192,768]{2,1,0:T(8,128)(2,1)} %fusion.5), channel_id=1, source_target_pairs={{0,2},{1,3},{2,0},{3,1},{4,6},{5,7},{6,4},{7,5},{8,10},{9,11},{10,... | collective-permute-start | bytes 1769480 | tf_op jit(solution)/shard_map/ppermute | solution.py:603
  499.5 37.6 %collective-permute-start.11 = (bf16[384,768]{1,0:T(8,128)(2,1)S(1)}, bf16[384,768]{1,0:T(8,128)(2,1)S(1)}, u32[]{:S(2)}, u32[]{:S(2)}) collective-permute-start(bf16[384,768]{1,0:T(8,128)(2,1)S(1)} %fusion.6), channel_id=1, source_target_pairs={{0,2},{1,3},{2,0},{3,1},{4,6},{5,7},{6,4},{7,5},{8,10},{9,11},{10,... | collective-permute-start | bytes 1769480 | tf_op jit(solution)/shard_map/ppermute | solution.py:603
  508.3 19.5 %collective-permute-start.7 = (bf16[192,768]{1,0:T(8,128)(2,1)S(1)}, bf16[192,768]{1,0:T(8,128)(2,1)S(1)}, u32[]{:S(2)}, u32[]{:S(2)}) collective-permute-start(bf16[192,768]{1,0:T(8,128)(2,1)S(1)} %fusion.11), channel_id=1, source_target_pairs={{0,2},{1,3},{2,0},{3,1},{4,6},{5,7},{6,4},{7,5},{8,10},{9,11},{10,... | collective-permute-start | bytes 884744 | tf_op jit(solution)/shard_map/ppermute | solution.py:603
  511.2 17.8 %collective-permute-start.4 = (bf16[192,768]{1,0:T(8,128)(2,1)S(1)}, bf16[192,768]{1,0:T(8,128)(2,1)S(1)}, u32[]{:S(2)}, u32[]{:S(2)}) collective-permute-start(bf16[192,768]{1,0:T(8,128)(2,1)S(1)} %fusion.7), channel_id=1, source_target_pairs={{0,4},{1,5},{2,6},{3,7},{4,0},{5,1},{6,2},{7,3},{8,12},{9,13},{10,... | collective-permute-start | bytes 884744 | tf_op jit(solution)/shard_map/ppermute | solution.py:603
  514.4 24.3 %collective-permute-start.9 = (bf16[384,768]{1,0:T(8,128)(2,1)S(1)}, bf16[384,768]{1,0:T(8,128)(2,1)S(1)}, u32[]{:S(2)}, u32[]{:S(2)}) collective-permute-start(bf16[384,768]{1,0:T(8,128)(2,1)S(1)} %fusion.1), channel_id=1, source_target_pairs={{0,4},{1,5},{2,6},{3,7},{4,0},{5,1},{6,2},{7,3},{8,12},{9,13},{10,... | collective-permute-start | bytes 1769480 | tf_op jit(solution)/shard_map/ppermute | solution.py:603
  531.2 26.7 %all-to-all-start.6 = ((bf16[4,112,768]{2,1,0:T(8,128)(2,1)}), bf16[4,112,768]{2,1,0:T(8,128)(2,1)S(1)}, u32[]{:S(2)}, u32[]{:S(2)}) async-start(bf16[4,112,768]{2,1,0:T(8,128)(2,1)} %pad_maximum_fusion.1), calls=%async_computation.8 | async-start | bytes 1376256 | tf_op jit(solution)/shard_map/all_to_all | solution.py:641
  557.9 32.3 %all-to-all-start.7 = ((bf16[4,192,768]{2,1,0:T(8,128)(2,1)}), bf16[4,192,768]{2,1,0:T(8,128)(2,1)S(1)}, u32[]{:S(2)}, u32[]{:S(2)}) async-start(bf16[4,192,768]{2,1,0:T(8,128)(2,1)} %bitcast.65), calls=%async_computation.9 | async-start | bytes 2359296 | tf_op jit(solution)/shard_map/all_to_all | solution.py:641
  591.1 18.9 %all-to-all-start.9 = ((bf16[4,96,768]{2,1,0:T(8,128)(2,1)}), bf16[4,96,768]{2,1,0:T(8,128)(2,1)S(1)}, u32[]{:S(2)}, u32[]{:S(2)}) async-start(bf16[4,96,768]{2,1,0:T(8,128)(2,1)} %broadcast_in_dim.29), calls=%async_computation.11 | async-start | bytes 1179648 | tf_op jit(solution)/shard_map/all_to_all | solution.py:645
  611.1 32.4 %all-to-all-start.8 = ((bf16[4,192,768]{2,1,0:T(8,128)(2,1)}), bf16[4,192,768]{2,1,0:T(8,128)(2,1)}, u32[]{:S(2)}, u32[]{:S(2)}) async-start(bf16[4,192,768]{2,1,0:T(8,128)(2,1)} %broadcast_in_dim.27), calls=%async_computation.10 | async-start | bytes 2359296 | tf_op jit(solution)/shard_map/all_to_all | solution.py:645
  (7 other events, 29.0 us)
Sparse Core Ops, SparseCore 0:
  221.8 93.4 reduce-scatter.2
  318.7 59.4 reduce-scatter.4
  466.3 82.0 all-reduce.3

commit v3 on v2

--- a/solution.py
+++ b/solution.py
@@ -83,13 +83,50 @@
     block, windows, length, width, hidden, n_alias, first_clip, passes = dims
     if block == 0:
         cotangent, refs = refs[0], refs[1:]
-    gain, shift, w_in, w_out, w_expand, b_expand, w_reduce = refs[:7]
+    gain, shift, w_in_h, w_out_h, w_expand_h, b_expand, w_reduce_h = refs[:7]
     refs = refs[7 + n_alias :]
     if passes:
         refs = refs[1:]
     if block == 0:
         out, *refs = refs
-    normed_o, triple_o, recip_o, raised_o, attended_o, middle_o, normed2_o, active_o, slope_o, extra_o = refs
+    kept, extra_o, scratch = refs[:9], refs[9], refs[10:]
+    buffers, weights, kept_sems, weight_sems = scratch[:9], scratch[9:-2], scratch[-2], scratch[-1]
+    normed_o, triple_o, recip_o, raised_o, attended_o, middle_o, normed2_o, active_o, slope_o = buffers
+    step = pl.program_id(0)
+    clip = first_clip + step
+    rows = windows * length
+
+    def place(index):
+        size = buffers[index].shape[0]
+        return pl.ds(pl.multiple_of(clip * size, size), size)
+
+    def copy_out(index, columns=slice(None)):
+        if index == 3:
+            target = kept[index].at[place(index)]
+        else:
+            target = kept[index].at[place(index), columns]
+        source = buffers[index] if index == 3 else buffers[index].at[:, columns]
+        return pltpu.make_async_copy(source, target, kept_sems.at[index])
+
+    loads = [
+        pltpu.make_async_copy(source.at[block], target, weight_sems.at[k])
+        for k, (source, target) in enumerate(
+            zip((w_in_h, w_out_h, w_expand_h, w_reduce_h), weights)
+        )
+    ]
+    w_in, w_out, w_expand = weights[:3]
+
+    @pl.when(step == 0)
+    def _():
+        for load in loads:
+            load.start()
+        loads[0].wait()
+
+    @pl.when(step > 0)
+    def _():
+        for index in range(7):
+            copy_out(index).wait()
+
     stream = load_rows(x, ("tokens", "tubes")[block], windows)
     if block == 0:
         for w in range(windows):
@@ -99,14 +136,16 @@
     stream = stream.astype(WIDE)
     n, unused = normalize(stream)
     normed_o[...] = (n * gain[block, 0] + shift[block, 0]).astype(LOW)
+    copy_out(0).start()
     for c in chunks(3 * width, width):
         triple_o[:, c] = dot(normed_o[...], w_in[:, c]).astype(LOW)
+    copy_out(1).start()
     first = lax.broadcasted_iota(jnp.int32, (length, PAIR), 1) < HEAD_DIM
     ones_a, ones_b = split_heads(first, jnp.ones((length, PAIR), LOW))
     if block == 1:
         key = lax.broadcasted_iota(jnp.int32, (1, length), 1)
-        kept = key // TUBE < counts[first_clip + pl.program_id(0)]
-        bias = jnp.where(kept, 0.0, -1e30).astype(WIDE)
+        kept_key = key // TUBE < counts[clip]
+        bias = jnp.where(kept_key, 0.0, -1e30).astype(WIDE)
     for w in range(windows):
         span = slice(w * length, (w + 1) * length)
         for p, c in enumerate(chunks(width, PAIR)):
@@ -137,10 +176,26 @@
             recip = 1.0 / sums[:, PAIR:]
             recip_o[span, c] = recip
             attended_o[span, c] = (sums[:, :PAIR] * recip).astype(LOW)
-    middle = stream + dot(attended_o[...], w_out[...])
+    for index in (2, 3, 4):
+        copy_out(index).start()
+
+    @pl.when(step == 0)
+    def _():
+        for load in loads[1:]:
+            load.wait()
+
+    @pl.when(step > 0)
+    def _():
+        for index in (7, 8):
+            copy_out(index).wait()
+
+    middle = load_rows(x, ("tokens", "tubes")[block], windows).astype(WIDE)
+    middle = middle + dot(attended_o[...], w_out[...])
     middle_o[...] = middle
+    copy_out(5).start()
     n, unused = normalize(middle)
     normed2_o[...] = (n * gain[block, 1] + shift[block, 1]).astype(LOW)
+    copy_out(6).start()
     total = middle
     for c in chunks(hidden, 512):
         pre = dot(normed2_o[...], w_expand[:, c]) + b_expand[block : block + 1, c]
@@ -148,10 +203,17 @@
         active = (pre * below).astype(LOW)
         active_o[:, c] = active
         slope_o[:, c] = (below + pre * (BELL_PEAK * jnp.exp(-0.5 * pre * pre))).astype(LOW)
+        copy_out(7, c).start()
+        copy_out(8, c).start()
         if block == 0:
-            total = total + dot(active, w_reduce[c, :])
+            total = total + dot(active, weights[3][c, :])
     if block == 0:
         store_rows(out, "frames", windows, total.astype(LOW))
+
+    @pl.when(step == pl.num_programs(0) - 1)
+    def _():
+        for index in range(9):
+            copy_out(index).wait()
 
 
 def output_kernel(windows, active, middle, w_reduce, *refs):
@@ -356,17 +418,17 @@
     kept = [
         (rows, width), (rows, 3 * width), (rows, width), raised, (rows, width),
         (rows, width), (rows, width), (rows, hidden), (rows, hidden),
-        travel if block == 0 else (rows, width),
     ]
-    types = [LOW, LOW, WIDE, LOW, LOW, WIDE, LOW, LOW, LOW, LOW]
-    specs, outs = [], []
-    for index, (shape, kind) in enumerate(zip(kept, types)):
-        if index == 3:
-            specs.append(pl.BlockSpec(shape, lambda i: (i + first, 0, 0, 0)))
-            outs.append(jax.ShapeDtypeStruct((clips * windows,) + shape[1:], kind))
-        else:
-            specs.append(clip_spec(shape, first))
-            outs.append(jax.ShapeDtypeStruct(all_clips(shape, clips), kind))
+    types = [LOW, LOW, WIDE, LOW, LOW, WIDE, LOW, LOW, LOW]
+    buffers = [pltpu.VMEM(shape, kind) for shape, kind in zip(kept, types)]
+    extra = travel if block == 0 else (rows, width)
+    specs = [ANY] * len(kept) + [clip_spec(extra, first)]
+    outs = [
+        jax.ShapeDtypeStruct((clips * shape[0],) + shape[1:], kind)
+        for shape, kind in zip(kept, types)
+    ]
+    outs.append(jax.ShapeDtypeStruct(all_clips(extra, clips), LOW))
+    loaded = [w_in, w_out, w_expand] + ([w_reduce] if block == 0 else [])
     if block == 0:
         specs = [clip_spec(travel)] + specs
         outs = [jax.ShapeDtypeStruct(all_clips(travel, steps), LOW)] + outs
@@ -385,11 +447,11 @@
     in_specs += [
         whole(gain.shape),
         whole(shift.shape),
-        layer(w_in.shape[1:], block),
-        layer(w_out.shape[1:], block),
-        layer(w_expand.shape[1:], block),
+        ANY,
+        ANY,
+        ANY,
         whole(b_expand.shape),
-        layer(w_reduce.shape[1:], block),
+        ANY,
     ]
     dims = (block, windows, length, width, hidden, len(alias), first, through is not None)
     got = pl.pallas_call(
@@ -399,6 +461,9 @@
         out_specs=specs,
         out_shape=outs,
         input_output_aliases={len(ins) + i: base + i for i in range(len(alias))},
+        scratch_shapes=buffers
+        + [pltpu.VMEM(v.shape[1:], LOW) for v in loaded]
+        + [pltpu.SemaphoreType.DMA((len(kept),)), pltpu.SemaphoreType.DMA((len(loaded),))],
         compiler_params=params(),
         cost_estimate=cost(36 if block == 0 else 30),
         name=f"forward_{block}",
@@ -566,7 +631,7 @@
     )(place, active, grad, *alias, *after)
 
 
-def outer_columns(place, left, right, last, parts, is_split, after=(), skip=0):
+def outer_columns(place, left, right, last, parts, is_split, after=(), skip=0, through=()):
     total, width = left.shape
     steps = right.shape[1] // width
     blocks = steps + (1 if last else 0)
@@ -583,13 +648,14 @@
     return pl.pallas_call(
         functools.partial(outer_kernel, bool(last), is_split),
         grid=(blocks,),
-        in_specs=in_specs + [ANY] * len(after),
-        out_specs=[spec] * arrays,
-        out_shape=[shape] * arrays,
+        in_specs=in_specs + [ANY] * (len(through) + len(after)),
+        out_specs=[ANY] * len(through) + [spec] * arrays,
+        out_shape=[jax.ShapeDtypeStruct(v.shape, v.dtype) for v in through] + [shape] * arrays,
+        input_output_aliases={len(ins) + i: i for i in range(len(through))},
         compiler_params=params(),
         cost_estimate=cost(4 * blocks),
         name="outer_columns",
-    )(*ins, *after)
+    )(*ins, *through, *after)
 
 
 def add_all(values):
@@ -629,21 +695,22 @@
     return value
 
 
-def sum_clips(total, small):
+def clip_blocks(total):
     size = lax.axis_size("clip")
     rows = -(-total.shape[0] // (16 * size)) * 16
-    blocks = jnp.pad(total, ((0, rows * size - total.shape[0]), (0, 0)))
-    blocks = blocks.reshape(size, rows, total.shape[1])
-    sent = blocks
-    if small is not None:
-        small = jnp.broadcast_to(small[None], (size,) + small.shape)
-        sent = jnp.concatenate([blocks, small], axis=1)
-    got = lax.all_to_all(sent, "clip", 0, 0)
-    mine = add_all([v[:rows] for v in got])
-    if small is not None:
-        small = jnp.sum(got[:, rows:].astype(WIDE), axis=0)
-    everything = lax.all_to_all(jnp.broadcast_to(mine[None], blocks.shape), "clip", 0, 0)
-    return everything.reshape(size * rows, -1), small
+    total = jnp.pad(total, ((0, rows * size - total.shape[0]), (0, 0)))
+    return total.reshape(size, rows, total.shape[1])
+
+
+def over_clips(*values):
+    value = values[0] if len(values) == 1 else jnp.concatenate(values, axis=1)
+    got = lax.all_to_all(value, "clip", 0, 0)
+    cuts = [sum(v.shape[1] for v in values[: i + 1]) for i in range(len(values))]
+    return [got[:, cut - v.shape[1] : cut] for cut, v in zip(cuts, values)]
+
+
+def to_all_clips(value):
+    return jnp.broadcast_to(value[None], (lax.axis_size("clip"),) + value.shape)
 
 
 def gather_kernel(block, plan, n_in, n_outs, *refs):
@@ -660,23 +727,20 @@
                 start += length
 
 
-def gather(block, sources, plan, outs, through):
+def gather(block, sources, plan, outs):
     filled = not isinstance(outs[0], jax.ShapeDtypeStruct)
     extra = list(outs) if filled else []
-    passed = [] if through is None else [through]
     specs = [
         pl.BlockSpec((1,) + v.shape[1:], lambda i: (block, 0, 0)) for v in outs
     ]
-    ins = [*sources, *extra, *passed]
+    ins = [*sources, *extra]
     aliases = {len(sources) + i: i for i in range(len(extra))}
-    if passed:
-        aliases[len(ins) - 1] = len(outs)
     return pl.pallas_call(
         functools.partial(gather_kernel, block, plan, len(ins), len(outs)),
         grid=(1,),
-        in_specs=[whole(v.shape) for v in sources] + [ANY] * (len(extra) + len(passed)),
-        out_specs=specs + [ANY] * len(passed),
-        out_shape=[jax.ShapeDtypeStruct(v.shape, v.dtype) for v in [*outs, *passed]],
+        in_specs=[whole(v.shape) for v in sources] + [ANY] * len(extra),
+        out_specs=specs,
+        out_shape=[jax.ShapeDtypeStruct(v.shape, v.dtype) for v in outs],
         input_output_aliases=aliases,
         compiler_params=params(),
         cost_estimate=cost(4),
@@ -747,23 +811,22 @@
         0, grad_boundary, slope, middle, weights, shapes, [mixed]
     )
     mixed = exchange(mixed)
-    mlp1_sum, attention1_sum = lax.psum((mlp1_scattered, attention1_scattered), "clip")
+    mlp1_sum = lax.psum(mlp1_scattered, "clip")
     reduce0 = outer_rows(place, active, rows0, parts, True, None, [mlp1_scattered])
-    expand0 = outer_columns(place, normed2, pre, [], parts, True, [reduce0[0]])
+    expand0 = outer_columns(
+        place, normed2, pre, [attended, mid], parts, True, [reduce0[0]]
+    )
     (grad_triple,) = attention_back(
         0, None, mid, triple, recip, raised, attended, weights, shapes, [expand0[0]]
     )
     steps_c, steps_d = sum_frames(*reduce0, False), sum_frames(*expand0, True)
     sent = [next(steps_c), next(steps_d)]
-    attention0 = outer_columns(
-        place, normed, grad_triple, [attended, mid], parts, True, [*sent, attention1_scattered]
-    )
-    send, gain01, shift01, grad_tokens, mixed = finish(
-        tokens, mid, grad_triple, mixed, weights, shapes, attention0[0]
-    )
-    cut = send.shape[1] // 2
-    steps_a = sum_frames(send[:, :cut], attention0[1][:, :cut], False)
-    steps_b = sum_frames(send[:, cut:], attention0[1][:, cut:], True)
+    attention1_scattered, gain01, shift01, grad_tokens, mixed = finish(
+        tokens, mid, grad_triple, mixed, weights, shapes, attention1_scattered, sent
+    )
+    backward = [list(range(lax.axis_size("clip")))[::-1]]
+    attention1_sum = lax.psum(attention1_scattered, "clip", axis_index_groups=backward)
+    sent = [next(steps_c), next(steps_d)]
 
     def by_owner(*values):
         return jnp.concatenate([v.reshape(parts, -1) for v in values], axis=1)
@@ -773,7 +836,14 @@
     ).astype(LOW)
     count = small.shape[1]
     small = jnp.pad(small, ((0, 0), (0, SMALL_ROWS * width - count)))
-    small = add_all(list(exchange(small.reshape(parts, SMALL_ROWS, width))))
+    small, send, keep = outer_columns(
+        place, normed, grad_triple, [], parts, True, [*sent, mlp1_sum], 0,
+        [small.reshape(parts, SMALL_ROWS, width)],
+    )
+    cut = send.shape[1] // 2
+    steps_a = sum_frames(send[:, :cut], keep[:, :cut], False)
+    steps_b = sum_frames(send[:, cut:], keep[:, cut:], True)
+    small = add_all(list(exchange(small)))
     last = jnp.concatenate([last_of(steps_a), last_of(steps_b)], axis=0)
     outs = [
         (2, hidden // parts, width),
@@ -782,16 +852,24 @@
         (2, part, width),
     ]
     outs = [jax.ShapeDtypeStruct(v, WIDE) for v in outs]
-    mlp_plan = ((0, 1), (1, columns))
-    attention_plan = ((2, 3), (3, 1))
     mlp0_sum = jnp.concatenate([last_of(steps_c), last_of(steps_d)], axis=0)
-    outs = gather(1, [mlp1_sum, attention1_sum], (mlp_plan, attention_plan), outs, mlp0_sum)
-    *outs, mlp0_sum = outs
-    mlp0_sum, unused = sum_clips(mlp0_sum, None)
-    attention0_sum, small = sum_clips(last, small)
-    small = small.reshape(-1)[:count].reshape(2, -1)
+    (mlp0_sum,) = over_clips(clip_blocks(mlp0_sum))
+    mlp0_sum = to_all_clips(add_all(list(mlp0_sum)))
+    mlp0_sum, in0_sum, small = over_clips(mlp0_sum, clip_blocks(last), to_all_clips(small))
+    in0_sum = to_all_clips(add_all(list(in0_sum)))
+    (in0_sum,) = over_clips(in0_sum)
+    small = jnp.sum(small.astype(WIDE), axis=0).reshape(-1)[:count].reshape(2, -1)
+    outs = gather(
+        1,
+        [mlp1_sum, attention1_sum],
+        (((0, 1), (1, columns)), ((2, 3), (3, 1))),
+        outs,
+    )
     grad_reduce, grad_expand, grad_in, grad_out = gather(
-        0, [mlp0_sum, attention0_sum], (mlp_plan, attention_plan), outs, None
+        0,
+        [mlp0_sum.reshape(-1, width), in0_sum.reshape(-1, width)],
+        (((0, 1), (1, columns), (3, 1)), ((2, 3),)),
+        outs,
     )
     return (
         mixed,

time: 663 us -> 624 us (0.941)
  waiting for transfers between devices: 144 us -> 127 us
  Pallas kernels: 401 us -> 386 us
  starting transfers between devices: 58.7 us -> 49 us
    pallas_call x4, Pallas kernels: 129 us -> 113 us  [forward(): pl.pallas_call(functools.partial(forward_kernel, dims), grid=(steps,), in...]
    all_to_all x4 -> x3, waiting for transfers between devices: 76.2 us -> 63.7 us  [over_clips(): got = lax.all_to_all(value, 'clip', 0, 0)]
    all_to_all x6, waiting for transfers between devices: 42.4 us -> 31.8 us  [exchange(): return lax.all_to_all(value, 'frame', 0, 0)]
    all_to_all x4 -> x3, starting transfers between devices: 17.1 us -> 13.2 us  [over_clips(): got = lax.all_to_all(value, 'clip', 0, 0)]
  transfers between devices with their start and end apart: 25 -> 25, of which waited for: 10 -> 12; matrix products, arithmetic and copies ran while one was open for 5% -> 6% of each run, Pallas kernels for 44% -> 47%
where the time goes in v3:
time: 624 us; the launch traced here: 614 us
  Pallas kernels  386 us (62%)
  waiting for transfers between devices  127 us (20%)
  starting transfers between devices  49 us (8%)
  other arithmetic  25.8 us (4%)
  between operations  14.6 us (2%)
  local copies, waits for them, and re-layouts  11.9 us (2%)
    pallas_call x4, Pallas kernels, forward(): pl.pallas_call(functools.partial(forward_kernel, dims), grid=(steps,), in...  113 us
    pallas_call x2, Pallas kernels, attention_back(): pl.pallas_call(functools.partial(attention_back_kernel, (block, windows,...  77.7 us
    pallas_call x4, Pallas kernels, outer_columns(): pl.pallas_call(functools.partial(outer_kernel, bool(last), is_split), gri...  64.3 us
    all_to_all x3, waiting for transfers between devices, over_clips(): got = lax.all_to_all(value, 'clip', 0, 0)  63.7 us
    pallas_call x2, Pallas kernels, mlp_back(): pl.pallas_call(functools.partial(mlp_back_kernel, (block, windows, width,...  63.6 us
    all_to_all x6, waiting for transfers between devices, exchange(): return lax.all_to_all(value, 'frame', 0, 0)  31.8 us
    pallas_call x2, Pallas kernels, outer_rows(): pl.pallas_call(functools.partial(outer_kernel, False, is_split), grid_spe...  29.5 us
    all_to_all x6, starting transfers between devices, exchange(): return lax.all_to_all(value, 'frame', 0, 0)  27 us
  transfers between devices with their start and end apart: 25, of which 12 were waited for; matrix products, arithmetic and copies ran while one was open for 6% of the time, Pallas kernels for 47%

profile of v3, /device:TPU:0, one launch (start us, length us, event | category | flops | bytes accessed | tf_op | source)
XLA Modules:
  0.0 614.1 jit_solution(10750223448999184868)
XLA Ops:
  7.2 30.6 %forward_0.2 = (bf16[8,2,2,32,768]{4,3,2,1,0:T(8,128)(2,1)}, bf16[2048,768]{1,0:T(8,128)(2,1)}, bf16[2048,2304]{1,0:T(8,128)(2,1)}, f32[2048,768]{1,0:T(8,128)},...) custom-call(s32[4]{0:T(128)} %counts.7, ...), custom_call_target="tpu_custom_call" | custom-call | flops 12600000512 | bytes 37800000 | tf_op jit(solution)/shard_map/forward_0/pallas_call | solution.py:457
  37.8 5.5 all-to-all-start
  43.2 30.6 %forward_0.3 = (bf16[8,2,2,32,768]{4,3,2,1,0:T(8,128)(2,1)}, bf16[2048,768]{1,0:T(8,128)(2,1)}, bf16[2048,2304]{1,0:T(8,128)(2,1)}, f32[2048,768]{1,0:T(8,128)},...) custom-call(s32[4]{0:T(128)} %counts.7, ...), custom_call_target="tpu_custom_call", output_to_operand_aliasing={{1}: (10, {}), {2}: (11, {}), {3}: (12, {}), {4}: (13, {}),... | custom-call | flops 12600000512 | bytes 37800000 | tf_op jit(solution)/shard_map/forward_0/pallas_call | solution.py:457
  73.9 4.7 all-to-all-start.2
  78.6 25.9 %forward_1.2 = (bf16[8,4,2,32,768]{4,3,2,1,0:T(8,128)(2,1)}, bf16[2048,768]{1,0:T(8,128)(2,1)}, bf16[2048,2304]{1,0:T(8,128)(2,1)}, f32[2048,768]{1,0:T(8,128)},...) custom-call(s32[4]{0:T(128)} %counts.7, ...), custom_call_target="tpu_custom_call", output_to_operand_aliasing={{0}: (9, {})} | custom-call | flops 10499999744 | bytes 31500000 | tf_op jit(solution)/shard_map/forward_1/pallas_call | solution.py:457
  104.5 4.5 all-to-all-start.1
  109.2 25.8 %forward_1.3 = (bf16[2048,768]{1,0:T(8,128)(2,1)}, bf16[2048,2304]{1,0:T(8,128)(2,1)}, f32[2048,768]{1,0:T(8,128)}, bf16[8,6,256,512]{3,2,1,0:T(8,128)(2,1)}, bf...) custom-call(s32[4]{0:T(128)} %counts.7, ...), custom_call_target="tpu_custom_call", output_to_operand_aliasing={{0}: (9, {}), {1}: (10, {}), {2}: (11, {}), {3}: (12, {}), ... | custom-call | flops 10499999744 | bytes 31500000 | tf_op jit(solution)/shard_map/forward_1/pallas_call | solution.py:457
  135.0 11.9 %all-to-all-done.1.refs_0_ = bf16[8,4,2,32,768]{4,3,2,1,0:T(8,128)(2,1)} async-done(((bf16[8,4,2,32,768]{4,3,2,1,0:T(8,128)(2,1)}), bf16[8,4,2,32,768]{4,3,2,1,0:T(8,128)(2,1)}, u32[]{:S(2)}, u32[]{:S(2)}) %all-to-all-start.1) | async-done | bytes 3145760 | tf_op jit(solution)/shard_map/all_to_all | solution.py:752
  146.9 31.9 %mlp_back_1.1 = (bf16[2048,768]{1,0:T(8,128)(2,1)}, bf16[2048,3072]{1,0:T(8,128)(2,1)}, f32[2048,768]{1,0:T(8,128)}, f32[1,3072]{1,0:T(1,128)}, f32[1,768]{1,0:T(1,128)}, /*index=5*/f32[1,768]{1,0:T(1,128)}) custom-call(bf16[8,4,2,32,768]{4,3,2,1,0:T(8,128)(2,1)} %all-to-all-done.1.refs_0_, bf16[2048,3072]{1,0:T(8,128)(2,1)} %get-tuple-element.115.refs_1_, ...), custom_call_target="tpu_custom_call" | custom-call | flops 35000000512 | bytes 105000000 | tf_op jit(solution)/shard_map/mlp_back_1/pallas_call | solution.py:508
  178.8 14.6 %outer_columns.4.refs_0_ = bf16[8,768,768]{2,1,0:T(8,128)(2,1)} custom-call(s32[1]{0:T(128)} %bitcast.place, bf16[2048,768]{1,0:T(8,128)(2,1)} %get-tuple-element.125.left, bf16[2048,3072]{1,0:T(8,128)(2,1)} %get-tuple-element.126.right), custom_call_target="tpu_custom_call" | custom-call | flops 5600000000 | bytes 16800000 | tf_op jit(solution)/shard_map/outer_columns/pallas_call | solution.py:648
  193.4 14.5 %outer_rows.2.refs_9_ = bf16[8,768,768]{2,1,0:T(8,128)(2,1)} custom-call(s32[1]{0:T(128)} %bitcast.place, bf16[2048,3072]{1,0:T(8,128)(2,1)} %get-tuple-element.123.left.active, bf16[2048,768]{1,0:T(8,128)(2,1)} %get-tuple-element.124.right, bf16[8,768,768]{2,1,0:T(8,128)(2,1)} %outer_columns.4.refs_0_), custom_call_target="tpu_custom_call", output_to_operand_aliasing={{}: (3, {})} | custom-call | flops 4899999744 | bytes 14700000 | tf_op jit(solution)/shard_map/outer_rows/pallas_call | solution.py:612
  207.9 46.6 %attention_back_1.1 = (bf16[2048,2304]{1,0:T(8,128)(2,1)}, f32[1,768]{1,0:T(1,128)}, f32[1,768]{1,0:T(1,128)}, bf16[8,4,2,32,768]{4,3,2,1,0:T(8,128)(2,1)}) custom-call(f32[2048,768]{1,0:T(8,128)} %get-tuple-element.117.refs_0_.refs_1_, bf16[2048,2304]{1,0:T(8,128)(2,1)} %get-tuple-element.118.refs_1_, f32[2048,768]{1,0:T(8,128)} %get-tuple-element.119.refs_2_, ...), custom_call_target="tpu_custom_call" | custom-call | flops 14700000256 | bytes 44100000 | tf_op jit(solution)/shard_map/attention_back_1/pallas_call | solution.py:554
  254.5 4.5 all-to-all-start.3
  259.0 17.7 %outer_columns.5.refs_0_ = bf16[8,384,768]{2,1,0:T(8,128)(2,1)} custom-call(s32[1]{0:T(128)} %bitcast.place, bf16[2048,768]{1,0:T(8,128)(2,1)} %get-tuple-element.130.left, bf16[2048,2304]{1,0:T(8,128)(2,1)} %get-tuple-element.131.right, bf16[2048,768]{1,0:T(8,128)(2,1)} %get-tuple-element.121.refs_4_.refs_0_, f32[2048,768]{1,0:T(8,128)} %get-tuple-element.117.refs_0_.refs_1_), custom_call_target="tpu_custom_call" | custom-call | flops 5600000000 | bytes 16800000 | tf_op jit(solution)/shard_map/outer_columns/pallas_call | solution.py:648
  276.7 15.1 %output.1 = (bf16[8,384,768]{2,1,0:T(8,128)(2,1)}, bf16[8,4,2,32,768]{4,3,2,1,0:T(8,128)(2,1)}) custom-call(bf16[2048,3072]{1,0:T(8,128)(2,1)} %get-tuple-element.123.left.active, f32[2048,768]{1,0:T(8,128)} %get-tuple-element.116.refs_2_.middle, bf16[2,3072,768]{2,1,0:T(8,128)(2,1)} %refs_5_.14, ...), custom_call_target="tpu_custom_call", output_to_operand_aliasing={{0}: (3, {})} | custom-call | flops 4899999744 | bytes 14700000 | tf_op jit(solution)/shard_map/output/pallas_call | solution.py:479
  291.8 17.6 %all-to-all-done.3.refs_0_ = bf16[8,4,2,32,768]{4,3,2,1,0:T(8,128)(2,1)} async-done(((bf16[8,4,2,32,768]{4,3,2,1,0:T(8,128)(2,1)}), bf16[8,4,2,32,768]{4,3,2,1,0:T(8,128)(2,1)}, u32[]{:S(2)}, u32[]{:S(2)}) %all-to-all-start.3) | async-done | bytes 3145760 | tf_op jit(solution)/shard_map/all_to_all | solution.py:752
  309.5 31.7 %mlp_back_0.1 = (bf16[8,4,2,32,768]{4,3,2,1,0:T(8,128)(2,1)}, bf16[2048,768]{1,0:T(8,128)(2,1)}, bf16[2048,3072]{1,0:T(8,128)(2,1)}, f32[2048,768]{1,0:T(8,128)}...) custom-call(bf16[8,4,2,32,768]{4,3,2,1,0:T(8,128)(2,1)} %all-to-all-done.3.refs_0_, ...), custom_call_target="tpu_custom_call", output_to_operand_aliasing={{0}: (6, {})} | custom-call | flops 35000000512 | bytes 105000000 | tf_op jit(solution)/shard_map/mlp_back_0/pallas_call | solution.py:508
  341.1 14.9 %outer_rows.3 = (bf16[4,384,768]{2,1,0:T(8,128)(2,1)}, bf16[4,384,768]{2,1,0:T(8,128)(2,1)}) custom-call(s32[1]{0:T(128)} %bitcast.place, bf16[2048,3072]{1,0:T(8,128)(2,1)} %get-tuple-element.140.left, bf16[2048,768]{1,0:T(8,128)(2,1)} %get-tuple-element.141.right, bf16[768,768]{1,0:T(8,128)(2,1)} %bitcast.75), custom_call_target="tpu_custom_call" | custom-call | flops 4899999744 | bytes 14700000 | tf_op jit(solution)/shard_map/outer_rows/pallas_call | solution.py:612
  356.1 20.1 %outer_columns.6 = (bf16[4,480,768]{2,1,0:T(8,128)(2,1)}, bf16[4,480,768]{2,1,0:T(8,128)(2,1)}) custom-call(s32[1]{0:T(128)} %bitcast.place, bf16[2048,768]{1,0:T(8,128)(2,1)} %get-tuple-element.138.left, bf16[2048,3072]{1,0:T(8,128)(2,1)} %get-tuple-element.139.right, bf16[2048,768]{1,0:T(8,128)(2,1)} %get-tuple-element.137.refs_0_.refs_4_, ...), custom_call_target="tpu_custom_call" | custom-call | flops 7000000000 | bytes 21000000 | tf_op jit(solution)/shard_map/outer_columns/pallas_call | solution.py:648
  376.8 4.5 all-to-all-start.4
  392.5 31.2 %attention_back_0.1.triple.right = bf16[2048,2304]{1,0:T(8,128)(2,1)} custom-call(f32[2048,768]{1,0:T(8,128)} %get-tuple-element.133.refs_1_.refs_0_.mid, bf16[2048,2304]{1,0:T(8,128)(2,1)} %get-tuple-element.134.refs_1_, f32[2048,768]{1,0:T(8,128)} %get-tuple-element.135.refs_2_, bf16[8,6,256,512]{3,2,1,0:T(8,128)(2,1)} %get-tuple-element.136.refs_3_, ...), custom_call_target="tpu_custom_call" | custom-call | flops 10499999744 | bytes 31500000 | tf_op jit(solution)/shard_map/attention_back_0/pallas_call | solution.py:554
  423.6 16.0 %finish.1 = (bf16[384,768]{1,0:T(8,128)(2,1)}, f32[1,768]{1,0:T(1,128)}, f32[1,768]{1,0:T(1,128)}, bf16[4,2,256,768]{3,2,1,0:T(8,128)(2,1)}, bf16[4,2,256,768]{3,2,1,0:T(8,128)(2,1)}) custom-call(bf16[4,2,256,768]{3,2,1,0:T(8,128)(2,1)} %x.11, f32[2048,768]{1,0:T(8,128)} %get-tuple-element.133.refs_1_.refs_0_.mid, ...), custom_call_target="tpu_custom_call", output_to_operand_aliasing={{0}: (6, {})} | custom-call | flops 5249999872 | bytes 15750000 | tf_op jit(solution)/shard_map/finish/pallas_call | solution.py:574
  454.0 11.9 %outer_columns.7 = (bf16[8,16,768]{2,1,0:T(8,128)(2,1)}, bf16[4,288,768]{2,1,0:T(8,128)(2,1)}, bf16[4,288,768]{2,1,0:T(8,128)(2,1)}) custom-call(s32[1]{0:T(128)} %bitcast.place, bf16[2048,768]{1,0:T(8,128)(2,1)} %get-tuple-element.150.left, bf16[2048,2304]{1,0:T(8,128)(2,1)} %attention_back_0.1.triple.right, ...), custom_call_target="tpu_custom_call", output_to_operand_aliasing={{0}: (3, {})} | custom-call | flops 4200000000 | bytes 12600000 | tf_op jit(solution)/shard_map/outer_columns/pallas_call | solution.py:648
  470.4 3.4 all-to-all-start.6
  479.9 6.2 %all-to-all-start.5 = ((bf16[4,224,768]{2,1,0:T(8,128)(2,1)}), bf16[4,224,768]{2,1,0:T(8,128)(2,1)S(1)}, u32[]{:S(2)}, u32[]{:S(2)}) async-start(bf16[4,224,768]{2,1,0:T(8,128)(2,1)} %bitcast.12), calls=%async_computation.7 | async-start | bytes 2752512 | tf_op jit(solution)/shard_map/all_to_all | solution.py:707
  489.7 9.0 %collective-permute-done.10 = bf16[2,144,768]{2,1,0:T(8,128)(2,1)S(1)} collective-permute-done((bf16[2,144,768]{2,1,0:T(8,128)(2,1)S(1)}, bf16[2,144,768]{2,1,0:T(8,128)(2,1)S(1)}, u32[]{:S(2)}, u32[]{:S(2)}) %collective-permute-start.10) | collective-permute-done | bytes 442400 | tf_op jit(solution)/shard_map/ppermute | solution.py:669
  508.6 9.9 %all-to-all-done.5 = bf16[4,224,768]{2,1,0:T(8,128)(2,1)S(1)} async-done(((bf16[4,224,768]{2,1,0:T(8,128)(2,1)}), bf16[4,224,768]{2,1,0:T(8,128)(2,1)S(1)}, u32[]{:S(2)}, u32[]{:S(2)}) %all-to-all-start.5) | async-done | bytes 1376288 | tf_op jit(solution)/shard_map/all_to_all | solution.py:707
  520.2 3.6 all-to-all-start.7
  524.4 53.8 %all-to-all-done.7 = bf16[4,320,768]{2,1,0:T(8,128)(2,1)S(1)} async-done(((bf16[4,320,768]{2,1,0:T(8,128)(2,1)}), bf16[4,320,768]{2,1,0:T(8,128)(2,1)S(1)}, u32[]{:S(2)}, u32[]{:S(2)}) %all-to-all-start.7) | async-done | bytes 1966112 | tf_op jit(solution)/shard_map/all_to_all | solution.py:707
  580.4 3.5 all-to-all-start.8
  583.8 10.5 %all-reduce.8.cloned.1.call-done.refs_1_ = bf16[384,768]{1,0:T(8,128)(2,1)} async-done(((bf16[384,768]{1,0:T(8,128)(2,1)}), bf16[384,768]{1,0:T(8,128)(2,1)}) %all-reduce.8.cloned.1.call-update) | async-done | bytes 589840 | tf_op jit(solution)/shard_map/psum | solution.py:828
  603.8 3.3 gather.3
  (112 shorter events, 64.3 us)
Async XLA Ops:
  37.8 36.1 %all-to-all-start = ((bf16[8,2,2,32,768]{4,3,2,1,0:T(8,128)(2,1)}), bf16[8,2,2,32,768]{4,3,2,1,0:T(8,128)(2,1)}, u32[]{:S(2)}, u32[]{:S(2)}) async-start(bf16[8,2,2,32,768]{4,3,2,1,0:T(8,128)(2,1)} %get-tuple-element.91), calls=%async_computation | async-start | bytes 3145728 | tf_op jit(solution)/shard_map/all_to_all | solution.py:752
  73.9 30.6 %all-to-all-start.2 = ((bf16[8,2,2,32,768]{4,3,2,1,0:T(8,128)(2,1)}), bf16[8,2,2,32,768]{4,3,2,1,0:T(8,128)(2,1)}, u32[]{:S(2)}, u32[]{:S(2)}) async-start(bf16[8,2,2,32,768]{4,3,2,1,0:T(8,128)(2,1)} %get-tuple-element.104), calls=%async_computation.2 | async-start | bytes 3145728 | tf_op jit(solution)/shard_map/all_to_all | solution.py:752
  104.5 42.4 %all-to-all-start.1 = ((bf16[8,4,2,32,768]{4,3,2,1,0:T(8,128)(2,1)}), bf16[8,4,2,32,768]{4,3,2,1,0:T(8,128)(2,1)}, u32[]{:S(2)}, u32[]{:S(2)}) async-start(bf16[8,4,2,32,768]{4,3,2,1,0:T(8,128)(2,1)} %get-tuple-element.103), calls=%async_computation.1 | async-start | bytes 6291456 | tf_op jit(solution)/shard_map/all_to_all | solution.py:752
  109.0 232.1 %reduce-scatter.3.cloned.1.call-start = ((), (), s32[]{:S(2)}) async-start(), calls=%async_computation.11 | async-start | bytes 10616832 | tf_op jit(solution)/shard_map/reduce_scatter | solution.py:789
  254.5 55.0 %all-to-all-start.3 = ((bf16[8,4,2,32,768]{4,3,2,1,0:T(8,128)(2,1)}), bf16[8,4,2,32,768]{4,3,2,1,0:T(8,128)(2,1)}, u32[]{:S(2)}, u32[]{:S(2)}) async-start(bf16[8,4,2,32,768]{4,3,2,1,0:T(8,128)(2,1)} %get-tuple-element.127), calls=%async_computation.3 | async-start | bytes 6291456 | tf_op jit(solution)/shard_map/all_to_all | solution.py:752
  259.0 164.7 %reduce-scatter.5.cloned.1.call-start = ((), (), s32[]{:S(2)}) async-start(), calls=%async_computation.12 | async-start | bytes 5308416 | tf_op jit(solution)/shard_map/reduce_scatter | solution.py:789
  376.2 12.5 %collective-permute-start.1 = (bf16[4,480,768]{2,1,0:T(8,128)(2,1)}, bf16[4,480,768]{2,1,0:T(8,128)(2,1)}, u32[]{:S(2)}, u32[]{:S(2)}) collective-permute-start(bf16[4,480,768]{2,1,0:T(8,128)(2,1)} %get-tuple-element.143.refs_6_), channel_id=1, source_target_pairs={{0,1},{1,0},{2,3},{3,2},{4,5},{5,4},{6,7},{7,6},{8,9},{9,8},{10,11... | collective-permute-start | bytes 8847368 | tf_op jit(solution)/shard_map/ppermute | solution.py:669
  376.2 9.1 %collective-permute-start = (bf16[4,384,768]{2,1,0:T(8,128)(2,1)}, bf16[4,384,768]{2,1,0:T(8,128)(2,1)}, u32[]{:S(2)}, u32[]{:S(2)}) collective-permute-start(bf16[4,384,768]{2,1,0:T(8,128)(2,1)} %get-tuple-element.142.refs_2_), channel_id=1, source_target_pairs={{0,1},{1,0},{2,3},{3,2},{4,5},{5,4},{6,7},{7,6},{8,9},{9,8},{10,11... | collective-permute-start | bytes 7077896 | tf_op jit(solution)/shard_map/ppermute | solution.py:669
  376.7 4.7 copy-start.7
  376.7 5.0 copy-start.4
  376.7 5.1 copy-start.10
  376.7 5.1 copy-start.11
  376.8 5.3 copy-start.5
  376.8 46.9 %all-to-all-start.4 = ((bf16[8,4,2,32,768]{4,3,2,1,0:T(8,128)(2,1)}), bf16[8,4,2,32,768]{4,3,2,1,0:T(8,128)(2,1)}, u32[]{:S(2)}, u32[]{:S(2)}) async-start(bf16[8,4,2,32,768]{4,3,2,1,0:T(8,128)(2,1)} %get-tuple-element.144), calls=%async_computation.5 | async-start | bytes 6291456 | tf_op jit(solution)/shard_map/all_to_all | solution.py:752
  381.2 72.7 %all-reduce.6.cloned.1.call-start = ((), (), s32[]{:S(2)}) async-start(), calls=%async_computation.13 | async-start | bytes 2359296 | tf_op jit(solution)/shard_map/psum | solution.py:814
  382.1 6.6 %copy-start.1 = (bf16[4,480,768]{2,1,0:T(8,128)(2,1)S(1)}, bf16[4,480,768]{2,1,0:T(8,128)(2,1)}, u32[]{:S(2)}) copy-start(bf16[4,480,768]{2,1,0:T(8,128)(2,1)} %get-tuple-element.147) | copy-start | bytes 8847364
  388.2 55.3 %collective-permute-start.2 = (bf16[2,384,768]{2,1,0:T(8,128)(2,1)}, bf16[2,384,768]{2,1,0:T(8,128)(2,1)}, u32[]{:S(2)}, u32[]{:S(2)}) collective-permute-start(bf16[2,384,768]{2,1,0:T(8,128)(2,1)} %fusion.4.refs_1_), channel_id=1, source_target_pairs={{0,2},{1,3},{2,0},{3,1},{4,6},{5,7},{6,4},{7,5},{8,10},{9,11},{10,... | collective-permute-start | bytes 3538952 | tf_op jit(solution)/shard_map/ppermute | solution.py:669
  391.5 58.7 %collective-permute-start.4 = (bf16[2,480,768]{2,1,0:T(8,128)(2,1)}, bf16[2,480,768]{2,1,0:T(8,128)(2,1)}, u32[]{:S(2)}, u32[]{:S(2)}) collective-permute-start(bf16[2,480,768]{2,1,0:T(8,128)(2,1)} %add_convert_fusion.refs_2_), channel_id=1, source_target_pairs={{0,4},{1,5},{2,6},{3,7},{4,0},{5,1},{6,2},{7,3},{8,12},{9,13},{10,... | collective-permute-start | bytes 4423688 | tf_op jit(solution)/shard_map/ppermute | solution.py:669
  446.0 22.7 %collective-permute-start.3 = (bf16[384,768]{1,0:T(8,128)(2,1)}, bf16[384,768]{1,0:T(8,128)(2,1)S(1)}, u32[]{:S(2)}, u32[]{:S(2)}) collective-permute-start(bf16[384,768]{1,0:T(8,128)(2,1)} %fusion.5.refs_1_), channel_id=1, source_target_pairs={{0,4},{1,5},{2,6},{3,7},{4,0},{5,1},{6,2},{7,3},{8,12},{9,13},{10,... | collective-permute-start | bytes 1769480 | tf_op jit(solution)/shard_map/ppermute | solution.py:669
  452.9 21.4 %collective-permute-start.5 = (bf16[480,768]{1,0:T(8,128)(2,1)}, bf16[480,768]{1,0:T(8,128)(2,1)}, u32[]{:S(2)}, u32[]{:S(2)}) collective-permute-start(bf16[480,768]{1,0:T(8,128)(2,1)} %fusion.10.refs_2_), channel_id=1, source_target_pairs={{0,2},{1,3},{2,0},{3,1},{4,6},{5,7},{6,4},{7,5},{8,10},{9,11},{10,... | collective-permute-start | bytes 2211848 | tf_op jit(solution)/shard_map/ppermute | solution.py:669
  468.6 17.5 %collective-permute-start.9 = (bf16[4,144,768]{2,1,0:T(8,128)(2,1)}, bf16[4,144,768]{2,1,0:T(8,128)(2,1)}, u32[]{:S(2)}, u32[]{:S(2)}) collective-permute-start(bf16[4,144,768]{2,1,0:T(8,128)(2,1)} %get-tuple-element.174), channel_id=1, source_target_pairs={{0,1},{1,0},{2,3},{3,2},{4,5},{5,4},{6,7},{7,6},{8,9},{9,8},{10,11... | collective-permute-start | bytes 2654216 | tf_op jit(solution)/shard_map/ppermute | solution.py:669
  470.4 9.6 %all-to-all-start.6 = ((bf16[8,16,768]{2,1,0:T(8,128)(2,1)}), bf16[8,16,768]{2,1,0:T(8,128)(2,1)S(1)}, u32[]{:S(2)}, u32[]{:S(2)}) async-start(bf16[8,16,768]{2,1,0:T(8,128)(2,1)} %get-tuple-element.163), calls=%async_computation.8 | async-start | bytes 393216 | tf_op jit(solution)/shard_map/all_to_all | solution.py:752
  473.8 14.2 %collective-permute-start.6 = (bf16[4,144,768]{2,1,0:T(8,128)(2,1)}, bf16[4,144,768]{2,1,0:T(8,128)(2,1)}, u32[]{:S(2)}, u32[]{:S(2)}) collective-permute-start(bf16[4,144,768]{2,1,0:T(8,128)(2,1)} %get-tuple-element.173), channel_id=1, source_target_pairs={{0,1},{1,0},{2,3},{3,2},{4,5},{5,4},{6,7},{7,6},{8,9},{9,8},{10,11... | collective-permute-start | bytes 2654216 | tf_op jit(solution)/shard_map/ppermute | solution.py:669
  476.4 9.7 %copy-start.3 = (bf16[4,288,768]{2,1,0:T(8,128)(2,1)S(1)}, bf16[4,288,768]{2,1,0:T(8,128)(2,1)}, u32[]{:S(2)}) copy-start(bf16[4,288,768]{2,1,0:T(8,128)(2,1)} %get-tuple-element.161) | copy-start | bytes 5308420
  479.9 38.6 %all-to-all-start.5 = ((bf16[4,224,768]{2,1,0:T(8,128)(2,1)}), bf16[4,224,768]{2,1,0:T(8,128)(2,1)S(1)}, u32[]{:S(2)}, u32[]{:S(2)}) async-start(bf16[4,224,768]{2,1,0:T(8,128)(2,1)} %bitcast.12), calls=%async_computation.7 | async-start | bytes 2752512 | tf_op jit(solution)/shard_map/all_to_all | solution.py:707
  487.3 11.4 %collective-permute-start.10 = (bf16[2,144,768]{2,1,0:T(8,128)(2,1)S(1)}, bf16[2,144,768]{2,1,0:T(8,128)(2,1)S(1)}, u32[]{:S(2)}, u32[]{:S(2)}) collective-permute-start(bf16[2,144,768]{2,1,0:T(8,128)(2,1)S(1)} %add_convert_fusion.3), channel_id=1, source_target_pairs={{0,4},{1,5},{2,6},{3,7},{4,0},{5,1},{6,2},{7,3},{8,12},{9,13},{10,... | collective-permute-start | bytes 1327112 | tf_op jit(solution)/shard_map/ppermute | solution.py:669
  489.0 11.4 %collective-permute-start.7 = (bf16[2,144,768]{2,1,0:T(8,128)(2,1)S(1)}, bf16[2,144,768]{2,1,0:T(8,128)(2,1)S(1)}, u32[]{:S(2)}, u32[]{:S(2)}) collective-permute-start(bf16[2,144,768]{2,1,0:T(8,128)(2,1)S(1)} %fusion.12), channel_id=1, source_target_pairs={{0,2},{1,3},{2,0},{3,1},{4,6},{5,7},{6,4},{7,5},{8,10},{9,11},{10,... | collective-permute-start | bytes 1327112 | tf_op jit(solution)/shard_map/ppermute | solution.py:669
  499.7 6.0 collective-permute-start.11
  501.5 6.0 collective-permute-start.8
  520.2 57.9 %all-to-all-start.7 = ((bf16[4,320,768]{2,1,0:T(8,128)(2,1)}), bf16[4,320,768]{2,1,0:T(8,128)(2,1)S(1)}, u32[]{:S(2)}, u32[]{:S(2)}) async-start(bf16[4,320,768]{2,1,0:T(8,128)(2,1)} %pad_maximum_fusion), calls=%async_computation.9 | async-start | bytes 3932160 | tf_op jit(solution)/shard_map/all_to_all | solution.py:707
  523.8 70.5 %all-reduce.8.cloned.1.call-start = ((), (), s32[]{:S(2)}) async-start(), calls=%async_computation.14 | async-start | bytes 1179648 | tf_op jit(solution)/shard_map/psum | solution.py:828
  580.4 22.7 %all-to-all-start.8 = ((bf16[4,80,768]{2,1,0:T(8,128)(2,1)}), bf16[4,80,768]{2,1,0:T(8,128)(2,1)S(1)}, u32[]{:S(2)}, u32[]{:S(2)}) async-start(bf16[4,80,768]{2,1,0:T(8,128)(2,1)} %broadcast_in_dim.29), calls=%async_computation.10 | async-start | bytes 983040 | tf_op jit(solution)/shard_map/all_to_all | solution.py:707
  (5 other events, 16.0 us)
Sparse Core Ops, SparseCore 0:
  208.0 93.4 reduce-scatter.2
  305.0 59.4 reduce-scatter.4
  384.6 58.5 all-reduce.5
  526.8 67.4 all-reduce.7

commit v4 on v3

--- a/solution.py
+++ b/solution.py
@@ -387,6 +387,22 @@
     if len(shape) == 3:
         return (clips,) + shape
     return (shape[0], clips) + shape[1:]
+
+
+def window_spec(layout, shapes, width):
+    clips, windows, length, parts = shapes
+    owned = length // parts
+    if layout == "tokens":
+        return pl.BlockSpec((1, 1, length, width), lambda i: (i // windows, i % windows, 0, 0))
+    if layout == "frames":
+        return pl.BlockSpec(
+            (parts, 1, 1, owned, width), lambda i: (0, i // windows, i % windows, 0, 0)
+        )
+    if layout == "tubes":
+        return pl.BlockSpec(
+            (parts, 1, windows, TUBE, width), lambda i: (0, i // windows, 0, i % windows, 0)
+        )
+    return pl.BlockSpec((length, width), lambda i: (i, 0))
 
 
 ANY = pl.BlockSpec(memory_space=pl.ANY)
@@ -473,7 +489,7 @@
     return got
 
 
-def output(active, middle, weights, shapes, through):
+def output(active, middle, weights, shapes):
     clips, windows, length, parts, rows, width, hidden = sizes(weights, shapes)
     travel = (parts, windows, length // parts, width)
     return pl.pallas_call(
@@ -483,18 +499,13 @@
             clip_spec((rows, hidden)),
             clip_spec((rows, width)),
             layer(weights[6].shape[1:], 1),
-        ]
-        + [ANY],
-        out_specs=[ANY, clip_spec(travel)],
-        out_shape=[
-            jax.ShapeDtypeStruct(through.shape, through.dtype),
-            jax.ShapeDtypeStruct(all_clips(travel, clips), LOW),
         ],
-        input_output_aliases={3: 0},
+        out_specs=clip_spec(travel),
+        out_shape=jax.ShapeDtypeStruct(all_clips(travel, clips), LOW),
         compiler_params=params(),
         cost_estimate=cost(14),
         name="output",
-    )(active, middle, weights[6], through)
+    )(active, middle, weights[6])
 
 
 def mlp_back(block, g, slope, middle, weights, shapes, through=()):
@@ -525,7 +536,7 @@
         + [jax.ShapeDtypeStruct(s, k) for s, k in kinds[3:]],
         input_output_aliases={6 + i: i for i in range(len(through))},
         compiler_params=params(),
-        cost_estimate=cost(100),
+        cost_estimate=cost(400),
         name=f"mlp_back_{block}",
     )(g, slope, middle, gain, w_expand, w_reduce, *through)
 
@@ -534,32 +545,35 @@
     gain, shift, w_in, w_out, w_expand, b_expand, w_reduce = weights
     clips, windows, length, parts, rows, width, hidden = sizes(weights, shapes)
     travel = (parts, windows, length // parts, width)
+    flat = window_spec("rows", shapes, width)
+    wide = window_spec("rows", shapes, 3 * width)
     ins = [mid, triple, recip, raised, attended, w_out]
     in_specs = [
-        clip_spec((rows, width)),
-        clip_spec((rows, 3 * width)),
-        clip_spec((rows, width)),
-        pl.BlockSpec((windows,) + raised.shape[1:], lambda i: (i, 0, 0, 0)),
-        clip_spec((rows, width)),
+        flat,
+        wide,
+        flat,
+        pl.BlockSpec((1,) + raised.shape[1:], lambda i: (i, 0, 0, 0)),
+        flat,
         layer(w_out.shape[1:], block),
     ]
-    out_specs = [clip_spec((rows, 3 * width))]
+    out_specs = [wide]
     out_shape = [jax.ShapeDtypeStruct((clips * rows, 3 * width), LOW)]
     if block == 1:
         ins += [x, gain, w_in]
-        in_specs += [clip_spec((rows, width)), whole(gain.shape), layer(w_in.shape[1:], block)]
-        out_specs += [pl.BlockSpec((1, width), lambda i: (0, 0))] * 2 + [clip_spec(travel)]
+        in_specs += [flat, whole(gain.shape), layer(w_in.shape[1:], block)]
+        out_specs += [pl.BlockSpec((1, width), lambda i: (0, 0))] * 2
+        out_specs += [window_spec("tubes", shapes, width)]
         out_shape += [jax.ShapeDtypeStruct((1, width), WIDE)] * 2
         out_shape += [jax.ShapeDtypeStruct(all_clips(travel, clips), LOW)]
     return pl.pallas_call(
-        functools.partial(attention_back_kernel, (block, windows, length, width)),
-        grid=(clips,),
+        functools.partial(attention_back_kernel, (block, 1, length, width)),
+        grid=(clips * windows,),
         in_specs=in_specs + [ANY] * len(after),
         out_specs=out_specs,
         out_shape=out_shape,
-        scratch_shapes=[pltpu.VMEM((rows, width), LOW)],
+        scratch_shapes=[pltpu.VMEM((length, width), LOW)],
         compiler_params=params(),
-        cost_estimate=cost(42 if block else 30),
+        cost_estimate=cost(42 if block else 0.01),
         name=f"attention_back_{block}",
     )(*ins, *after)
 
@@ -581,20 +595,21 @@
             whole(gain.shape),
             layer(w_in.shape[1:], 0),
             clip_spec(travel),
-            ANY,
         ]
-        + [ANY] * len(after),
-        out_specs=[ANY, sums_spec, sums_spec, clip_spec(tokens), clip_spec(tokens)],
-        out_shape=[jax.ShapeDtypeStruct(through.shape, through.dtype), sums, sums]
+        + [ANY] * (len(through) + len(after)),
+        out_specs=[ANY] * len(through)
+        + [sums_spec, sums_spec, clip_spec(tokens), clip_spec(tokens)],
+        out_shape=[jax.ShapeDtypeStruct(v.shape, v.dtype) for v in through]
+        + [sums, sums]
         + [jax.ShapeDtypeStruct(all_clips(tokens, clips), LOW)] * 2,
-        input_output_aliases={6: 0},
+        input_output_aliases={6 + i: i for i in range(len(through))},
         compiler_params=params(),
-        cost_estimate=cost(15),
+        cost_estimate=cost(0.01),
         name="finish",
-    )(x, mid, triple, gain, w_in, mixed, through, *after)
-
-
-def outer_rows(place, active, grad, parts, is_split, into=None, after=()):
+    )(x, mid, triple, gain, w_in, mixed, *through, *after)
+
+
+def outer_rows(place, active, grad, parts, is_split, after=()):
     total, width = grad.shape
     hidden = active.shape[1]
     steps = hidden // width
@@ -606,8 +621,7 @@
         shape = jax.ShapeDtypeStruct((parts // 2, rows, width), LOW)
     else:
         spec = pl.BlockSpec((group, rows, width), lambda i, place: (i, 0, 0))
-        shape = jax.ShapeDtypeStruct(into.shape, LOW)
-    alias = [] if into is None else [into]
+        shape = jax.ShapeDtypeStruct((parts, rows, width), LOW)
     arrays = 2 if is_split else 1
     return pl.pallas_call(
         functools.partial(outer_kernel, False, is_split),
@@ -620,18 +634,19 @@
                     (total, width), lambda i, place: (0, 0), pipeline_mode=pl.Buffered(1)
                 ),
             ]
-            + [ANY] * (len(alias) + len(after)),
+            + [ANY] * len(after),
             out_specs=[spec] * arrays,
         ),
         out_shape=[shape] * arrays,
-        input_output_aliases={3: 0} if alias else {},
         compiler_params=params(),
         cost_estimate=cost(14),
         name="outer_rows",
-    )(place, active, grad, *alias, *after)
-
-
-def outer_columns(place, left, right, last, parts, is_split, after=(), skip=0, through=()):
+    )(place, active, grad, *after)
+
+
+def outer_columns(
+    place, left, right, last, parts, is_split, after=(), skip=0, through=(), room=0, into=()
+):
     total, width = left.shape
     steps = right.shape[1] // width
     blocks = steps + (1 if last else 0)
@@ -644,18 +659,21 @@
     in_specs += [whole((total, width))] * len(last)
     owners, arrays = (parts // 2, 2) if is_split else (parts, 1)
     spec = pl.BlockSpec((owners, width // parts, width), lambda i: (0, i + skip, 0))
-    shape = jax.ShapeDtypeStruct((owners, (blocks + skip) * width // parts, width), LOW)
+    shape = jax.ShapeDtypeStruct((owners, (blocks + skip + room) * width // parts, width), LOW)
+    aliases = {len(ins) + i: i for i in range(len(through))}
+    if into:
+        aliases[len(ins)] = 0
     return pl.pallas_call(
         functools.partial(outer_kernel, bool(last), is_split),
         grid=(blocks,),
-        in_specs=in_specs + [ANY] * (len(through) + len(after)),
+        in_specs=in_specs + [ANY] * (len(into) + len(through) + len(after)),
         out_specs=[ANY] * len(through) + [spec] * arrays,
         out_shape=[jax.ShapeDtypeStruct(v.shape, v.dtype) for v in through] + [shape] * arrays,
-        input_output_aliases={len(ins) + i: i for i in range(len(through))},
+        input_output_aliases=aliases,
         compiler_params=params(),
-        cost_estimate=cost(4 * blocks),
+        cost_estimate=cost(4 * blocks if blocks > 3 else 1),
         name="outer_columns",
-    )(*ins, *through, *after)
+    )(*ins, *into, *through, *after)
 
 
 def add_all(values):
@@ -683,7 +701,9 @@
         axis = left.index(bit)
         left.remove(bit)
         far = add_all([lax.index_in_dim(t, 1, axis, keepdims=False) for t in terms])
-        yield far
+        again = yield far
+        if again is not None:
+            terms[0] = again.reshape(shape)
         terms = [lax.index_in_dim(t, 0, axis, keepdims=False) for t in terms]
         terms.append(swap(far, "frame", 1 << bit))
     yield add_all(terms)
@@ -727,20 +747,21 @@
                 start += length
 
 
-def gather(block, sources, plan, outs):
+def gather(block, sources, plan, outs, through=()):
     filled = not isinstance(outs[0], jax.ShapeDtypeStruct)
     extra = list(outs) if filled else []
     specs = [
         pl.BlockSpec((1,) + v.shape[1:], lambda i: (block, 0, 0)) for v in outs
     ]
-    ins = [*sources, *extra]
+    ins = [*sources, *extra, *through]
     aliases = {len(sources) + i: i for i in range(len(extra))}
+    aliases.update({len(ins) - len(through) + i: len(outs) + i for i in range(len(through))})
     return pl.pallas_call(
         functools.partial(gather_kernel, block, plan, len(ins), len(outs)),
         grid=(1,),
-        in_specs=[whole(v.shape) for v in sources] + [ANY] * len(extra),
-        out_specs=specs,
-        out_shape=[jax.ShapeDtypeStruct(v.shape, v.dtype) for v in outs],
+        in_specs=[whole(v.shape) for v in sources] + [ANY] * (len(extra) + len(through)),
+        out_specs=specs + [ANY] * len(through),
+        out_shape=[jax.ShapeDtypeStruct(v.shape, v.dtype) for v in [*outs, *through]],
         input_output_aliases=aliases,
         compiler_params=params(),
         cost_estimate=cost(4),
@@ -789,44 +810,44 @@
         return lax.psum_scatter(value, "frame", scatter_dimension=0, tiled=True)[0]
 
     normed, triple, recip, raised, attended, middle, normed2, active, slope, stream = saved1
-    rows1, pre, mid, bias1, gain12, shift12 = mlp_back(
-        1, cotangent_tubes, slope, middle, weights, shapes
-    )
+    mixed = output(active, middle, weights, shapes)
+    mixed, rows1, pre, mid, bias1, gain12, shift12 = mlp_back(
+        1, cotangent_tubes, slope, middle, weights, shapes, [mixed]
+    )
+    mixed = exchange(mixed)
     columns = hidden // width
-    (mlp1,) = outer_columns(place, normed2, pre, [], parts, False, [], columns)
-    (mlp1,) = outer_rows(place, active, rows1, parts, False, mlp1)
-    mlp1_scattered = scatter(mlp1)
+    (reduce1,) = outer_rows(place, active, rows1, parts, False)
+    reduce1_sum = scatter(reduce1)
     grad_triple, gain11, shift11, grad_boundary = attention_back(
-        1, stream, mid, triple, recip, raised, attended, weights, shapes, [mlp1]
+        1, stream, mid, triple, recip, raised, attended, weights, shapes, [reduce1]
     )
     grad_boundary = exchange(grad_boundary)
-    (attention1,) = outer_columns(
-        place, normed, grad_triple, [attended, mid], parts, False
-    )
-    attention1, mixed = output(active, middle, weights, shapes, attention1)
-    attention1_scattered = scatter(attention1)
+    (rest1,) = outer_columns(place, normed2, pre, [], parts, False, room=columns)
+    (rest1,) = outer_columns(
+        place, normed, grad_triple, [attended, mid], parts, False, [reduce1_sum], columns,
+        into=[rest1],
+    )
 
     normed, triple, recip, raised, attended, middle, normed2, active, slope = saved0[:9]
-    mixed, rows0, pre, mid, bias0, gain02, shift02 = mlp_back(
-        0, grad_boundary, slope, middle, weights, shapes, [mixed]
-    )
-    mixed = exchange(mixed)
-    mlp1_sum = lax.psum(mlp1_scattered, "clip")
-    reduce0 = outer_rows(place, active, rows0, parts, True, None, [mlp1_scattered])
+    rows0, pre, mid, bias0, gain02, shift02 = mlp_back(
+        0, grad_boundary, slope, middle, weights, shapes, ()
+    )
+    rest1_sum = scatter(rest1)
+    reduce0 = outer_rows(place, active, rows0, parts, True)
     expand0 = outer_columns(
         place, normed2, pre, [attended, mid], parts, True, [reduce0[0]]
     )
     (grad_triple,) = attention_back(
-        0, None, mid, triple, recip, raised, attended, weights, shapes, [expand0[0]]
+        0, None, mid, triple, recip, raised, attended, weights, shapes, [expand0[0], rest1_sum]
     )
     steps_c, steps_d = sum_frames(*reduce0, False), sum_frames(*expand0, True)
     sent = [next(steps_c), next(steps_d)]
-    attention1_scattered, gain01, shift01, grad_tokens, mixed = finish(
-        tokens, mid, grad_triple, mixed, weights, shapes, attention1_scattered, sent
-    )
-    backward = [list(range(lax.axis_size("clip")))[::-1]]
-    attention1_sum = lax.psum(attention1_scattered, "clip", axis_index_groups=backward)
-    sent = [next(steps_c), next(steps_d)]
+    keep_r, keep_e, gain01, shift01, grad_tokens, mixed = finish(
+        tokens, mid, grad_triple, mixed, weights, shapes,
+        [reduce0[1], expand0[1]], sent,
+    )
+    reduce1_sum, rest1_sum = lax.psum((reduce1_sum, rest1_sum), "clip")
+    sent = [steps_c.send(keep_r), steps_d.send(keep_e)]
 
     def by_owner(*values):
         return jnp.concatenate([v.reshape(parts, -1) for v in values], axis=1)
@@ -837,14 +858,9 @@
     count = small.shape[1]
     small = jnp.pad(small, ((0, 0), (0, SMALL_ROWS * width - count)))
     small, send, keep = outer_columns(
-        place, normed, grad_triple, [], parts, True, [*sent, mlp1_sum], 0,
+        place, normed, grad_triple, [], parts, True, sent, 0,
         [small.reshape(parts, SMALL_ROWS, width)],
     )
-    cut = send.shape[1] // 2
-    steps_a = sum_frames(send[:, :cut], keep[:, :cut], False)
-    steps_b = sum_frames(send[:, cut:], keep[:, cut:], True)
-    small = add_all(list(exchange(small)))
-    last = jnp.concatenate([last_of(steps_a), last_of(steps_b)], axis=0)
     outs = [
         (2, hidden // parts, width),
         (2, part, hidden),
@@ -852,6 +868,18 @@
         (2, part, width),
     ]
     outs = [jax.ShapeDtypeStruct(v, WIDE) for v in outs]
+    *outs, keep = gather(
+        1,
+        [reduce1_sum, rest1_sum],
+        (((0, 1),), ((1, columns), (2, 3), (3, 1))),
+        outs,
+        [keep],
+    )
+    cut = send.shape[1] // 2
+    steps_a = sum_frames(send[:, :cut], keep[:, :cut], False)
+    steps_b = sum_frames(send[:, cut:], keep[:, cut:], True)
+    small = add_all(list(exchange(small)))
+    last = jnp.concatenate([last_of(steps_a), last_of(steps_b)], axis=0)
     mlp0_sum = jnp.concatenate([last_of(steps_c), last_of(steps_d)], axis=0)
     (mlp0_sum,) = over_clips(clip_blocks(mlp0_sum))
     mlp0_sum = to_all_clips(add_all(list(mlp0_sum)))
@@ -859,12 +887,6 @@
     in0_sum = to_all_clips(add_all(list(in0_sum)))
     (in0_sum,) = over_clips(in0_sum)
     small = jnp.sum(small.astype(WIDE), axis=0).reshape(-1)[:count].reshape(2, -1)
-    outs = gather(
-        1,
-        [mlp1_sum, attention1_sum],
-        (((0, 1), (1, columns)), ((2, 3), (3, 1))),
-        outs,
-    )
     grad_reduce, grad_expand, grad_in, grad_out = gather(
         0,
         [mlp0_sum.reshape(-1, width), in0_sum.reshape(-1, width)],

time: 624 us -> 602 us (0.965)
  waiting for transfers between devices: 127 us -> 66.3 us
  blocking collectives: 0 us -> 45.7 us
    all_to_all x3 -> x2, waiting for transfers between devices: 63.7 us -> 9 us  [over_clips(): got = lax.all_to_all(value, 'clip', 0, 0)]
    all_to_all x0 -> x1, blocking collectives: none -> 45.7 us  [over_clips(): got = lax.all_to_all(value, 'clip', 0, 0)]
    all_to_all x6, waiting for transfers between devices: 31.8 us -> 8.19 us  [exchange(): return lax.all_to_all(value, 'frame', 0, 0)]
    psum x2 -> x1, waiting for transfers between devices: 10.5 us -> 26.5 us  [local(): reduce1_sum, rest1_sum = lax.psum((reduce1_sum, rest1_sum), 'clip')]
    all_to_all x3 -> x2, starting transfers between devices: 13.2 us -> 7.83 us  [over_clips(): got = lax.all_to_all(value, 'clip', 0, 0)]
  transfers between devices with their start and end apart: 25 -> 23, of which waited for: 12 -> 10; matrix products, arithmetic and copies ran while one was open for 6% -> 5% of each run, Pallas kernels for 47% -> 51%
where the time goes in v4:
time: 602 us; the launch traced here: 592 us
  Pallas kernels  384 us (64%)
  waiting for transfers between devices  66.3 us (11%)
  starting transfers between devices  47.6 us (8%)
  blocking collectives  45.7 us (8%)
  other arithmetic  23.9 us (4%)
  between operations  14.5 us (2%)
  local copies, waits for them, and re-layouts  10.5 us (2%)
    pallas_call x4, Pallas kernels, forward(): pl.pallas_call(functools.partial(forward_kernel, dims), grid=(steps,), in...  113 us
    pallas_call x2, Pallas kernels, attention_back(): pl.pallas_call(functools.partial(attention_back_kernel, (block, 1, length...  72.9 us
    pallas_call x2, Pallas kernels, mlp_back(): pl.pallas_call(functools.partial(mlp_back_kernel, (block, windows, width,...  66.2 us
    pallas_call x4, Pallas kernels, outer_columns(): pl.pallas_call(functools.partial(outer_kernel, bool(last), is_split), gri...  64.2 us
    all_to_all x1, blocking collectives, over_clips(): got = lax.all_to_all(value, 'clip', 0, 0)  45.7 us
    pallas_call x2, Pallas kernels, outer_rows(): pl.pallas_call(functools.partial(outer_kernel, False, is_split), grid_spe...  29.5 us
    all_to_all x6, starting transfers between devices, exchange(): return lax.all_to_all(value, 'frame', 0, 0)  27.3 us
    psum x1, waiting for transfers between devices, local(): reduce1_sum, rest1_sum = lax.psum((reduce1_sum, rest1_sum), 'clip')  26.5 us
  transfers between devices with their start and end apart: 23, of which 10 were waited for; matrix products, arithmetic and copies ran while one was open for 5% of the time, Pallas kernels for 51%

profile of v4, /device:TPU:0, one launch (start us, length us, event | category | flops | bytes accessed | tf_op | source)
XLA Modules:
  0.0 592.3 jit_solution(4185371648931552892)
XLA Ops:
  7.2 30.6 %forward_0.2 = (bf16[8,2,2,32,768]{4,3,2,1,0:T(8,128)(2,1)}, bf16[2048,768]{1,0:T(8,128)(2,1)}, bf16[2048,2304]{1,0:T(8,128)(2,1)}, f32[2048,768]{1,0:T(8,128)},...) custom-call(s32[4]{0:T(128)} %counts.7, ...), custom_call_target="tpu_custom_call" | custom-call | flops 12600000512 | bytes 37800000 | tf_op jit(solution)/shard_map/forward_0/pallas_call | solution.py:473
  37.8 5.7 all-to-all-start
  43.5 30.6 %forward_0.3 = (bf16[8,2,2,32,768]{4,3,2,1,0:T(8,128)(2,1)}, bf16[2048,768]{1,0:T(8,128)(2,1)}, bf16[2048,2304]{1,0:T(8,128)(2,1)}, f32[2048,768]{1,0:T(8,128)},...) custom-call(s32[4]{0:T(128)} %counts.7, ...), custom_call_target="tpu_custom_call", output_to_operand_aliasing={{1}: (10, {}), {2}: (11, {}), {3}: (12, {}), {4}: (13, {}),... | custom-call | flops 12600000512 | bytes 37800000 | tf_op jit(solution)/shard_map/forward_0/pallas_call | solution.py:473
  74.1 4.5 all-to-all-start.2
  78.6 25.8 %forward_1.2 = (bf16[8,4,2,32,768]{4,3,2,1,0:T(8,128)(2,1)}, bf16[2048,768]{1,0:T(8,128)(2,1)}, bf16[2048,2304]{1,0:T(8,128)(2,1)}, f32[2048,768]{1,0:T(8,128)},...) custom-call(s32[4]{0:T(128)} %counts.7, ...), custom_call_target="tpu_custom_call", output_to_operand_aliasing={{0}: (9, {})} | custom-call | flops 10499999744 | bytes 31500000 | tf_op jit(solution)/shard_map/forward_1/pallas_call | solution.py:473
  104.4 4.5 all-to-all-start.1
  109.2 25.9 %forward_1.3 = (bf16[2048,768]{1,0:T(8,128)(2,1)}, bf16[2048,2304]{1,0:T(8,128)(2,1)}, f32[2048,768]{1,0:T(8,128)}, bf16[8,6,256,512]{3,2,1,0:T(8,128)(2,1)}, bf...) custom-call(s32[4]{0:T(128)} %counts.7, ...), custom_call_target="tpu_custom_call", output_to_operand_aliasing={{0}: (9, {}), {1}: (10, {}), {2}: (11, {}), {3}: (12, {}), ... | custom-call | flops 10499999744 | bytes 31500000 | tf_op jit(solution)/shard_map/forward_1/pallas_call | solution.py:473
  135.1 15.2 %output.1.refs_6_ = bf16[8,4,2,32,768]{4,3,2,1,0:T(8,128)(2,1)} custom-call(bf16[2048,3072]{1,0:T(8,128)(2,1)} %get-tuple-element.117.active.left, f32[2048,768]{1,0:T(8,128)} %get-tuple-element.116.middle.refs_2_, bf16[2,3072,768]{2,1,0:T(8,128)(2,1)} %refs_5_.14), custom_call_target="tpu_custom_call" | custom-call | flops 4899999744 | bytes 14700000 | tf_op jit(solution)/shard_map/output/pallas_call | solution.py:495
  150.3 32.1 %mlp_back_1.1 = (bf16[8,4,2,32,768]{4,3,2,1,0:T(8,128)(2,1)}, bf16[2048,768]{1,0:T(8,128)(2,1)}, bf16[2048,3072]{1,0:T(8,128)(2,1)}, f32[2048,768]{1,0:T(8,128)}...) custom-call(bf16[8,4,2,32,768]{4,3,2,1,0:T(8,128)(2,1)} %all-to-all-done.1.refs_0_, ...), custom_call_target="tpu_custom_call", output_to_operand_aliasing={{0}: (6, {})} | custom-call | flops 140000002048 | bytes 420000000 | tf_op jit(solution)/shard_map/mlp_back_1/pallas_call | solution.py:519
  182.4 14.5 %outer_rows.2.refs_9_ = bf16[8,384,768]{2,1,0:T(8,128)(2,1)} custom-call(s32[1]{0:T(128)} %bitcast.place, bf16[2048,3072]{1,0:T(8,128)(2,1)} %get-tuple-element.117.active.left, bf16[2048,768]{1,0:T(8,128)(2,1)} %get-tuple-element.124.right), custom_call_target="tpu_custom_call" | custom-call | flops 4899999744 | bytes 14700000 | tf_op jit(solution)/shard_map/outer_rows/pallas_call | solution.py:626
  196.9 45.1 %attention_back_1.1 = (bf16[2048,2304]{1,0:T(8,128)(2,1)}, f32[1,768]{1,0:T(1,128)}, f32[1,768]{1,0:T(1,128)}, bf16[8,4,2,32,768]{4,3,2,1,0:T(8,128)(2,1)}) custom-call(f32[2048,768]{1,0:T(8,128)} %get-tuple-element.118.refs_0_.refs_1_, bf16[2048,2304]{1,0:T(8,128)(2,1)} %get-tuple-element.119.refs_1_, f32[2048,768]{1,0:T(8,128)} %get-tuple-element.120.refs_2_, ...), custom_call_target="tpu_custom_call" | custom-call | flops 14700000256 | bytes 44100000 | tf_op jit(solution)/shard_map/attention_back_1/pallas_call | solution.py:568
  242.1 4.5 all-to-all-start.3
  246.6 14.8 %outer_columns.5.refs_2_ = bf16[8,768,768]{2,1,0:T(8,128)(2,1)} custom-call(s32[1]{0:T(128)} %bitcast.place, bf16[2048,768]{1,0:T(8,128)(2,1)} %get-tuple-element.141.left, bf16[2048,3072]{1,0:T(8,128)(2,1)} %get-tuple-element.142.right), custom_call_target="tpu_custom_call" | custom-call | flops 5600000000 | bytes 16800000 | tf_op jit(solution)/shard_map/outer_columns/pallas_call | solution.py:666
  261.4 17.3 %outer_columns.6 = bf16[8,768,768]{2,1,0:T(8,128)(2,1)} custom-call(s32[1]{0:T(128)} %bitcast.place, bf16[2048,768]{1,0:T(8,128)(2,1)} %get-tuple-element.139.left, bf16[2048,2304]{1,0:T(8,128)(2,1)} %get-tuple-element.140.right, bf16[2048,768]{1,0:T(8,128)(2,1)} %get-tuple-element.122.refs_4_.refs_0_, ...), custom_call_target="tpu_custom_call", output_to_operand_aliasing={{}: (5, {})} | custom-call | flops 5600000000 | bytes 16800000 | tf_op jit(solution)/shard_map/outer_columns/pallas_call | solution.py:666
  278.8 7.9 %all-to-all-done.3.refs_0_ = bf16[8,4,2,32,768]{4,3,2,1,0:T(8,128)(2,1)} async-done(((bf16[8,4,2,32,768]{4,3,2,1,0:T(8,128)(2,1)}), bf16[8,4,2,32,768]{4,3,2,1,0:T(8,128)(2,1)}, u32[]{:S(2)}, u32[]{:S(2)}) %all-to-all-start.3) | async-done | bytes 3145760 | tf_op jit(solution)/shard_map/all_to_all | solution.py:773
  286.7 34.1 %mlp_back_0.1 = (bf16[2048,768]{1,0:T(8,128)(2,1)}, bf16[2048,3072]{1,0:T(8,128)(2,1)}, f32[2048,768]{1,0:T(8,128)}, f32[1,3072]{1,0:T(1,128)}, f32[1,768]{1,0:T(1,128)}, /*index=5*/f32[1,768]{1,0:T(1,128)}) custom-call(bf16[8,4,2,32,768]{4,3,2,1,0:T(8,128)(2,1)} %all-to-all-done.3.refs_0_, bf16[2048,3072]{1,0:T(8,128)(2,1)} %get-tuple-element.126.refs_1_, ...), custom_call_target="tpu_custom_call" | custom-call | flops 140000002048 | bytes 420000000 | tf_op jit(solution)/shard_map/mlp_back_0/pallas_call | solution.py:519
  320.8 15.0 %outer_rows.3 = (bf16[4,384,768]{2,1,0:T(8,128)(2,1)}, bf16[4,384,768]{2,1,0:T(8,128)(2,1)}) custom-call(s32[1]{0:T(128)} %bitcast.place, bf16[2048,3072]{1,0:T(8,128)(2,1)} %get-tuple-element.135.left, bf16[2048,768]{1,0:T(8,128)(2,1)} %get-tuple-element.136.right), custom_call_target="tpu_custom_call" | custom-call | flops 4899999744 | bytes 14700000 | tf_op jit(solution)/shard_map/outer_rows/pallas_call | solution.py:626
  335.8 20.2 %outer_columns.4 = (bf16[4,480,768]{2,1,0:T(8,128)(2,1)}, bf16[4,480,768]{2,1,0:T(8,128)(2,1)}) custom-call(s32[1]{0:T(128)} %bitcast.place, bf16[2048,768]{1,0:T(8,128)(2,1)} %get-tuple-element.133.left, bf16[2048,3072]{1,0:T(8,128)(2,1)} %get-tuple-element.134.right, bf16[2048,768]{1,0:T(8,128)(2,1)} %get-tuple-element.132.refs_0_.refs_4_, ...), custom_call_target="tpu_custom_call" | custom-call | flops 7000000000 | bytes 21000000 | tf_op jit(solution)/shard_map/outer_columns/pallas_call | solution.py:666
  356.5 4.7 all-to-all-start.4
  370.9 27.7 %attention_back_0.1.triple.right = bf16[2048,2304]{1,0:T(8,128)(2,1)} custom-call(f32[2048,768]{1,0:T(8,128)} %get-tuple-element.128.refs_1_.refs_0_.mid, bf16[2048,2304]{1,0:T(8,128)(2,1)} %get-tuple-element.129.refs_1_, f32[2048,768]{1,0:T(8,128)} %get-tuple-element.130.refs_2_, bf16[8,6,256,512]{3,2,1,0:T(8,128)(2,1)} %get-tuple-element.131.refs_3_, ...), custom_call_target="tpu_custom_call" | custom-call | flops 3500000 | bytes 10500 | tf_op jit(solution)/shard_map/attention_back_0/pallas_call | solution.py:568
  399.6 16.2 %finish.1 = (bf16[4,384,768]{2,1,0:T(8,128)(2,1)}, bf16[4,480,768]{2,1,0:T(8,128)(2,1)}, f32[1,768]{1,0:T(1,128)}, f32[1,768]{1,0:T(1,128)}, bf16[4,2,256,768]{3...) custom-call(bf16[4,2,256,768]{3,2,1,0:T(8,128)(2,1)} %x.11, ...), custom_call_target="tpu_custom_call", output_to_operand_aliasing={{0}: (6, {}), {1}: (7, {})} | custom-call | flops 3500000 | bytes 10500 | tf_op jit(solution)/shard_map/finish/pallas_call | solution.py:588
  415.8 7.7 %collective-permute-done.2 = bf16[2,384,768]{2,1,0:T(8,128)(2,1)} collective-permute-done((bf16[2,384,768]{2,1,0:T(8,128)(2,1)}, bf16[2,384,768]{2,1,0:T(8,128)(2,1)}, u32[]{:S(2)}, u32[]{:S(2)}) %collective-permute-start.2) | collective-permute-done | bytes 1179680 | tf_op jit(solution)/shard_map/ppermute | solution.py:687
  434.4 11.9 %outer_columns.7 = (bf16[8,16,768]{2,1,0:T(8,128)(2,1)}, bf16[4,288,768]{2,1,0:T(8,128)(2,1)}, bf16[4,288,768]{2,1,0:T(8,128)(2,1)}) custom-call(s32[1]{0:T(128)} %bitcast.place, bf16[2048,768]{1,0:T(8,128)(2,1)} %get-tuple-element.150.left, bf16[2048,2304]{1,0:T(8,128)(2,1)} %attention_back_0.1.triple.right, ...), custom_call_target="tpu_custom_call", output_to_operand_aliasing={{0}: (3, {})} | custom-call | flops 350000000 | bytes 1050000 | tf_op jit(solution)/shard_map/outer_columns/pallas_call | solution.py:666
  446.3 3.4 all-to-all-start.6
  458.3 4.4 all-to-all-start.5
  462.7 26.5 %all-reduce.6.cloned.1.call-done = (bf16[384,768]{1,0:T(8,128)(2,1)}, bf16[768,768]{1,0:T(8,128)(2,1)}) async-done(((bf16[384,768]{1,0:T(8,128)(2,1)}, bf16[768,768]{1,0:T(8,128)(2,1)}), (bf16[384,768]{1,0:T(8,128)(2,1)}, bf16[768,768]{1,0:T(8,128)(2,1)})) %all-reduce.6.cloned.1.call-update) | async-done | bytes 1769488 | tf_op jit(solution)/shard_map/psum | solution.py:849
  489.2 3.3 gather.2
  499.0 7.5 %collective-permute-done.10 = bf16[2,144,768]{2,1,0:T(8,128)(2,1)S(1)} collective-permute-done((bf16[2,144,768]{2,1,0:T(8,128)(2,1)S(1)}, bf16[2,144,768]{2,1,0:T(8,128)(2,1)S(1)}, u32[]{:S(2)}, u32[]{:S(2)}) %collective-permute-start.10) | collective-permute-done | bytes 442400 | tf_op jit(solution)/shard_map/ppermute | solution.py:687
  518.9 45.7 %all_to_all.45 = bf16[4,320,768]{2,1,0:T(8,128)(2,1)S(1)} all-to-all(bf16[4,320,768]{2,1,0:T(8,128)(2,1)S(1)} %pad_maximum_fusion), channel_id=1, replica_groups=mesh['clip'=4,'frame'=8] {'clip'}, dimensions={0} | all-to-all | bytes 3932160 | tf_op jit(solution)/shard_map/all_to_all | solution.py:727
  565.6 3.5 all-to-all-start.8
  572.2 9.0 %all-to-all-done.8 = bf16[4,80,768]{2,1,0:T(8,128)(2,1)S(1)} async-done(((bf16[4,80,768]{2,1,0:T(8,128)(2,1)}), bf16[4,80,768]{2,1,0:T(8,128)(2,1)S(1)}, u32[]{:S(2)}, u32[]{:S(2)}) %all-to-all-start.8) | async-done | bytes 491552 | tf_op jit(solution)/shard_map/all_to_all | solution.py:727
  582.0 3.3 gather.3
  (112 shorter events, 54.5 us)
Async XLA Ops:
  37.8 36.3 %all-to-all-start = ((bf16[8,2,2,32,768]{4,3,2,1,0:T(8,128)(2,1)}), bf16[8,2,2,32,768]{4,3,2,1,0:T(8,128)(2,1)}, u32[]{:S(2)}, u32[]{:S(2)}) async-start(bf16[8,2,2,32,768]{4,3,2,1,0:T(8,128)(2,1)} %get-tuple-element.91), calls=%async_computation | async-start | bytes 3145728 | tf_op jit(solution)/shard_map/all_to_all | solution.py:773
  74.1 30.3 %all-to-all-start.2 = ((bf16[8,2,2,32,768]{4,3,2,1,0:T(8,128)(2,1)}), bf16[8,2,2,32,768]{4,3,2,1,0:T(8,128)(2,1)}, u32[]{:S(2)}, u32[]{:S(2)}) async-start(bf16[8,2,2,32,768]{4,3,2,1,0:T(8,128)(2,1)} %get-tuple-element.104), calls=%async_computation.2 | async-start | bytes 3145728 | tf_op jit(solution)/shard_map/all_to_all | solution.py:773
  104.4 45.9 %all-to-all-start.1 = ((bf16[8,4,2,32,768]{4,3,2,1,0:T(8,128)(2,1)}), bf16[8,4,2,32,768]{4,3,2,1,0:T(8,128)(2,1)}, u32[]{:S(2)}, u32[]{:S(2)}) async-start(bf16[8,4,2,32,768]{4,3,2,1,0:T(8,128)(2,1)} %get-tuple-element.103), calls=%async_computation.1 | async-start | bytes 6291456 | tf_op jit(solution)/shard_map/all_to_all | solution.py:773
  108.9 152.5 %reduce-scatter.3.cloned.1.call-start = ((), (), s32[]{:S(2)}) async-start(), calls=%async_computation.11 | async-start | bytes 5308416 | tf_op jit(solution)/shard_map/reduce_scatter | solution.py:810
  242.1 44.6 %all-to-all-start.3 = ((bf16[8,4,2,32,768]{4,3,2,1,0:T(8,128)(2,1)}), bf16[8,4,2,32,768]{4,3,2,1,0:T(8,128)(2,1)}, u32[]{:S(2)}, u32[]{:S(2)}) async-start(bf16[8,4,2,32,768]{4,3,2,1,0:T(8,128)(2,1)} %get-tuple-element.125), calls=%async_computation.3 | async-start | bytes 6291456 | tf_op jit(solution)/shard_map/all_to_all | solution.py:773
  246.5 124.3 %reduce-scatter.5.cloned.1.call-start = ((), (), s32[]{:S(2)}) async-start(), calls=%async_computation.12 | async-start | bytes 10616832 | tf_op jit(solution)/shard_map/reduce_scatter | solution.py:810
  356.0 5.7 collective-permute-start.1
  356.0 10.3 %collective-permute-start = (bf16[4,384,768]{2,1,0:T(8,128)(2,1)}, bf16[4,384,768]{2,1,0:T(8,128)(2,1)}, u32[]{:S(2)}, u32[]{:S(2)}) collective-permute-start(bf16[4,384,768]{2,1,0:T(8,128)(2,1)} %get-tuple-element.137.refs_2_), channel_id=1, source_target_pairs={{0,1},{1,0},{2,3},{3,2},{4,5},{5,4},{6,7},{7,6},{8,9},{9,8},{10,11... | collective-permute-start | bytes 7077896 | tf_op jit(solution)/shard_map/ppermute | solution.py:687
  356.5 43.1 %all-to-all-start.4 = ((bf16[8,4,2,32,768]{4,3,2,1,0:T(8,128)(2,1)}), bf16[8,4,2,32,768]{4,3,2,1,0:T(8,128)(2,1)}, u32[]{:S(2)}, u32[]{:S(2)}) async-start(bf16[8,4,2,32,768]{4,3,2,1,0:T(8,128)(2,1)} %get-tuple-element.143), calls=%async_computation.6 | async-start | bytes 6291456 | tf_op jit(solution)/shard_map/all_to_all | solution.py:773
  364.7 5.6 copy-start.11
  364.7 5.7 copy-start.8
  364.7 5.7 copy-start.9
  364.7 6.0 %copy-start.4 = (f32[1,3072]{1,0:T(1,128)S(1)}, f32[1,3072]{1,0:T(1,128)}, u32[]{:S(2)}) copy-start(f32[1,3072]{1,0:T(1,128)} %get-tuple-element.160) | copy-start | bytes 36868
  364.8 6.0 %copy-start.5 = (f32[1,3072]{1,0:T(1,128)S(1)}, f32[1,3072]{1,0:T(1,128)}, u32[]{:S(2)}) copy-start(f32[1,3072]{1,0:T(1,128)} %get-tuple-element.155) | copy-start | bytes 36868
  364.8 65.4 %collective-permute-start.4 = (bf16[2,480,768]{2,1,0:T(8,128)(2,1)}, bf16[2,480,768]{2,1,0:T(8,128)(2,1)}, u32[]{:S(2)}, u32[]{:S(2)}) collective-permute-start(bf16[2,480,768]{2,1,0:T(8,128)(2,1)} %add_convert_fusion.refs_3_), channel_id=1, source_target_pairs={{0,4},{1,5},{2,6},{3,7},{4,0},{5,1},{6,2},{7,3},{8,12},{9,13},{10,... | collective-permute-start | bytes 4423688 | tf_op jit(solution)/shard_map/ppermute | solution.py:687
  368.8 54.7 %collective-permute-start.2 = (bf16[2,384,768]{2,1,0:T(8,128)(2,1)}, bf16[2,384,768]{2,1,0:T(8,128)(2,1)}, u32[]{:S(2)}, u32[]{:S(2)}) collective-permute-start(bf16[2,384,768]{2,1,0:T(8,128)(2,1)} %fusion.4.refs_2_), channel_id=1, source_target_pairs={{0,2},{1,3},{2,0},{3,1},{4,6},{5,7},{6,4},{7,5},{8,10},{9,11},{10,... | collective-permute-start | bytes 3538952 | tf_op jit(solution)/shard_map/ppermute | solution.py:687
  398.6 90.6 %all-reduce.6.cloned.1.call-start = ((), (), s32[]{:S(2)}) async-start(), calls=%async_computation.13 | async-start | bytes 3538944 | tf_op jit(solution)/shard_map/psum | solution.py:849
  423.5 9.7 %copy-start.6 = (f32[1,768]{1,0:T(1,128)S(1)}, f32[1,768]{1,0:T(1,128)}, u32[]{:S(2)}) copy-start(f32[1,768]{1,0:T(1,128)} %get-tuple-element.152) | copy-start | bytes 9220
  423.5 9.7 %copy-start.7 = (f32[1,768]{1,0:T(1,128)S(1)}, f32[1,768]{1,0:T(1,128)}, u32[]{:S(2)}) copy-start(f32[1,768]{1,0:T(1,128)} %get-tuple-element.154) | copy-start | bytes 9220
  423.5 9.9 %copy-start.12 = (f32[1,768]{1,0:T(1,128)S(1)}, f32[1,768]{1,0:T(1,128)}, u32[]{:S(2)}) copy-start(f32[1,768]{1,0:T(1,128)} %get-tuple-element.151) | copy-start | bytes 9220
  423.5 9.9 %copy-start.13 = (f32[1,768]{1,0:T(1,128)S(1)}, f32[1,768]{1,0:T(1,128)}, u32[]{:S(2)}) copy-start(f32[1,768]{1,0:T(1,128)} %get-tuple-element.153) | copy-start | bytes 9220
  426.0 27.1 %collective-permute-start.3 = (bf16[384,768]{1,0:T(8,128)(2,1)}, bf16[384,768]{1,0:T(8,128)(2,1)}, u32[]{:S(2)}, u32[]{:S(2)}) collective-permute-start(bf16[384,768]{1,0:T(8,128)(2,1)} %fusion.5.refs_1_), channel_id=1, source_target_pairs={{0,4},{1,5},{2,6},{3,7},{4,0},{5,1},{6,2},{7,3},{8,12},{9,13},{10,... | collective-permute-start | bytes 1769480 | tf_op jit(solution)/shard_map/ppermute | solution.py:687
  432.0 22.9 %collective-permute-start.5 = (bf16[480,768]{1,0:T(8,128)(2,1)S(1)}, bf16[480,768]{1,0:T(8,128)(2,1)}, u32[]{:S(2)}, u32[]{:S(2)}) collective-permute-start(bf16[480,768]{1,0:T(8,128)(2,1)S(1)} %fusion.10.refs_2_), channel_id=1, source_target_pairs={{0,2},{1,3},{2,0},{3,1},{4,6},{5,7},{6,4},{7,5},{8,10},{9,11},{10,... | collective-permute-start | bytes 2211848 | tf_op jit(solution)/shard_map/ppermute | solution.py:687
  446.3 12.0 %all-to-all-start.6 = ((bf16[8,16,768]{2,1,0:T(8,128)(2,1)}), bf16[8,16,768]{2,1,0:T(8,128)(2,1)S(1)}, u32[]{:S(2)}, u32[]{:S(2)}) async-start(bf16[8,16,768]{2,1,0:T(8,128)(2,1)} %get-tuple-element.164), calls=%async_computation.8 | async-start | bytes 393216 | tf_op jit(solution)/shard_map/all_to_all | solution.py:773
  452.5 41.2 %collective-permute-start.9 = (bf16[4,144,768]{2,1,0:T(8,128)(2,1)}, bf16[4,144,768]{2,1,0:T(8,128)(2,1)}, u32[]{:S(2)}, u32[]{:S(2)}) collective-permute-start(bf16[4,144,768]{2,1,0:T(8,128)(2,1)} %get-tuple-element.176), channel_id=1, source_target_pairs={{0,1},{1,0},{2,3},{3,2},{4,5},{5,4},{6,7},{7,6},{8,9},{9,8},{10,11... | collective-permute-start | bytes 2654216 | tf_op jit(solution)/shard_map/ppermute | solution.py:687
  452.9 43.4 %collective-permute-start.6 = (bf16[4,144,768]{2,1,0:T(8,128)(2,1)}, bf16[4,144,768]{2,1,0:T(8,128)(2,1)}, u32[]{:S(2)}, u32[]{:S(2)}) collective-permute-start(bf16[4,144,768]{2,1,0:T(8,128)(2,1)} %get-tuple-element.175), channel_id=1, source_target_pairs={{0,1},{1,0},{2,3},{3,2},{4,5},{5,4},{6,7},{7,6},{8,9},{9,8},{10,11... | collective-permute-start | bytes 2654216 | tf_op jit(solution)/shard_map/ppermute | solution.py:687
  458.3 58.9 %all-to-all-start.5 = ((bf16[4,224,768]{2,1,0:T(8,128)(2,1)}), bf16[4,224,768]{2,1,0:T(8,128)(2,1)}, u32[]{:S(2)}, u32[]{:S(2)}) async-start(bf16[4,224,768]{2,1,0:T(8,128)(2,1)} %bitcast.13), calls=%async_computation.7 | async-start | bytes 2752512 | tf_op jit(solution)/shard_map/all_to_all | solution.py:727
  495.0 11.5 %collective-permute-start.10 = (bf16[2,144,768]{2,1,0:T(8,128)(2,1)S(1)}, bf16[2,144,768]{2,1,0:T(8,128)(2,1)S(1)}, u32[]{:S(2)}, u32[]{:S(2)}) collective-permute-start(bf16[2,144,768]{2,1,0:T(8,128)(2,1)S(1)} %add_convert_fusion.3), channel_id=1, source_target_pairs={{0,4},{1,5},{2,6},{3,7},{4,0},{5,1},{6,2},{7,3},{8,12},{9,13},{10,... | collective-permute-start | bytes 1327112 | tf_op jit(solution)/shard_map/ppermute | solution.py:687
  497.5 11.6 %collective-permute-start.7 = (bf16[2,144,768]{2,1,0:T(8,128)(2,1)S(1)}, bf16[2,144,768]{2,1,0:T(8,128)(2,1)S(1)}, u32[]{:S(2)}, u32[]{:S(2)}) collective-permute-start(bf16[2,144,768]{2,1,0:T(8,128)(2,1)S(1)} %fusion.12), channel_id=1, source_target_pairs={{0,2},{1,3},{2,0},{3,1},{4,6},{5,7},{6,4},{7,5},{8,10},{9,11},{10,... | collective-permute-start | bytes 1327112 | tf_op jit(solution)/shard_map/ppermute | solution.py:687
  507.7 6.0 %collective-permute-start.11 = (bf16[144,768]{1,0:T(8,128)(2,1)S(1)}, bf16[144,768]{1,0:T(8,128)(2,1)S(1)}, u32[]{:S(2)}, u32[]{:S(2)}) collective-permute-start(bf16[144,768]{1,0:T(8,128)(2,1)S(1)} %fusion.18), channel_id=1, source_target_pairs={{0,2},{1,3},{2,0},{3,1},{4,6},{5,7},{6,4},{7,5},{8,10},{9,11},{10,... | collective-permute-start | bytes 663560 | tf_op jit(solution)/shard_map/ppermute | solution.py:687
  510.1 6.0 %collective-permute-start.8 = (bf16[144,768]{1,0:T(8,128)(2,1)S(1)}, bf16[144,768]{1,0:T(8,128)(2,1)S(1)}, u32[]{:S(2)}, u32[]{:S(2)}) collective-permute-start(bf16[144,768]{1,0:T(8,128)(2,1)S(1)} %fusion.13), channel_id=1, source_target_pairs={{0,4},{1,5},{2,6},{3,7},{4,0},{5,1},{6,2},{7,3},{8,12},{9,13},{10,... | collective-permute-start | bytes 663560 | tf_op jit(solution)/shard_map/ppermute | solution.py:687
  565.6 15.7 %all-to-all-start.8 = ((bf16[4,80,768]{2,1,0:T(8,128)(2,1)}), bf16[4,80,768]{2,1,0:T(8,128)(2,1)S(1)}, u32[]{:S(2)}, u32[]{:S(2)}) async-start(bf16[4,80,768]{2,1,0:T(8,128)(2,1)} %broadcast_in_dim.29), calls=%async_computation.10 | async-start | bytes 983040 | tf_op jit(solution)/shard_map/all_to_all | solution.py:727
  (5 other events, 19.0 us)
Sparse Core Ops, SparseCore 0:
  197.1 58.3 reduce-scatter.2
  278.9 78.5 reduce-scatter.4
  402.0 87.1 all-reduce.5

commit v5 on v4

--- a/solution.py
+++ b/solution.py
@@ -235,7 +235,7 @@
         shift_o[...] = jnp.zeros_like(shift_o)
 
     total = None
-    for c in chunks(hidden, 512):
+    for c in chunks(hidden, 1024):
         pre = (dot(grad, w_reduce[c, :], 1, 1) * slope[:, c].astype(WIDE)).astype(LOW)
         pre_o[:, c] = pre
         bias_o[:, c] += jnp.sum(pre.astype(WIDE), axis=0, keepdims=True)
@@ -309,12 +309,15 @@
         gain_o[...] = jnp.zeros_like(gain_o)
         shift_o[...] = jnp.zeros_like(shift_o)
 
-    total = dot(triple[...], w_in[...], 1, 1)
-    n, scale = normalize(load_rows(x, x_layout, windows).astype(WIDE))
-    gain_o[...] += jnp.sum(total * n, axis=0, keepdims=True)
-    shift_o[...] += jnp.sum(total, axis=0, keepdims=True)
-    grad_x = (mid[...] + normalize_back(n, scale, gain[block, 0], total)).astype(LOW)
-    store_rows(out, layout, windows, grad_x)
+    stream = load_rows(x, x_layout, windows)
+    length = stream.shape[0] // windows
+    totals = [dot(triple[span, :], w_in[...], 1, 1) for span in chunks(windows * length, length)]
+    for w, (span, total) in enumerate(zip(chunks(windows * length, length), totals)):
+        n, scale = normalize(stream[span].astype(WIDE))
+        gain_o[...] += jnp.sum(total * n, axis=0, keepdims=True)
+        shift_o[...] += jnp.sum(total, axis=0, keepdims=True)
+        grad_x = (mid[span, :] + normalize_back(n, scale, gain[block, 0], total)).astype(LOW)
+        store_window(out, layout, w, grad_x)
 
 
 def finish_kernel(windows, x, mid, triple, gain, w_in, mixed, *refs):

time: 602 us -> 600 us (level)
  no operation moved by 1% of the time
where the time goes in v5:
time: 600 us; the launch traced here: 591 us
  Pallas kernels  382 us (64%)
  waiting for transfers between devices  66.7 us (11%)
  starting transfers between devices  47.9 us (8%)
  blocking collectives  45.8 us (8%)
  other arithmetic  23.9 us (4%)
  between operations  14.5 us (2%)
  local copies, waits for them, and re-layouts  10.5 us (2%)
    pallas_call x4, Pallas kernels, forward(): pl.pallas_call(functools.partial(forward_kernel, dims), grid=(steps,), in...  113 us
    pallas_call x2, Pallas kernels, attention_back(): pl.pallas_call(functools.partial(attention_back_kernel, (block, 1, length...  72.9 us
    pallas_call x2, Pallas kernels, mlp_back(): pl.pallas_call(functools.partial(mlp_back_kernel, (block, windows, width,...  64.7 us
    pallas_call x4, Pallas kernels, outer_columns(): pl.pallas_call(functools.partial(outer_kernel, bool(last), is_split), gri...  64.2 us
    all_to_all x1, blocking collectives, over_clips(): got = lax.all_to_all(value, 'clip', 0, 0)  45.8 us
    pallas_call x2, Pallas kernels, outer_rows(): pl.pallas_call(functools.partial(outer_kernel, False, is_split), grid_spe...  29.4 us
    all_to_all x6, starting transfers between devices, exchange(): return lax.all_to_all(value, 'frame', 0, 0)  27.3 us
    psum x1, waiting for transfers between devices, local(): reduce1_sum, rest1_sum = lax.psum((reduce1_sum, rest1_sum), 'clip')  26.6 us
  transfers between devices with their start and end apart: 23, of which 10 were waited for; matrix products, arithmetic and copies ran while one was open for 5% of the time, Pallas kernels for 51%

profile of v5, /device:TPU:0, one launch (start us, length us, event | category | flops | bytes accessed | tf_op | source)
XLA Modules:
  0.0 590.9 jit_solution(15810217630754680455)
XLA Ops:
  7.2 30.6 %forward_0.2 = (bf16[8,2,2,32,768]{4,3,2,1,0:T(8,128)(2,1)}, bf16[2048,768]{1,0:T(8,128)(2,1)}, bf16[2048,2304]{1,0:T(8,128)(2,1)}, f32[2048,768]{1,0:T(8,128)},...) custom-call(s32[4]{0:T(128)} %counts.7, ...), custom_call_target="tpu_custom_call" | custom-call | flops 12600000512 | bytes 37800000 | tf_op jit(solution)/shard_map/forward_0/pallas_call | solution.py:476
  37.8 5.7 all-to-all-start
  43.5 30.6 %forward_0.3 = (bf16[8,2,2,32,768]{4,3,2,1,0:T(8,128)(2,1)}, bf16[2048,768]{1,0:T(8,128)(2,1)}, bf16[2048,2304]{1,0:T(8,128)(2,1)}, f32[2048,768]{1,0:T(8,128)},...) custom-call(s32[4]{0:T(128)} %counts.7, ...), custom_call_target="tpu_custom_call", output_to_operand_aliasing={{1}: (10, {}), {2}: (11, {}), {3}: (12, {}), {4}: (13, {}),... | custom-call | flops 12600000512 | bytes 37800000 | tf_op jit(solution)/shard_map/forward_0/pallas_call | solution.py:476
  74.1 4.5 all-to-all-start.2
  78.6 25.8 %forward_1.2 = (bf16[8,4,2,32,768]{4,3,2,1,0:T(8,128)(2,1)}, bf16[2048,768]{1,0:T(8,128)(2,1)}, bf16[2048,2304]{1,0:T(8,128)(2,1)}, f32[2048,768]{1,0:T(8,128)},...) custom-call(s32[4]{0:T(128)} %counts.7, ...), custom_call_target="tpu_custom_call", output_to_operand_aliasing={{0}: (9, {})} | custom-call | flops 10499999744 | bytes 31500000 | tf_op jit(solution)/shard_map/forward_1/pallas_call | solution.py:476
  104.4 4.5 all-to-all-start.1
  109.2 25.9 %forward_1.3 = (bf16[2048,768]{1,0:T(8,128)(2,1)}, bf16[2048,2304]{1,0:T(8,128)(2,1)}, f32[2048,768]{1,0:T(8,128)}, bf16[8,6,256,512]{3,2,1,0:T(8,128)(2,1)}, bf...) custom-call(s32[4]{0:T(128)} %counts.7, ...), custom_call_target="tpu_custom_call", output_to_operand_aliasing={{0}: (9, {}), {1}: (10, {}), {2}: (11, {}), {3}: (12, {}), ... | custom-call | flops 10499999744 | bytes 31500000 | tf_op jit(solution)/shard_map/forward_1/pallas_call | solution.py:476
  135.1 15.2 %output.1.refs_6_ = bf16[8,4,2,32,768]{4,3,2,1,0:T(8,128)(2,1)} custom-call(bf16[2048,3072]{1,0:T(8,128)(2,1)} %get-tuple-element.117.active.left, f32[2048,768]{1,0:T(8,128)} %get-tuple-element.116.middle.refs_2_, bf16[2,3072,768]{2,1,0:T(8,128)(2,1)} %refs_5_.14), custom_call_target="tpu_custom_call" | custom-call | flops 4899999744 | bytes 14700000 | tf_op jit(solution)/shard_map/output/pallas_call | solution.py:498
  150.3 31.3 %mlp_back_1.1 = (bf16[8,4,2,32,768]{4,3,2,1,0:T(8,128)(2,1)}, bf16[2048,768]{1,0:T(8,128)(2,1)}, bf16[2048,3072]{1,0:T(8,128)(2,1)}, f32[2048,768]{1,0:T(8,128)}...) custom-call(bf16[8,4,2,32,768]{4,3,2,1,0:T(8,128)(2,1)} %all-to-all-done.1.refs_0_, ...), custom_call_target="tpu_custom_call", output_to_operand_aliasing={{0}: (6, {})} | custom-call | flops 140000002048 | bytes 420000000 | tf_op jit(solution)/shard_map/mlp_back_1/pallas_call | solution.py:522
  181.6 14.5 %outer_rows.2.refs_9_ = bf16[8,384,768]{2,1,0:T(8,128)(2,1)} custom-call(s32[1]{0:T(128)} %bitcast.place, bf16[2048,3072]{1,0:T(8,128)(2,1)} %get-tuple-element.117.active.left, bf16[2048,768]{1,0:T(8,128)(2,1)} %get-tuple-element.124.right), custom_call_target="tpu_custom_call" | custom-call | flops 4899999744 | bytes 14700000 | tf_op jit(solution)/shard_map/outer_rows/pallas_call | solution.py:629
  196.2 45.1 %attention_back_1.1 = (bf16[2048,2304]{1,0:T(8,128)(2,1)}, f32[1,768]{1,0:T(1,128)}, f32[1,768]{1,0:T(1,128)}, bf16[8,4,2,32,768]{4,3,2,1,0:T(8,128)(2,1)}) custom-call(f32[2048,768]{1,0:T(8,128)} %get-tuple-element.118.refs_0_.refs_1_, bf16[2048,2304]{1,0:T(8,128)(2,1)} %get-tuple-element.119.refs_1_, f32[2048,768]{1,0:T(8,128)} %get-tuple-element.120.refs_2_, ...), custom_call_target="tpu_custom_call" | custom-call | flops 14700000256 | bytes 44100000 | tf_op jit(solution)/shard_map/attention_back_1/pallas_call | solution.py:571
  241.3 4.5 all-to-all-start.3
  245.8 14.8 %outer_columns.5.refs_2_ = bf16[8,768,768]{2,1,0:T(8,128)(2,1)} custom-call(s32[1]{0:T(128)} %bitcast.place, bf16[2048,768]{1,0:T(8,128)(2,1)} %get-tuple-element.141.left, bf16[2048,3072]{1,0:T(8,128)(2,1)} %get-tuple-element.142.right), custom_call_target="tpu_custom_call" | custom-call | flops 5600000000 | bytes 16800000 | tf_op jit(solution)/shard_map/outer_columns/pallas_call | solution.py:669
  260.6 17.3 %outer_columns.6 = bf16[8,768,768]{2,1,0:T(8,128)(2,1)} custom-call(s32[1]{0:T(128)} %bitcast.place, bf16[2048,768]{1,0:T(8,128)(2,1)} %get-tuple-element.139.left, bf16[2048,2304]{1,0:T(8,128)(2,1)} %get-tuple-element.140.right, bf16[2048,768]{1,0:T(8,128)(2,1)} %get-tuple-element.122.refs_4_.refs_0_, ...), custom_call_target="tpu_custom_call", output_to_operand_aliasing={{}: (5, {})} | custom-call | flops 5600000000 | bytes 16800000 | tf_op jit(solution)/shard_map/outer_columns/pallas_call | solution.py:669
  278.0 7.9 %all-to-all-done.3.refs_0_ = bf16[8,4,2,32,768]{4,3,2,1,0:T(8,128)(2,1)} async-done(((bf16[8,4,2,32,768]{4,3,2,1,0:T(8,128)(2,1)}), bf16[8,4,2,32,768]{4,3,2,1,0:T(8,128)(2,1)}, u32[]{:S(2)}, u32[]{:S(2)}) %all-to-all-start.3) | async-done | bytes 3145760 | tf_op jit(solution)/shard_map/all_to_all | solution.py:776
  285.9 33.4 %mlp_back_0.1 = (bf16[2048,768]{1,0:T(8,128)(2,1)}, bf16[2048,3072]{1,0:T(8,128)(2,1)}, f32[2048,768]{1,0:T(8,128)}, f32[1,3072]{1,0:T(1,128)}, f32[1,768]{1,0:T(1,128)}, /*index=5*/f32[1,768]{1,0:T(1,128)}) custom-call(bf16[8,4,2,32,768]{4,3,2,1,0:T(8,128)(2,1)} %all-to-all-done.3.refs_0_, bf16[2048,3072]{1,0:T(8,128)(2,1)} %get-tuple-element.126.refs_1_, ...), custom_call_target="tpu_custom_call" | custom-call | flops 140000002048 | bytes 420000000 | tf_op jit(solution)/shard_map/mlp_back_0/pallas_call | solution.py:522
  319.3 14.8 %outer_rows.3 = (bf16[4,384,768]{2,1,0:T(8,128)(2,1)}, bf16[4,384,768]{2,1,0:T(8,128)(2,1)}) custom-call(s32[1]{0:T(128)} %bitcast.place, bf16[2048,3072]{1,0:T(8,128)(2,1)} %get-tuple-element.135.left, bf16[2048,768]{1,0:T(8,128)(2,1)} %get-tuple-element.136.right), custom_call_target="tpu_custom_call" | custom-call | flops 4899999744 | bytes 14700000 | tf_op jit(solution)/shard_map/outer_rows/pallas_call | solution.py:629
  334.1 20.2 %outer_columns.4 = (bf16[4,480,768]{2,1,0:T(8,128)(2,1)}, bf16[4,480,768]{2,1,0:T(8,128)(2,1)}) custom-call(s32[1]{0:T(128)} %bitcast.place, bf16[2048,768]{1,0:T(8,128)(2,1)} %get-tuple-element.133.left, bf16[2048,3072]{1,0:T(8,128)(2,1)} %get-tuple-element.134.right, bf16[2048,768]{1,0:T(8,128)(2,1)} %get-tuple-element.132.refs_0_.refs_4_, ...), custom_call_target="tpu_custom_call" | custom-call | flops 7000000000 | bytes 21000000 | tf_op jit(solution)/shard_map/outer_columns/pallas_call | solution.py:669
  354.8 4.7 all-to-all-start.4
  369.2 27.7 %attention_back_0.1.triple.right = bf16[2048,2304]{1,0:T(8,128)(2,1)} custom-call(f32[2048,768]{1,0:T(8,128)} %get-tuple-element.128.refs_1_.refs_0_.mid, bf16[2048,2304]{1,0:T(8,128)(2,1)} %get-tuple-element.129.refs_1_, f32[2048,768]{1,0:T(8,128)} %get-tuple-element.130.refs_2_, bf16[8,6,256,512]{3,2,1,0:T(8,128)(2,1)} %get-tuple-element.131.refs_3_, ...), custom_call_target="tpu_custom_call" | custom-call | flops 3500000 | bytes 10500 | tf_op jit(solution)/shard_map/attention_back_0/pallas_call | solution.py:571
  397.9 15.7 %finish.1 = (bf16[4,384,768]{2,1,0:T(8,128)(2,1)}, bf16[4,480,768]{2,1,0:T(8,128)(2,1)}, f32[1,768]{1,0:T(1,128)}, f32[1,768]{1,0:T(1,128)}, bf16[4,2,256,768]{3...) custom-call(bf16[4,2,256,768]{3,2,1,0:T(8,128)(2,1)} %x.11, ...), custom_call_target="tpu_custom_call", output_to_operand_aliasing={{0}: (6, {}), {1}: (7, {})} | custom-call | flops 3500000 | bytes 10500 | tf_op jit(solution)/shard_map/finish/pallas_call | solution.py:591
  413.7 8.1 %collective-permute-done.2 = bf16[2,384,768]{2,1,0:T(8,128)(2,1)} collective-permute-done((bf16[2,384,768]{2,1,0:T(8,128)(2,1)}, bf16[2,384,768]{2,1,0:T(8,128)(2,1)}, u32[]{:S(2)}, u32[]{:S(2)}) %collective-permute-start.2) | collective-permute-done | bytes 1179680 | tf_op jit(solution)/shard_map/ppermute | solution.py:690
  432.8 11.9 %outer_columns.7 = (bf16[8,16,768]{2,1,0:T(8,128)(2,1)}, bf16[4,288,768]{2,1,0:T(8,128)(2,1)}, bf16[4,288,768]{2,1,0:T(8,128)(2,1)}) custom-call(s32[1]{0:T(128)} %bitcast.place, bf16[2048,768]{1,0:T(8,128)(2,1)} %get-tuple-element.150.left, bf16[2048,2304]{1,0:T(8,128)(2,1)} %attention_back_0.1.triple.right, ...), custom_call_target="tpu_custom_call", output_to_operand_aliasing={{0}: (3, {})} | custom-call | flops 350000000 | bytes 1050000 | tf_op jit(solution)/shard_map/outer_columns/pallas_call | solution.py:669
  444.7 3.4 all-to-all-start.6
  456.6 4.5 all-to-all-start.5
  461.1 26.6 %all-reduce.6.cloned.1.call-done = (bf16[384,768]{1,0:T(8,128)(2,1)}, bf16[768,768]{1,0:T(8,128)(2,1)}) async-done(((bf16[384,768]{1,0:T(8,128)(2,1)}, bf16[768,768]{1,0:T(8,128)(2,1)}), (bf16[384,768]{1,0:T(8,128)(2,1)}, bf16[768,768]{1,0:T(8,128)(2,1)})) %all-reduce.6.cloned.1.call-update) | async-done | bytes 1769488 | tf_op jit(solution)/shard_map/psum | solution.py:852
  487.7 3.3 gather.2
  497.6 7.5 %collective-permute-done.10 = bf16[2,144,768]{2,1,0:T(8,128)(2,1)S(1)} collective-permute-done((bf16[2,144,768]{2,1,0:T(8,128)(2,1)S(1)}, bf16[2,144,768]{2,1,0:T(8,128)(2,1)S(1)}, u32[]{:S(2)}, u32[]{:S(2)}) %collective-permute-start.10) | collective-permute-done | bytes 442400 | tf_op jit(solution)/shard_map/ppermute | solution.py:690
  517.4 45.8 %all_to_all.45 = bf16[4,320,768]{2,1,0:T(8,128)(2,1)S(1)} all-to-all(bf16[4,320,768]{2,1,0:T(8,128)(2,1)S(1)} %pad_maximum_fusion), channel_id=1, replica_groups=mesh['clip'=4,'frame'=8] {'clip'}, dimensions={0} | all-to-all | bytes 3932160 | tf_op jit(solution)/shard_map/all_to_all | solution.py:730
  564.1 3.5 all-to-all-start.8
  570.8 9.0 %all-to-all-done.8 = bf16[4,80,768]{2,1,0:T(8,128)(2,1)S(1)} async-done(((bf16[4,80,768]{2,1,0:T(8,128)(2,1)}), bf16[4,80,768]{2,1,0:T(8,128)(2,1)S(1)}, u32[]{:S(2)}, u32[]{:S(2)}) %all-to-all-start.8) | async-done | bytes 491552 | tf_op jit(solution)/shard_map/all_to_all | solution.py:730
  580.6 3.3 gather.3
  (112 shorter events, 54.6 us)
Async XLA Ops:
  37.8 36.3 %all-to-all-start = ((bf16[8,2,2,32,768]{4,3,2,1,0:T(8,128)(2,1)}), bf16[8,2,2,32,768]{4,3,2,1,0:T(8,128)(2,1)}, u32[]{:S(2)}, u32[]{:S(2)}) async-start(bf16[8,2,2,32,768]{4,3,2,1,0:T(8,128)(2,1)} %get-tuple-element.91), calls=%async_computation | async-start | bytes 3145728 | tf_op jit(solution)/shard_map/all_to_all | solution.py:776
  74.1 30.3 %all-to-all-start.2 = ((bf16[8,2,2,32,768]{4,3,2,1,0:T(8,128)(2,1)}), bf16[8,2,2,32,768]{4,3,2,1,0:T(8,128)(2,1)}, u32[]{:S(2)}, u32[]{:S(2)}) async-start(bf16[8,2,2,32,768]{4,3,2,1,0:T(8,128)(2,1)} %get-tuple-element.104), calls=%async_computation.2 | async-start | bytes 3145728 | tf_op jit(solution)/shard_map/all_to_all | solution.py:776
  104.4 45.9 %all-to-all-start.1 = ((bf16[8,4,2,32,768]{4,3,2,1,0:T(8,128)(2,1)}), bf16[8,4,2,32,768]{4,3,2,1,0:T(8,128)(2,1)}, u32[]{:S(2)}, u32[]{:S(2)}) async-start(bf16[8,4,2,32,768]{4,3,2,1,0:T(8,128)(2,1)} %get-tuple-element.103), calls=%async_computation.1 | async-start | bytes 6291456 | tf_op jit(solution)/shard_map/all_to_all | solution.py:776
  108.9 151.7 %reduce-scatter.3.cloned.1.call-start = ((), (), s32[]{:S(2)}) async-start(), calls=%async_computation.11 | async-start | bytes 5308416 | tf_op jit(solution)/shard_map/reduce_scatter | solution.py:813
  241.3 44.6 %all-to-all-start.3 = ((bf16[8,4,2,32,768]{4,3,2,1,0:T(8,128)(2,1)}), bf16[8,4,2,32,768]{4,3,2,1,0:T(8,128)(2,1)}, u32[]{:S(2)}, u32[]{:S(2)}) async-start(bf16[8,4,2,32,768]{4,3,2,1,0:T(8,128)(2,1)} %get-tuple-element.125), calls=%async_computation.3 | async-start | bytes 6291456 | tf_op jit(solution)/shard_map/all_to_all | solution.py:776
  245.8 123.4 %reduce-scatter.5.cloned.1.call-start = ((), (), s32[]{:S(2)}) async-start(), calls=%async_computation.12 | async-start | bytes 10616832 | tf_op jit(solution)/shard_map/reduce_scatter | solution.py:813
  354.3 5.7 collective-permute-start.1
  354.3 10.3 %collective-permute-start = (bf16[4,384,768]{2,1,0:T(8,128)(2,1)}, bf16[4,384,768]{2,1,0:T(8,128)(2,1)}, u32[]{:S(2)}, u32[]{:S(2)}) collective-permute-start(bf16[4,384,768]{2,1,0:T(8,128)(2,1)} %get-tuple-element.137.refs_2_), channel_id=1, source_target_pairs={{0,1},{1,0},{2,3},{3,2},{4,5},{5,4},{6,7},{7,6},{8,9},{9,8},{10,11... | collective-permute-start | bytes 7077896 | tf_op jit(solution)/shard_map/ppermute | solution.py:690
  354.8 43.1 %all-to-all-start.4 = ((bf16[8,4,2,32,768]{4,3,2,1,0:T(8,128)(2,1)}), bf16[8,4,2,32,768]{4,3,2,1,0:T(8,128)(2,1)}, u32[]{:S(2)}, u32[]{:S(2)}) async-start(bf16[8,4,2,32,768]{4,3,2,1,0:T(8,128)(2,1)} %get-tuple-element.143), calls=%async_computation.6 | async-start | bytes 6291456 | tf_op jit(solution)/shard_map/all_to_all | solution.py:776
  363.1 5.6 copy-start.11
  363.1 5.7 copy-start.8
  363.1 5.7 copy-start.9
  363.1 6.0 %copy-start.4 = (f32[1,3072]{1,0:T(1,128)S(1)}, f32[1,3072]{1,0:T(1,128)}, u32[]{:S(2)}) copy-start(f32[1,3072]{1,0:T(1,128)} %get-tuple-element.160) | copy-start | bytes 36868
  363.1 6.0 %copy-start.5 = (f32[1,3072]{1,0:T(1,128)S(1)}, f32[1,3072]{1,0:T(1,128)}, u32[]{:S(2)}) copy-start(f32[1,3072]{1,0:T(1,128)} %get-tuple-element.155) | copy-start | bytes 36868
  363.1 65.4 %collective-permute-start.4 = (bf16[2,480,768]{2,1,0:T(8,128)(2,1)}, bf16[2,480,768]{2,1,0:T(8,128)(2,1)}, u32[]{:S(2)}, u32[]{:S(2)}) collective-permute-start(bf16[2,480,768]{2,1,0:T(8,128)(2,1)} %add_convert_fusion.refs_3_), channel_id=1, source_target_pairs={{0,4},{1,5},{2,6},{3,7},{4,0},{5,1},{6,2},{7,3},{8,12},{9,13},{10,... | collective-permute-start | bytes 4423688 | tf_op jit(solution)/shard_map/ppermute | solution.py:690
  367.1 54.7 %collective-permute-start.2 = (bf16[2,384,768]{2,1,0:T(8,128)(2,1)}, bf16[2,384,768]{2,1,0:T(8,128)(2,1)}, u32[]{:S(2)}, u32[]{:S(2)}) collective-permute-start(bf16[2,384,768]{2,1,0:T(8,128)(2,1)} %fusion.4.refs_2_), channel_id=1, source_target_pairs={{0,2},{1,3},{2,0},{3,1},{4,6},{5,7},{6,4},{7,5},{8,10},{9,11},{10,... | collective-permute-start | bytes 3538952 | tf_op jit(solution)/shard_map/ppermute | solution.py:690
  396.9 90.8 %all-reduce.6.cloned.1.call-start = ((), (), s32[]{:S(2)}) async-start(), calls=%async_computation.13 | async-start | bytes 3538944 | tf_op jit(solution)/shard_map/psum | solution.py:852
  421.8 9.7 %copy-start.6 = (f32[1,768]{1,0:T(1,128)S(1)}, f32[1,768]{1,0:T(1,128)}, u32[]{:S(2)}) copy-start(f32[1,768]{1,0:T(1,128)} %get-tuple-element.152) | copy-start | bytes 9220
  421.8 9.7 %copy-start.7 = (f32[1,768]{1,0:T(1,128)S(1)}, f32[1,768]{1,0:T(1,128)}, u32[]{:S(2)}) copy-start(f32[1,768]{1,0:T(1,128)} %get-tuple-element.154) | copy-start | bytes 9220
  421.8 9.9 %copy-start.12 = (f32[1,768]{1,0:T(1,128)S(1)}, f32[1,768]{1,0:T(1,128)}, u32[]{:S(2)}) copy-start(f32[1,768]{1,0:T(1,128)} %get-tuple-element.151) | copy-start | bytes 9220
  421.8 9.9 %copy-start.13 = (f32[1,768]{1,0:T(1,128)S(1)}, f32[1,768]{1,0:T(1,128)}, u32[]{:S(2)}) copy-start(f32[1,768]{1,0:T(1,128)} %get-tuple-element.153) | copy-start | bytes 9220
  424.3 27.1 %collective-permute-start.3 = (bf16[384,768]{1,0:T(8,128)(2,1)}, bf16[384,768]{1,0:T(8,128)(2,1)}, u32[]{:S(2)}, u32[]{:S(2)}) collective-permute-start(bf16[384,768]{1,0:T(8,128)(2,1)} %fusion.5.refs_1_), channel_id=1, source_target_pairs={{0,4},{1,5},{2,6},{3,7},{4,0},{5,1},{6,2},{7,3},{8,12},{9,13},{10,... | collective-permute-start | bytes 1769480 | tf_op jit(solution)/shard_map/ppermute | solution.py:690
  430.4 22.9 %collective-permute-start.5 = (bf16[480,768]{1,0:T(8,128)(2,1)S(1)}, bf16[480,768]{1,0:T(8,128)(2,1)}, u32[]{:S(2)}, u32[]{:S(2)}) collective-permute-start(bf16[480,768]{1,0:T(8,128)(2,1)S(1)} %fusion.10.refs_2_), channel_id=1, source_target_pairs={{0,2},{1,3},{2,0},{3,1},{4,6},{5,7},{6,4},{7,5},{8,10},{9,11},{10,... | collective-permute-start | bytes 2211848 | tf_op jit(solution)/shard_map/ppermute | solution.py:690
  444.7 12.0 %all-to-all-start.6 = ((bf16[8,16,768]{2,1,0:T(8,128)(2,1)}), bf16[8,16,768]{2,1,0:T(8,128)(2,1)S(1)}, u32[]{:S(2)}, u32[]{:S(2)}) async-start(bf16[8,16,768]{2,1,0:T(8,128)(2,1)} %get-tuple-element.164), calls=%async_computation.8 | async-start | bytes 393216 | tf_op jit(solution)/shard_map/all_to_all | solution.py:776
  450.9 41.4 %collective-permute-start.9 = (bf16[4,144,768]{2,1,0:T(8,128)(2,1)}, bf16[4,144,768]{2,1,0:T(8,128)(2,1)}, u32[]{:S(2)}, u32[]{:S(2)}) collective-permute-start(bf16[4,144,768]{2,1,0:T(8,128)(2,1)} %get-tuple-element.176), channel_id=1, source_target_pairs={{0,1},{1,0},{2,3},{3,2},{4,5},{5,4},{6,7},{7,6},{8,9},{9,8},{10,11... | collective-permute-start | bytes 2654216 | tf_op jit(solution)/shard_map/ppermute | solution.py:690
  451.2 43.6 %collective-permute-start.6 = (bf16[4,144,768]{2,1,0:T(8,128)(2,1)}, bf16[4,144,768]{2,1,0:T(8,128)(2,1)}, u32[]{:S(2)}, u32[]{:S(2)}) collective-permute-start(bf16[4,144,768]{2,1,0:T(8,128)(2,1)} %get-tuple-element.175), channel_id=1, source_target_pairs={{0,1},{1,0},{2,3},{3,2},{4,5},{5,4},{6,7},{7,6},{8,9},{9,8},{10,11... | collective-permute-start | bytes 2654216 | tf_op jit(solution)/shard_map/ppermute | solution.py:690
  456.6 59.1 %all-to-all-start.5 = ((bf16[4,224,768]{2,1,0:T(8,128)(2,1)}), bf16[4,224,768]{2,1,0:T(8,128)(2,1)}, u32[]{:S(2)}, u32[]{:S(2)}) async-start(bf16[4,224,768]{2,1,0:T(8,128)(2,1)} %bitcast.13), calls=%async_computation.7 | async-start | bytes 2752512 | tf_op jit(solution)/shard_map/all_to_all | solution.py:730
  493.5 11.5 %collective-permute-start.10 = (bf16[2,144,768]{2,1,0:T(8,128)(2,1)S(1)}, bf16[2,144,768]{2,1,0:T(8,128)(2,1)S(1)}, u32[]{:S(2)}, u32[]{:S(2)}) collective-permute-start(bf16[2,144,768]{2,1,0:T(8,128)(2,1)S(1)} %add_convert_fusion.3), channel_id=1, source_target_pairs={{0,4},{1,5},{2,6},{3,7},{4,0},{5,1},{6,2},{7,3},{8,12},{9,13},{10,... | collective-permute-start | bytes 1327112 | tf_op jit(solution)/shard_map/ppermute | solution.py:690
  496.0 11.6 %collective-permute-start.7 = (bf16[2,144,768]{2,1,0:T(8,128)(2,1)S(1)}, bf16[2,144,768]{2,1,0:T(8,128)(2,1)S(1)}, u32[]{:S(2)}, u32[]{:S(2)}) collective-permute-start(bf16[2,144,768]{2,1,0:T(8,128)(2,1)S(1)} %fusion.12), channel_id=1, source_target_pairs={{0,2},{1,3},{2,0},{3,1},{4,6},{5,7},{6,4},{7,5},{8,10},{9,11},{10,... | collective-permute-start | bytes 1327112 | tf_op jit(solution)/shard_map/ppermute | solution.py:690
  506.2 6.0 %collective-permute-start.11 = (bf16[144,768]{1,0:T(8,128)(2,1)S(1)}, bf16[144,768]{1,0:T(8,128)(2,1)S(1)}, u32[]{:S(2)}, u32[]{:S(2)}) collective-permute-start(bf16[144,768]{1,0:T(8,128)(2,1)S(1)} %fusion.18), channel_id=1, source_target_pairs={{0,2},{1,3},{2,0},{3,1},{4,6},{5,7},{6,4},{7,5},{8,10},{9,11},{10,... | collective-permute-start | bytes 663560 | tf_op jit(solution)/shard_map/ppermute | solution.py:690
  508.6 6.0 %collective-permute-start.8 = (bf16[144,768]{1,0:T(8,128)(2,1)S(1)}, bf16[144,768]{1,0:T(8,128)(2,1)S(1)}, u32[]{:S(2)}, u32[]{:S(2)}) collective-permute-start(bf16[144,768]{1,0:T(8,128)(2,1)S(1)} %fusion.13), channel_id=1, source_target_pairs={{0,4},{1,5},{2,6},{3,7},{4,0},{5,1},{6,2},{7,3},{8,12},{9,13},{10,... | collective-permute-start | bytes 663560 | tf_op jit(solution)/shard_map/ppermute | solution.py:690
  564.1 15.7 %all-to-all-start.8 = ((bf16[4,80,768]{2,1,0:T(8,128)(2,1)}), bf16[4,80,768]{2,1,0:T(8,128)(2,1)S(1)}, u32[]{:S(2)}, u32[]{:S(2)}) async-start(bf16[4,80,768]{2,1,0:T(8,128)(2,1)} %broadcast_in_dim.29), calls=%async_computation.10 | async-start | bytes 983040 | tf_op jit(solution)/shard_map/all_to_all | solution.py:730
  (5 other events, 19.0 us)
Sparse Core Ops, SparseCore 0:
  196.3 58.3 reduce-scatter.2
  278.1 78.5 reduce-scatter.4
  400.3 87.3 all-reduce.5

commit v6 on v5

--- a/solution.py
+++ b/solution.py
@@ -720,7 +720,7 @@
 
 def clip_blocks(total):
     size = lax.axis_size("clip")
-    rows = -(-total.shape[0] // (16 * size)) * 16
+    rows = -(-total.shape[0] // (8 * size)) * 8
     total = jnp.pad(total, ((0, rows * size - total.shape[0]), (0, 0)))
     return total.reshape(size, rows, total.shape[1])
 

time: 600 us -> 597 us (level)
  no operation moved by 1% of the time
where the time goes in v6:
time: 597 us; the launch traced here: 588 us
  Pallas kernels  382 us (64%)
  waiting for transfers between devices  65.7 us (11%)
  starting transfers between devices  47.9 us (8%)
  blocking collectives  43.6 us (7%)
  other arithmetic  23.8 us (4%)
  between operations  14.5 us (2%)
  local copies, waits for them, and re-layouts  10.5 us (2%)
    pallas_call x4, Pallas kernels, forward(): pl.pallas_call(functools.partial(forward_kernel, dims), grid=(steps,), in...  113 us
    pallas_call x2, Pallas kernels, attention_back(): pl.pallas_call(functools.partial(attention_back_kernel, (block, 1, length...  72.9 us
    pallas_call x2, Pallas kernels, mlp_back(): pl.pallas_call(functools.partial(mlp_back_kernel, (block, windows, width,...  64.7 us
    pallas_call x4, Pallas kernels, outer_columns(): pl.pallas_call(functools.partial(outer_kernel, bool(last), is_split), gri...  64.2 us
    all_to_all x1, blocking collectives, over_clips(): got = lax.all_to_all(value, 'clip', 0, 0)  43.6 us
    pallas_call x2, Pallas kernels, outer_rows(): pl.pallas_call(functools.partial(outer_kernel, False, is_split), grid_spe...  29.4 us
    all_to_all x6, starting transfers between devices, exchange(): return lax.all_to_all(value, 'frame', 0, 0)  27.3 us
    psum x1, waiting for transfers between devices, local(): reduce1_sum, rest1_sum = lax.psum((reduce1_sum, rest1_sum), 'clip')  26.3 us
  transfers between devices with their start and end apart: 23, of which 10 were waited for; matrix products, arithmetic and copies ran while one was open for 5% of the time, Pallas kernels for 51%

profile of v6, /device:TPU:0, one launch (start us, length us, event | category | flops | bytes accessed | tf_op | source)
XLA Modules:
  0.0 587.5 jit_solution(10646835825083209737)
XLA Ops:
  7.2 30.6 %forward_0.2 = (bf16[8,2,2,32,768]{4,3,2,1,0:T(8,128)(2,1)}, bf16[2048,768]{1,0:T(8,128)(2,1)}, bf16[2048,2304]{1,0:T(8,128)(2,1)}, f32[2048,768]{1,0:T(8,128)},...) custom-call(s32[4]{0:T(128)} %counts.7, ...), custom_call_target="tpu_custom_call" | custom-call | flops 12600000512 | bytes 37800000 | tf_op jit(solution)/shard_map/forward_0/pallas_call | solution.py:476
  37.8 5.7 all-to-all-start
  43.5 30.6 %forward_0.3 = (bf16[8,2,2,32,768]{4,3,2,1,0:T(8,128)(2,1)}, bf16[2048,768]{1,0:T(8,128)(2,1)}, bf16[2048,2304]{1,0:T(8,128)(2,1)}, f32[2048,768]{1,0:T(8,128)},...) custom-call(s32[4]{0:T(128)} %counts.7, ...), custom_call_target="tpu_custom_call", output_to_operand_aliasing={{1}: (10, {}), {2}: (11, {}), {3}: (12, {}), {4}: (13, {}),... | custom-call | flops 12600000512 | bytes 37800000 | tf_op jit(solution)/shard_map/forward_0/pallas_call | solution.py:476
  74.1 4.5 all-to-all-start.2
  78.6 25.8 %forward_1.2 = (bf16[8,4,2,32,768]{4,3,2,1,0:T(8,128)(2,1)}, bf16[2048,768]{1,0:T(8,128)(2,1)}, bf16[2048,2304]{1,0:T(8,128)(2,1)}, f32[2048,768]{1,0:T(8,128)},...) custom-call(s32[4]{0:T(128)} %counts.7, ...), custom_call_target="tpu_custom_call", output_to_operand_aliasing={{0}: (9, {})} | custom-call | flops 10499999744 | bytes 31500000 | tf_op jit(solution)/shard_map/forward_1/pallas_call | solution.py:476
  104.4 4.5 all-to-all-start.1
  109.2 25.9 %forward_1.3 = (bf16[2048,768]{1,0:T(8,128)(2,1)}, bf16[2048,2304]{1,0:T(8,128)(2,1)}, f32[2048,768]{1,0:T(8,128)}, bf16[8,6,256,512]{3,2,1,0:T(8,128)(2,1)}, bf...) custom-call(s32[4]{0:T(128)} %counts.7, ...), custom_call_target="tpu_custom_call", output_to_operand_aliasing={{0}: (9, {}), {1}: (10, {}), {2}: (11, {}), {3}: (12, {}), ... | custom-call | flops 10499999744 | bytes 31500000 | tf_op jit(solution)/shard_map/forward_1/pallas_call | solution.py:476
  135.1 15.2 %output.1.refs_6_ = bf16[8,4,2,32,768]{4,3,2,1,0:T(8,128)(2,1)} custom-call(bf16[2048,3072]{1,0:T(8,128)(2,1)} %get-tuple-element.117.active.left, f32[2048,768]{1,0:T(8,128)} %get-tuple-element.116.middle.refs_2_, bf16[2,3072,768]{2,1,0:T(8,128)(2,1)} %refs_5_.14), custom_call_target="tpu_custom_call" | custom-call | flops 4899999744 | bytes 14700000 | tf_op jit(solution)/shard_map/output/pallas_call | solution.py:498
  150.3 31.3 %mlp_back_1.1 = (bf16[8,4,2,32,768]{4,3,2,1,0:T(8,128)(2,1)}, bf16[2048,768]{1,0:T(8,128)(2,1)}, bf16[2048,3072]{1,0:T(8,128)(2,1)}, f32[2048,768]{1,0:T(8,128)}...) custom-call(bf16[8,4,2,32,768]{4,3,2,1,0:T(8,128)(2,1)} %all-to-all-done.1.refs_0_, ...), custom_call_target="tpu_custom_call", output_to_operand_aliasing={{0}: (6, {})} | custom-call | flops 140000002048 | bytes 420000000 | tf_op jit(solution)/shard_map/mlp_back_1/pallas_call | solution.py:522
  181.6 14.5 %outer_rows.2.refs_9_ = bf16[8,384,768]{2,1,0:T(8,128)(2,1)} custom-call(s32[1]{0:T(128)} %bitcast.place, bf16[2048,3072]{1,0:T(8,128)(2,1)} %get-tuple-element.117.active.left, bf16[2048,768]{1,0:T(8,128)(2,1)} %get-tuple-element.124.right), custom_call_target="tpu_custom_call" | custom-call | flops 4899999744 | bytes 14700000 | tf_op jit(solution)/shard_map/outer_rows/pallas_call | solution.py:629
  196.2 45.1 %attention_back_1.1 = (bf16[2048,2304]{1,0:T(8,128)(2,1)}, f32[1,768]{1,0:T(1,128)}, f32[1,768]{1,0:T(1,128)}, bf16[8,4,2,32,768]{4,3,2,1,0:T(8,128)(2,1)}) custom-call(f32[2048,768]{1,0:T(8,128)} %get-tuple-element.118.refs_0_.refs_1_, bf16[2048,2304]{1,0:T(8,128)(2,1)} %get-tuple-element.119.refs_1_, f32[2048,768]{1,0:T(8,128)} %get-tuple-element.120.refs_2_, ...), custom_call_target="tpu_custom_call" | custom-call | flops 14700000256 | bytes 44100000 | tf_op jit(solution)/shard_map/attention_back_1/pallas_call | solution.py:571
  241.3 4.5 all-to-all-start.3
  245.8 14.8 %outer_columns.5.refs_2_ = bf16[8,768,768]{2,1,0:T(8,128)(2,1)} custom-call(s32[1]{0:T(128)} %bitcast.place, bf16[2048,768]{1,0:T(8,128)(2,1)} %get-tuple-element.141.left, bf16[2048,3072]{1,0:T(8,128)(2,1)} %get-tuple-element.142.right), custom_call_target="tpu_custom_call" | custom-call | flops 5600000000 | bytes 16800000 | tf_op jit(solution)/shard_map/outer_columns/pallas_call | solution.py:669
  260.6 17.3 %outer_columns.6 = bf16[8,768,768]{2,1,0:T(8,128)(2,1)} custom-call(s32[1]{0:T(128)} %bitcast.place, bf16[2048,768]{1,0:T(8,128)(2,1)} %get-tuple-element.139.left, bf16[2048,2304]{1,0:T(8,128)(2,1)} %get-tuple-element.140.right, bf16[2048,768]{1,0:T(8,128)(2,1)} %get-tuple-element.122.refs_4_.refs_0_, ...), custom_call_target="tpu_custom_call", output_to_operand_aliasing={{}: (5, {})} | custom-call | flops 5600000000 | bytes 16800000 | tf_op jit(solution)/shard_map/outer_columns/pallas_call | solution.py:669
  278.0 7.9 %all-to-all-done.3.refs_0_ = bf16[8,4,2,32,768]{4,3,2,1,0:T(8,128)(2,1)} async-done(((bf16[8,4,2,32,768]{4,3,2,1,0:T(8,128)(2,1)}), bf16[8,4,2,32,768]{4,3,2,1,0:T(8,128)(2,1)}, u32[]{:S(2)}, u32[]{:S(2)}) %all-to-all-start.3) | async-done | bytes 3145760 | tf_op jit(solution)/shard_map/all_to_all | solution.py:776
  285.9 33.4 %mlp_back_0.1 = (bf16[2048,768]{1,0:T(8,128)(2,1)}, bf16[2048,3072]{1,0:T(8,128)(2,1)}, f32[2048,768]{1,0:T(8,128)}, f32[1,3072]{1,0:T(1,128)}, f32[1,768]{1,0:T(1,128)}, /*index=5*/f32[1,768]{1,0:T(1,128)}) custom-call(bf16[8,4,2,32,768]{4,3,2,1,0:T(8,128)(2,1)} %all-to-all-done.3.refs_0_, bf16[2048,3072]{1,0:T(8,128)(2,1)} %get-tuple-element.126.refs_1_, ...), custom_call_target="tpu_custom_call" | custom-call | flops 140000002048 | bytes 420000000 | tf_op jit(solution)/shard_map/mlp_back_0/pallas_call | solution.py:522
  319.3 14.8 %outer_rows.3 = (bf16[4,384,768]{2,1,0:T(8,128)(2,1)}, bf16[4,384,768]{2,1,0:T(8,128)(2,1)}) custom-call(s32[1]{0:T(128)} %bitcast.place, bf16[2048,3072]{1,0:T(8,128)(2,1)} %get-tuple-element.135.left, bf16[2048,768]{1,0:T(8,128)(2,1)} %get-tuple-element.136.right), custom_call_target="tpu_custom_call" | custom-call | flops 4899999744 | bytes 14700000 | tf_op jit(solution)/shard_map/outer_rows/pallas_call | solution.py:629
  334.1 20.2 %outer_columns.4 = (bf16[4,480,768]{2,1,0:T(8,128)(2,1)}, bf16[4,480,768]{2,1,0:T(8,128)(2,1)}) custom-call(s32[1]{0:T(128)} %bitcast.place, bf16[2048,768]{1,0:T(8,128)(2,1)} %get-tuple-element.133.left, bf16[2048,3072]{1,0:T(8,128)(2,1)} %get-tuple-element.134.right, bf16[2048,768]{1,0:T(8,128)(2,1)} %get-tuple-element.132.refs_0_.refs_4_, ...), custom_call_target="tpu_custom_call" | custom-call | flops 7000000000 | bytes 21000000 | tf_op jit(solution)/shard_map/outer_columns/pallas_call | solution.py:669
  354.8 4.7 all-to-all-start.4
  369.2 27.7 %attention_back_0.1.triple.right = bf16[2048,2304]{1,0:T(8,128)(2,1)} custom-call(f32[2048,768]{1,0:T(8,128)} %get-tuple-element.128.refs_1_.refs_0_.mid, bf16[2048,2304]{1,0:T(8,128)(2,1)} %get-tuple-element.129.refs_1_, f32[2048,768]{1,0:T(8,128)} %get-tuple-element.130.refs_2_, bf16[8,6,256,512]{3,2,1,0:T(8,128)(2,1)} %get-tuple-element.131.refs_3_, ...), custom_call_target="tpu_custom_call" | custom-call | flops 3500000 | bytes 10500 | tf_op jit(solution)/shard_map/attention_back_0/pallas_call | solution.py:571
  397.9 15.7 %finish.1 = (bf16[4,384,768]{2,1,0:T(8,128)(2,1)}, bf16[4,480,768]{2,1,0:T(8,128)(2,1)}, f32[1,768]{1,0:T(1,128)}, f32[1,768]{1,0:T(1,128)}, bf16[4,2,256,768]{3...) custom-call(bf16[4,2,256,768]{3,2,1,0:T(8,128)(2,1)} %x.7, ...), custom_call_target="tpu_custom_call", output_to_operand_aliasing={{0}: (6, {}), {1}: (7, {})} | custom-call | flops 3500000 | bytes 10500 | tf_op jit(solution)/shard_map/finish/pallas_call | solution.py:591
  413.7 8.1 %collective-permute-done.2 = bf16[2,384,768]{2,1,0:T(8,128)(2,1)} collective-permute-done((bf16[2,384,768]{2,1,0:T(8,128)(2,1)}, bf16[2,384,768]{2,1,0:T(8,128)(2,1)}, u32[]{:S(2)}, u32[]{:S(2)}) %collective-permute-start.2) | collective-permute-done | bytes 1179680 | tf_op jit(solution)/shard_map/ppermute | solution.py:690
  432.8 11.9 %outer_columns.7 = (bf16[8,16,768]{2,1,0:T(8,128)(2,1)}, bf16[4,288,768]{2,1,0:T(8,128)(2,1)}, bf16[4,288,768]{2,1,0:T(8,128)(2,1)}) custom-call(s32[1]{0:T(128)} %bitcast.place, bf16[2048,768]{1,0:T(8,128)(2,1)} %get-tuple-element.150.left, bf16[2048,2304]{1,0:T(8,128)(2,1)} %attention_back_0.1.triple.right, ...), custom_call_target="tpu_custom_call", output_to_operand_aliasing={{0}: (3, {})} | custom-call | flops 350000000 | bytes 1050000 | tf_op jit(solution)/shard_map/outer_columns/pallas_call | solution.py:669
  444.7 3.4 all-to-all-start.6
  456.7 4.5 all-to-all-start.5
  461.2 26.3 %all-reduce.4.cloned.1.call-done = (bf16[384,768]{1,0:T(8,128)(2,1)}, bf16[768,768]{1,0:T(8,128)(2,1)}) async-done(((bf16[384,768]{1,0:T(8,128)(2,1)}, bf16[768,768]{1,0:T(8,128)(2,1)}), (bf16[384,768]{1,0:T(8,128)(2,1)}, bf16[768,768]{1,0:T(8,128)(2,1)})) %all-reduce.4.cloned.1.call-update) | async-done | bytes 1769488 | tf_op jit(solution)/shard_map/psum | solution.py:852
  487.4 3.3 gather.2
  497.3 7.5 %collective-permute-done.10 = bf16[2,144,768]{2,1,0:T(8,128)(2,1)S(1)} collective-permute-done((bf16[2,144,768]{2,1,0:T(8,128)(2,1)S(1)}, bf16[2,144,768]{2,1,0:T(8,128)(2,1)S(1)}, u32[]{:S(2)}, u32[]{:S(2)}) %collective-permute-start.10) | collective-permute-done | bytes 442400 | tf_op jit(solution)/shard_map/ppermute | solution.py:690
  517.1 43.6 %all_to_all.45 = bf16[4,304,768]{2,1,0:T(8,128)(2,1)S(1)} all-to-all(bf16[4,304,768]{2,1,0:T(8,128)(2,1)S(1)} %pad_maximum_fusion), channel_id=1, replica_groups=mesh['clip'=4,'frame'=8] {'clip'}, dimensions={0} | all-to-all | bytes 3735552 | tf_op jit(solution)/shard_map/all_to_all | solution.py:730
  561.6 3.5 all-to-all-start.8
  568.2 8.3 %all-to-all-done.8 = bf16[4,72,768]{2,1,0:T(8,128)(2,1)S(1)} async-done(((bf16[4,72,768]{2,1,0:T(8,128)(2,1)}), bf16[4,72,768]{2,1,0:T(8,128)(2,1)S(1)}, u32[]{:S(2)}, u32[]{:S(2)}) %all-to-all-start.8) | async-done | bytes 442400 | tf_op jit(solution)/shard_map/all_to_all | solution.py:730
  577.3 3.3 gather.3
  (112 shorter events, 54.5 us)
Async XLA Ops:
  37.8 36.3 %all-to-all-start = ((bf16[8,2,2,32,768]{4,3,2,1,0:T(8,128)(2,1)}), bf16[8,2,2,32,768]{4,3,2,1,0:T(8,128)(2,1)}, u32[]{:S(2)}, u32[]{:S(2)}) async-start(bf16[8,2,2,32,768]{4,3,2,1,0:T(8,128)(2,1)} %get-tuple-element.91), calls=%async_computation | async-start | bytes 3145728 | tf_op jit(solution)/shard_map/all_to_all | solution.py:776
  74.1 30.3 %all-to-all-start.2 = ((bf16[8,2,2,32,768]{4,3,2,1,0:T(8,128)(2,1)}), bf16[8,2,2,32,768]{4,3,2,1,0:T(8,128)(2,1)}, u32[]{:S(2)}, u32[]{:S(2)}) async-start(bf16[8,2,2,32,768]{4,3,2,1,0:T(8,128)(2,1)} %get-tuple-element.104), calls=%async_computation.2 | async-start | bytes 3145728 | tf_op jit(solution)/shard_map/all_to_all | solution.py:776
  104.4 45.9 %all-to-all-start.1 = ((bf16[8,4,2,32,768]{4,3,2,1,0:T(8,128)(2,1)}), bf16[8,4,2,32,768]{4,3,2,1,0:T(8,128)(2,1)}, u32[]{:S(2)}, u32[]{:S(2)}) async-start(bf16[8,4,2,32,768]{4,3,2,1,0:T(8,128)(2,1)} %get-tuple-element.103), calls=%async_computation.1 | async-start | bytes 6291456 | tf_op jit(solution)/shard_map/all_to_all | solution.py:776
  108.9 151.7 %reduce-scatter.3.cloned.1.call-start = ((), (), s32[]{:S(2)}) async-start(), calls=%async_computation.11 | async-start | bytes 5308416 | tf_op jit(solution)/shard_map/reduce_scatter | solution.py:813
  241.3 44.6 %all-to-all-start.3 = ((bf16[8,4,2,32,768]{4,3,2,1,0:T(8,128)(2,1)}), bf16[8,4,2,32,768]{4,3,2,1,0:T(8,128)(2,1)}, u32[]{:S(2)}, u32[]{:S(2)}) async-start(bf16[8,4,2,32,768]{4,3,2,1,0:T(8,128)(2,1)} %get-tuple-element.125), calls=%async_computation.3 | async-start | bytes 6291456 | tf_op jit(solution)/shard_map/all_to_all | solution.py:776
  245.8 123.4 %reduce-scatter.5.cloned.1.call-start = ((), (), s32[]{:S(2)}) async-start(), calls=%async_computation.12 | async-start | bytes 10616832 | tf_op jit(solution)/shard_map/reduce_scatter | solution.py:813
  354.3 5.7 collective-permute-start.1
  354.3 10.3 %collective-permute-start = (bf16[4,384,768]{2,1,0:T(8,128)(2,1)}, bf16[4,384,768]{2,1,0:T(8,128)(2,1)}, u32[]{:S(2)}, u32[]{:S(2)}) collective-permute-start(bf16[4,384,768]{2,1,0:T(8,128)(2,1)} %get-tuple-element.137.refs_2_), channel_id=1, source_target_pairs={{0,1},{1,0},{2,3},{3,2},{4,5},{5,4},{6,7},{7,6},{8,9},{9,8},{10,11... | collective-permute-start | bytes 7077896 | tf_op jit(solution)/shard_map/ppermute | solution.py:690
  354.8 43.1 %all-to-all-start.4 = ((bf16[8,4,2,32,768]{4,3,2,1,0:T(8,128)(2,1)}), bf16[8,4,2,32,768]{4,3,2,1,0:T(8,128)(2,1)}, u32[]{:S(2)}, u32[]{:S(2)}) async-start(bf16[8,4,2,32,768]{4,3,2,1,0:T(8,128)(2,1)} %get-tuple-element.143), calls=%async_computation.6 | async-start | bytes 6291456 | tf_op jit(solution)/shard_map/all_to_all | solution.py:776
  363.1 5.6 copy-start.11
  363.1 5.7 copy-start.8
  363.1 5.7 copy-start.9
  363.1 6.0 %copy-start.4 = (f32[1,3072]{1,0:T(1,128)S(1)}, f32[1,3072]{1,0:T(1,128)}, u32[]{:S(2)}) copy-start(f32[1,3072]{1,0:T(1,128)} %get-tuple-element.160) | copy-start | bytes 36868
  363.1 6.0 %copy-start.5 = (f32[1,3072]{1,0:T(1,128)S(1)}, f32[1,3072]{1,0:T(1,128)}, u32[]{:S(2)}) copy-start(f32[1,3072]{1,0:T(1,128)} %get-tuple-element.155) | copy-start | bytes 36868
  363.1 65.4 %collective-permute-start.4 = (bf16[2,480,768]{2,1,0:T(8,128)(2,1)}, bf16[2,480,768]{2,1,0:T(8,128)(2,1)}, u32[]{:S(2)}, u32[]{:S(2)}) collective-permute-start(bf16[2,480,768]{2,1,0:T(8,128)(2,1)} %add_convert_fusion.refs_3_), channel_id=1, source_target_pairs={{0,4},{1,5},{2,6},{3,7},{4,0},{5,1},{6,2},{7,3},{8,12},{9,13},{10,... | collective-permute-start | bytes 4423688 | tf_op jit(solution)/shard_map/ppermute | solution.py:690
  367.1 54.7 %collective-permute-start.2 = (bf16[2,384,768]{2,1,0:T(8,128)(2,1)}, bf16[2,384,768]{2,1,0:T(8,128)(2,1)}, u32[]{:S(2)}, u32[]{:S(2)}) collective-permute-start(bf16[2,384,768]{2,1,0:T(8,128)(2,1)} %fusion.1.refs_2_), channel_id=1, source_target_pairs={{0,2},{1,3},{2,0},{3,1},{4,6},{5,7},{6,4},{7,5},{8,10},{9,11},{10,... | collective-permute-start | bytes 3538952 | tf_op jit(solution)/shard_map/ppermute | solution.py:690
  396.9 90.5 %all-reduce.4.cloned.1.call-start = ((), (), s32[]{:S(2)}) async-start(), calls=%async_computation.13 | async-start | bytes 3538944 | tf_op jit(solution)/shard_map/psum | solution.py:852
  421.8 9.7 %copy-start.6 = (f32[1,768]{1,0:T(1,128)S(1)}, f32[1,768]{1,0:T(1,128)}, u32[]{:S(2)}) copy-start(f32[1,768]{1,0:T(1,128)} %get-tuple-element.152) | copy-start | bytes 9220
  421.8 9.7 %copy-start.7 = (f32[1,768]{1,0:T(1,128)S(1)}, f32[1,768]{1,0:T(1,128)}, u32[]{:S(2)}) copy-start(f32[1,768]{1,0:T(1,128)} %get-tuple-element.154) | copy-start | bytes 9220
  421.8 9.9 %copy-start.12 = (f32[1,768]{1,0:T(1,128)S(1)}, f32[1,768]{1,0:T(1,128)}, u32[]{:S(2)}) copy-start(f32[1,768]{1,0:T(1,128)} %get-tuple-element.151) | copy-start | bytes 9220
  421.8 9.9 %copy-start.13 = (f32[1,768]{1,0:T(1,128)S(1)}, f32[1,768]{1,0:T(1,128)}, u32[]{:S(2)}) copy-start(f32[1,768]{1,0:T(1,128)} %get-tuple-element.153) | copy-start | bytes 9220
  424.3 27.1 %collective-permute-start.3 = (bf16[384,768]{1,0:T(8,128)(2,1)}, bf16[384,768]{1,0:T(8,128)(2,1)}, u32[]{:S(2)}, u32[]{:S(2)}) collective-permute-start(bf16[384,768]{1,0:T(8,128)(2,1)} %fusion.2.refs_1_), channel_id=1, source_target_pairs={{0,4},{1,5},{2,6},{3,7},{4,0},{5,1},{6,2},{7,3},{8,12},{9,13},{10,... | collective-permute-start | bytes 1769480 | tf_op jit(solution)/shard_map/ppermute | solution.py:690
  430.4 22.9 %collective-permute-start.5 = (bf16[480,768]{1,0:T(8,128)(2,1)S(1)}, bf16[480,768]{1,0:T(8,128)(2,1)}, u32[]{:S(2)}, u32[]{:S(2)}) collective-permute-start(bf16[480,768]{1,0:T(8,128)(2,1)S(1)} %fusion.5.refs_2_), channel_id=1, source_target_pairs={{0,2},{1,3},{2,0},{3,1},{4,6},{5,7},{6,4},{7,5},{8,10},{9,11},{10,... | collective-permute-start | bytes 2211848 | tf_op jit(solution)/shard_map/ppermute | solution.py:690
  444.7 12.0 %all-to-all-start.6 = ((bf16[8,16,768]{2,1,0:T(8,128)(2,1)}), bf16[8,16,768]{2,1,0:T(8,128)(2,1)S(1)}, u32[]{:S(2)}, u32[]{:S(2)}) async-start(bf16[8,16,768]{2,1,0:T(8,128)(2,1)} %get-tuple-element.164), calls=%async_computation.8 | async-start | bytes 393216 | tf_op jit(solution)/shard_map/all_to_all | solution.py:776
  450.9 41.1 %collective-permute-start.9 = (bf16[4,144,768]{2,1,0:T(8,128)(2,1)}, bf16[4,144,768]{2,1,0:T(8,128)(2,1)}, u32[]{:S(2)}, u32[]{:S(2)}) collective-permute-start(bf16[4,144,768]{2,1,0:T(8,128)(2,1)} %get-tuple-element.176), channel_id=1, source_target_pairs={{0,1},{1,0},{2,3},{3,2},{4,5},{5,4},{6,7},{7,6},{8,9},{9,8},{10,11... | collective-permute-start | bytes 2654216 | tf_op jit(solution)/shard_map/ppermute | solution.py:690
  451.3 43.3 %collective-permute-start.6 = (bf16[4,144,768]{2,1,0:T(8,128)(2,1)}, bf16[4,144,768]{2,1,0:T(8,128)(2,1)}, u32[]{:S(2)}, u32[]{:S(2)}) collective-permute-start(bf16[4,144,768]{2,1,0:T(8,128)(2,1)} %get-tuple-element.175), channel_id=1, source_target_pairs={{0,1},{1,0},{2,3},{3,2},{4,5},{5,4},{6,7},{7,6},{8,9},{9,8},{10,11... | collective-permute-start | bytes 2654216 | tf_op jit(solution)/shard_map/ppermute | solution.py:690
  456.7 58.8 %all-to-all-start.5 = ((bf16[4,216,768]{2,1,0:T(8,128)(2,1)}), bf16[4,216,768]{2,1,0:T(8,128)(2,1)}, u32[]{:S(2)}, u32[]{:S(2)}) async-start(bf16[4,216,768]{2,1,0:T(8,128)(2,1)} %bitcast.13), calls=%async_computation.7 | async-start | bytes 2654208 | tf_op jit(solution)/shard_map/all_to_all | solution.py:730
  493.2 11.5 %collective-permute-start.10 = (bf16[2,144,768]{2,1,0:T(8,128)(2,1)S(1)}, bf16[2,144,768]{2,1,0:T(8,128)(2,1)S(1)}, u32[]{:S(2)}, u32[]{:S(2)}) collective-permute-start(bf16[2,144,768]{2,1,0:T(8,128)(2,1)S(1)} %add_convert_fusion.3), channel_id=1, source_target_pairs={{0,4},{1,5},{2,6},{3,7},{4,0},{5,1},{6,2},{7,3},{8,12},{9,13},{10,... | collective-permute-start | bytes 1327112 | tf_op jit(solution)/shard_map/ppermute | solution.py:690
  495.7 11.5 %collective-permute-start.7 = (bf16[2,144,768]{2,1,0:T(8,128)(2,1)S(1)}, bf16[2,144,768]{2,1,0:T(8,128)(2,1)S(1)}, u32[]{:S(2)}, u32[]{:S(2)}) collective-permute-start(bf16[2,144,768]{2,1,0:T(8,128)(2,1)S(1)} %fusion.6), channel_id=1, source_target_pairs={{0,2},{1,3},{2,0},{3,1},{4,6},{5,7},{6,4},{7,5},{8,10},{9,11},{10,... | collective-permute-start | bytes 1327112 | tf_op jit(solution)/shard_map/ppermute | solution.py:690
  505.9 6.0 %collective-permute-start.11 = (bf16[144,768]{1,0:T(8,128)(2,1)S(1)}, bf16[144,768]{1,0:T(8,128)(2,1)S(1)}, u32[]{:S(2)}, u32[]{:S(2)}) collective-permute-start(bf16[144,768]{1,0:T(8,128)(2,1)S(1)} %fusion.12), channel_id=1, source_target_pairs={{0,2},{1,3},{2,0},{3,1},{4,6},{5,7},{6,4},{7,5},{8,10},{9,11},{10,... | collective-permute-start | bytes 663560 | tf_op jit(solution)/shard_map/ppermute | solution.py:690
  508.3 6.0 %collective-permute-start.8 = (bf16[144,768]{1,0:T(8,128)(2,1)S(1)}, bf16[144,768]{1,0:T(8,128)(2,1)S(1)}, u32[]{:S(2)}, u32[]{:S(2)}) collective-permute-start(bf16[144,768]{1,0:T(8,128)(2,1)S(1)} %fusion.7), channel_id=1, source_target_pairs={{0,4},{1,5},{2,6},{3,7},{4,0},{5,1},{6,2},{7,3},{8,12},{9,13},{10,... | collective-permute-start | bytes 663560 | tf_op jit(solution)/shard_map/ppermute | solution.py:690
  561.6 14.9 %all-to-all-start.8 = ((bf16[4,72,768]{2,1,0:T(8,128)(2,1)}), bf16[4,72,768]{2,1,0:T(8,128)(2,1)S(1)}, u32[]{:S(2)}, u32[]{:S(2)}) async-start(bf16[4,72,768]{2,1,0:T(8,128)(2,1)} %broadcast_in_dim.29), calls=%async_computation.10 | async-start | bytes 884736 | tf_op jit(solution)/shard_map/all_to_all | solution.py:730
  (5 other events, 19.0 us)
Sparse Core Ops, SparseCore 0:
  196.3 58.3 reduce-scatter.2
  278.1 78.5 reduce-scatter.4
  400.3 87.0 all-reduce.3
